TPU v7x, 32 devices: a whole 2x2x4 slice. The times are simulated.
32 devices in a mesh: gx: 4 (over z), gy: 4 (over y, x), gz: 2 (over core).
Axes of the slice: x: 2, y: 2, z: 4, core: 2. Of those that a mesh axis runs over, the one named last changes fastest.
Arguments:
- tokens: bfloat16 [4, 2048, 2048], P('gx', ('gy', 'gz')), may hold values from -6 to 6
- lengths: int32 [4, 6], P('gx'), may hold values from 60 to 800, as said below
- ln1_gain: bfloat16 [2048], replicated, may hold values from 0.5 to 1.5
- ln1_bias: bfloat16 [2048], replicated, may hold values from -1 to 1
- qkv_weight: bfloat16 [2048, 3, 2048], P('gx', None, ('gy', 'gz')), may hold values from -0.125 to 0.125
- qkv_bias: bfloat16 [3, 2048], P(None, ('gy', 'gz')), may hold values from -3 to 3
- out_weight: bfloat16 [2048, 2048], P('gx', ('gy', 'gz')), may hold values from -1 to 1
- ln2_gain: bfloat16 [2048], replicated, may hold values from 0.5 to 1.5
- ln2_bias: bfloat16 [2048], replicated, may hold values from -1 to 1
- gate_up_weight: bfloat16 [2048, 2, 5632], P('gx', None, ('gy', 'gz')), may hold values from -0.125 to 0.125
- down_weight: bfloat16 [2048, 5632], P('gx', ('gy', 'gz')), may hold values from -0.078125 to 0.078125
- cotangent: bfloat16 [4, 2048, 2048], P('gx', ('gy', 'gz')), may hold values from -6 to 6
Outputs:
- activations: bfloat16 [4, 2048, 2048], P('gx', ('gy', 'gz'))
- input_grad: bfloat16 [4, 2048, 2048], P('gx', ('gy', 'gz'))
- ln1_gain_grad: float32 [2048], replicated
- ln1_bias_grad: float32 [2048], replicated
- qkv_weight_grad: float32 [2048, 3, 2048], P('gx', None, ('gy', 'gz'))
- qkv_bias_grad: float32 [3, 2048], P(None, ('gy', 'gz'))
- out_weight_grad: float32 [2048, 2048], P('gx', ('gy', 'gz'))
- ln2_gain_grad: float32 [2048], replicated
- ln2_bias_grad: float32 [2048], replicated
- gate_up_grad: float32 [2048, 2, 5632], P('gx', None, ('gy', 'gz'))
- down_grad: float32 [2048, 5632], P('gx', ('gy', 'gz'))
Inputs may be any that keep to these rules, and one draw needn't show every extreme that they name: Each sequence holds 6 documents in order, their lengths summing to 2048; every sequence has one document of exactly 800 tokens and one of exactly 60 tokens.
All inputs are finite; a program needn't handle non-finite values.
Results may differ from a plain program's by a relative error of at most 0.015.
Values may be sent and summed in bfloat16 or wider, within the bound.
No kernel may reach another device: no remote copies, remote signals or barrier semaphores. Data moves between devices by JAX's collectives and lax.ppermute only.
A program may use at most 320 MiB of HBM per device.

v0:
```python
import math

import jax
import jax.numpy as jnp
from jax import lax
from jax.experimental import pallas as pl
from jax.experimental.pallas import tpu as pltpu
from jax.sharding import PartitionSpec as P

HEAD_DIM = 64
ROT = 16
BF16 = jnp.bfloat16
F32 = jnp.float32
MIB = 1024 * 1024
SCALE = 1.0

SWAP_X = [(0, 1), (1, 0), (2, 3), (3, 2)]
SWAP_Y = [(0, 2), (2, 0), (1, 3), (3, 1)]
SWAP_FAR = [(0, 3), (3, 0), (1, 2), (2, 1)]
SWAP_CORE = [(0, 1), (1, 0)]


def to_x(values):
    return lax.ppermute(values, "gy", SWAP_X)


def to_y(values):
    return lax.ppermute(values, "gy", SWAP_Y)


def to_far(values):
    return lax.ppermute(values, "gy", SWAP_FAR)


def after(values, *others):
    return lax.optimization_barrier((values, others))[0]


def to_core(values):
    return lax.ppermute(values, "gz", SWAP_CORE)


def dot_nn(left, right):
    return lax.dot_general(left, right, (((1,), (0,)), ((), ())), preferred_element_type=F32)


def dot_nt(left, right):
    return lax.dot_general(left, right, (((1,), (1,)), ((), ())), preferred_element_type=F32)


def dot_tn(left, right):
    return lax.dot_general(left, right, (((0,), (0,)), ((), ())), preferred_element_type=F32)


def dot_tt(left, right):
    return lax.dot_general(left, right, (((0,), (1,)), ((), ())), preferred_element_type=F32)


VM = pl.BlockSpec(memory_space=pltpu.VMEM)
SM = pl.BlockSpec(memory_space=pltpu.SMEM)
ANY = pl.BlockSpec(memory_space=pl.ANY)


def params():
    return pltpu.CompilerParams(vmem_limit_bytes=58 * MIB)


def cost(flops, moved, scale=1):
    return pl.CostEstimate(
        flops=int(flops * scale * SCALE), bytes_accessed=int(moved * scale * SCALE), transcendentals=0
    )


def gather_first(block):
    return block, to_x(block), to_y(block), to_core(block)


def gather_plane(block, *between):
    return gather_second(gather_first(block), between)


def gather_second(first, between, later=None):
    block, from_x, from_y, other = first
    half = block.shape[0] // 2
    far_top = to_x(after(from_y[:half], *between))
    far_bottom = to_y(after(from_x[half:], *between))
    own = [(block, 0, 0), (from_x, 1, 0), (from_y, 2, 0), (far_top, 3, 0), (far_bottom, 3, half)]
    if later is not None:
        held = later(far_top, far_bottom)
        from_x, from_y, far_top, far_bottom = after((from_x, from_y, far_top, far_bottom), *held)
    return own + [
        (other, 4, 0),
        (to_core(from_x), 5, 0),
        (to_core(from_y), 6, 0),
        (to_core(far_top), 7, 0),
        (to_core(far_bottom), 7, half),
    ]


def exchange_first(own, sibling):
    came = to_core(sibling)
    sent = tuple(jnp.stack([own[step], came[step]]) for step in range(1, 4))
    return own[0], came[0], lax.optimization_barrier(sent)


def exchange_second(own, came, sent):
    return [own, came, to_x(sent[0]), to_y(sent[1]), to_far(sent[2])]


def exchanged_copies(refs, hold_of, sems):
    copies = [
        pltpu.make_async_copy(refs[0], hold_of(0), sems.at[0]),
        pltpu.make_async_copy(refs[1], hold_of(4), sems.at[4]),
    ]
    for step in range(1, 4):
        for core in range(2):
            chunk = step + 4 * core
            copies.append(
                pltpu.make_async_copy(refs[step + 1].at[core], hold_of(chunk), sems.at[chunk])
            )
    return copies


def scatter_first(own, sibling, rows):
    half = rows // 2
    came = to_core(sibling)

    def part(chunk, first):
        at = chunk * rows + first
        return (own[at : at + half].astype(F32) + came[at : at + half].astype(F32)).astype(BF16)

    for_x = jnp.concatenate([part(3, 0), part(1, 0)], axis=0)
    for_y = jnp.concatenate([part(3, half), part(2, half)], axis=0)
    return came, lax.optimization_barrier((for_x, for_y))


def scatter_second(own, came, sent, rows, *between):
    half = rows // 2
    from_x, from_y = after((to_x(sent[0]), to_y(sent[1])), *between)

    def part(chunk, first, more):
        at = chunk * rows + first
        total = own[at : at + half].astype(F32) + came[at : at + half].astype(F32)
        return (total + more.astype(F32)).astype(BF16)

    return [part(2, 0, from_x[:half]), part(1, half, from_y[:half])], [from_x, from_y]


def scatter_last(own, came, sent, arrived):
    y_top, x_bottom = to_y(sent[0]), to_x(sent[1])
    return own, came, arrived[0], x_bottom, y_top, arrived[1]


def summed(own_ref, came_ref, from_x, x_bottom, y_top, from_y):
    half = x_bottom.shape[0]
    total = own_ref[...].astype(F32) + came_ref[...].astype(F32)
    top = total[:half] + from_x[...].astype(F32) + y_top[...].astype(F32)
    bottom = total[half:] + x_bottom[...].astype(F32) + from_y[...].astype(F32)
    return jnp.concatenate([top, bottom], axis=0)


def sum_all(vectors, axes):
    for name, size in axes:
        step = 1
        while step < size:
            width = min(4, size // step)
            shifted = [
                lax.ppermute(vectors, name, [(i, i ^ (step * k)) for i in range(size)])
                for k in range(1, width)
            ]
            for other in shifted:
                vectors = vectors + other
            step *= width
    return vectors


def norm_parts(values):
    average = jnp.mean(values, axis=-1, keepdims=True)
    centered = values - average
    variance = jnp.mean(centered * centered, axis=-1, keepdims=True)
    rstd = lax.rsqrt(variance + 1e-05)
    return centered * rstd, rstd


def norm_one(tokens, gain, shift):
    def body(t_ref, g_ref, b_ref, o_ref):
        xhat, _ = norm_parts(t_ref[...].astype(F32))
        o_ref[...] = (xhat * g_ref[...] + b_ref[...]).astype(BF16)

    return pl.pallas_call(
        body,
        out_shape=jax.ShapeDtypeStruct(tokens.shape, BF16),
        in_specs=[VM] * 3,
        out_specs=VM,
        compiler_params=params(),
        cost_estimate=cost(0, 4 * tokens.size),
        name="norm_one",
    )(tokens, gain, shift)


def middle_norm(tokens, blocks, weight_pieces, gain, shift):
    rows, depth = tokens.shape
    layout, arrays = split_pieces(weight_pieces)
    width = blocks[0].shape[0]
    count = len(arrays)

    def body(t_ref, g_ref, b_ref, *refs):
        piece_refs = refs[:count]
        block_refs = refs[count : count + 5]
        m_ref, o_ref, hold, att, sems, b_sems = refs[count + 5 :]
        copies = exchanged_copies(
            block_refs, lambda chunk: att.at[pl.ds(chunk * width, width), :], b_sems
        )
        for copy in copies:
            copy.start()
        copies += [copy for _, copy in start_pieces(layout, piece_refs, width, hold, sems)]
        for copy in copies:
            copy.wait()
        middle = t_ref[...].astype(F32) + dot_tn(att[...], hold[...])
        m_ref[...] = middle
        xhat, _ = norm_parts(middle)
        o_ref[...] = (xhat * g_ref[...] + b_ref[...]).astype(BF16)

    return pl.pallas_call(
        body,
        out_shape=[
            jax.ShapeDtypeStruct((rows, depth), F32),
            jax.ShapeDtypeStruct((rows, depth), BF16),
        ],
        in_specs=[VM, VM, VM] + [ANY] * (count + 5),
        out_specs=[VM, VM],
        scratch_shapes=[
            pltpu.VMEM((8 * width, depth), BF16),
            pltpu.VMEM((8 * width, rows), BF16),
            pltpu.SemaphoreType.DMA((count,)),
            pltpu.SemaphoreType.DMA((8,)),
        ],
        compiler_params=params(),
        cost_estimate=cost(2 * rows * depth * 8 * width, 14 * MIB),
        name="middle_norm",
    )(tokens, gain, shift, *arrays, *blocks)


def norm_back_parts(v_ref, u_ref, part_refs, g_ref):
    e = summed(*part_refs)
    xhat, rstd = norm_parts(v_ref[...].astype(F32))
    d_xhat = e * g_ref[...]
    mean_d = jnp.mean(d_xhat, axis=-1, keepdims=True)
    mean_x = jnp.mean(d_xhat * xhat, axis=-1, keepdims=True)
    d_v = rstd * (d_xhat - mean_d - xhat * mean_x)
    sums = jnp.concatenate(
        [jnp.sum(e * xhat, axis=0, keepdims=True), jnp.sum(e, axis=0, keepdims=True)], axis=0
    )
    return u_ref[...].astype(F32) + d_v, sums


def norm_two_back(middle, cotangent, parts, gain, weight_pieces):
    rows, depth = middle.shape
    layout, arrays = split_pieces(weight_pieces)
    width = arrays[0].shape[0]
    count = len(arrays)

    def body(v_ref, u_ref, *refs):
        g_ref = refs[6]
        piece_refs = refs[7 : 7 + count]
        low_ref, sum_ref, wide_ref, *out_refs, hold, sems = refs[7 + count :]
        copies = start_pieces(layout, piece_refs, width, hold, sems)
        total, sum_ref[...] = norm_back_parts(v_ref, u_ref, refs[:6], g_ref)
        wide_ref[...] = total
        low_ref[...] = total.astype(BF16)
        for _, copy in copies:
            copy.wait()
        for chunk in range(8):
            block = dot_nt(hold[chunk * width : (chunk + 1) * width, :], low_ref[...]).astype(BF16)
            if chunk < 4:
                out_refs[chunk][...] = block
            else:
                out_refs[4][chunk - 4] = block

    whole = pl.BlockSpec((rows, depth), lambda i: (0, 0))
    line = pl.BlockSpec((1, depth), lambda i: (0, 0))
    two = pl.BlockSpec((2, depth), lambda i: (0, 0))
    half = pl.BlockSpec((rows // 2, depth), lambda i: (0, 0))
    second = pl.BlockSpec((rows // 2, depth), lambda i: (1, 0))
    block = pl.BlockSpec((width, rows), lambda i: (0, 0))
    outs = pl.pallas_call(
        body,
        grid=(1,),
        in_specs=[whole, whole, whole, whole, second, half, half, second, line] + [ANY] * count,
        out_specs=[whole, two, whole]
        + [block] * 4
        + [pl.BlockSpec((4, width, rows), lambda i: (0, 0, 0))],
        scratch_shapes=[
            pltpu.VMEM((8 * width, depth), BF16),
            pltpu.SemaphoreType.DMA((count,)),
        ],
        out_shape=[
            jax.ShapeDtypeStruct((rows, depth), BF16),
            jax.ShapeDtypeStruct((2, depth), F32),
            jax.ShapeDtypeStruct((rows, depth), F32),
        ]
        + [jax.ShapeDtypeStruct((width, rows), BF16)] * 4
        + [jax.ShapeDtypeStruct((4, width, rows), BF16)],
        compiler_params=params(),
        cost_estimate=cost(0, 0),
        name="norm_two_back",
    )(middle, cotangent, *parts, gain, *arrays)
    return outs[0], outs[1], outs[2], outs[3:7], outs[7]


def norm_one_back(tokens, d_middle, parts, gain):
    rows, depth = tokens.shape

    def body(v_ref, u_ref, *refs):
        g_ref, low_ref, sum_ref = refs[6:]
        total, sum_ref[...] = norm_back_parts(v_ref, u_ref, refs[:6], g_ref)
        low_ref[...] = total.astype(BF16)

    whole = pl.BlockSpec((rows, depth), lambda i: (0, 0))
    line = pl.BlockSpec((1, depth), lambda i: (0, 0))
    two = pl.BlockSpec((2, depth), lambda i: (0, 0))
    half = pl.BlockSpec((rows // 2, depth), lambda i: (0, 0))
    second = pl.BlockSpec((rows // 2, depth), lambda i: (1, 0))
    return pl.pallas_call(
        body,
        grid=(1,),
        out_shape=[
            jax.ShapeDtypeStruct((rows, depth), BF16),
            jax.ShapeDtypeStruct((2, depth), F32),
        ],
        in_specs=[whole, whole, whole, whole, second, half, half, second, line],
        out_specs=[whole, two],
        compiler_params=params(),
        cost_estimate=cost(0, 8 * MIB),
        name="norm_one_back",
    )(tokens, d_middle, *parts, gain)


def split_pieces(pieces):
    return [(chunk, first) for _, chunk, first in pieces], [piece for piece, _, _ in pieces]


def start_pieces(layout, piece_refs, rows, hold, sems, pos_ref=None):
    copies = []
    for number, ((chunk, first), ref) in enumerate(zip(layout, piece_refs)):
        if pos_ref is None:
            at = chunk * rows + first
        else:
            at = pl.multiple_of(pos_ref[chunk] * rows + first, 16)
        copy = pltpu.make_async_copy(ref, hold.at[pl.ds(at, ref.shape[0]), :], sems.at[number])
        copy.start()
        copies.append((chunk, copy))
    return copies


def column_copies(part, cols, layout, piece_refs, rows, hold, sems, pos_ref=None):
    columns = pl.ds(part * cols, cols)
    copies = []
    for number, ((chunk, first), ref) in enumerate(zip(layout, piece_refs)):
        if pos_ref is None:
            at = chunk * rows + first
        else:
            at = pl.multiple_of(pos_ref[chunk] * rows + first, 16)
        copies.append(
            pltpu.make_async_copy(
                ref.at[:, columns],
                hold.at[pl.ds(at, ref.shape[0]), columns],
                sems.at[part, number],
            )
        )
    return copies


def copy_columns(step, parts, cols, layout, piece_refs, rows, hold, sems, pos_ref=None):
    def copies(part):
        return column_copies(part, cols, layout, piece_refs, rows, hold, sems, pos_ref)

    @pl.when(step == 0)
    def _():
        for part in range(parts):
            for copy in copies(part):
                copy.start()

    for part in range(parts):

        @pl.when(step == part)
        def _(part=part):
            for copy in copies(part):
                copy.wait()


def weight_copies(w_ref, height, w_hold, w_sems):
    parts, _, cols = w_ref.shape
    return [
        pltpu.make_async_copy(
            w_ref.at[part, pl.ds(0, height)],
            w_hold.at[:, pl.ds(part * cols, cols)],
            w_sems.at[part],
        )
        for part in range(parts)
    ]


def wait_core(core_step, copies):
    for chunk, copy in copies:
        if chunk // 4 == core_step:
            copy.wait()


def project(pos, pieces, weight, bias, cosine, sine):
    layout, arrays = split_pieces(pieces)
    rows, depth = arrays[0].shape
    length = 8 * rows
    parts, tall, _ = weight.shape
    width = tall // 4
    count = len(arrays)
    half_rot = ROT // 2

    def body(pos_ref, w_ref, b_ref, c_ref, s_ref, *refs):
        piece_refs = refs[:count]
        out_ref, hold, w_hold, made, sems, w_sems, o_sems = refs[count:]
        w_copies = weight_copies(w_ref, 3 * width, w_hold, w_sems)
        for copy in w_copies:
            copy.start()
        copies = start_pieces(layout, piece_refs, rows, hold, sems)
        for copy in w_copies:
            copy.wait()
        kept = []
        for core_step in range(2):
            wait_core(core_step, copies)
            for chunk in range(4 * core_step, 4 * core_step + 4):
                block = hold[chunk * rows : (chunk + 1) * rows, :]
                lanes = chunk_lanes(pos_ref, chunk, rows)
                cosines, sines = c_ref[:, lanes], s_ref[:, lanes]
                for kind in range(3):
                    band = slice(kind * width, (kind + 1) * width)
                    turned = dot_nt(w_hold[band, :], block) + b_ref[band, :]
                    if kind < 2:
                        bands = []
                        for first in range(0, width, HEAD_DIM):
                            r_one = turned[first : first + half_rot]
                            r_two = turned[first + half_rot : first + ROT]
                            bands.append(r_one * cosines - r_two * sines)
                            bands.append(r_two * cosines + r_one * sines)
                            bands.append(turned[first + ROT : first + HEAD_DIM])
                        turned = jnp.concatenate(bands, axis=0)
                    if kind == 0:
                        turned = turned * (1.0 / math.sqrt(HEAD_DIM))
                    made[chunk, band, :] = turned.astype(BF16)
            for chunk in range(4 * core_step, 4 * core_step + 4):
                copy = pltpu.make_async_copy(
                    made.at[chunk],
                    out_ref.at[:, chunk_lanes(pos_ref, chunk, rows)],
                    o_sems.at[chunk],
                )
                copy.start()
                kept.append(copy)
        for copy in kept:
            copy.wait()

    return pl.pallas_call(
        body,
        in_specs=[SM, ANY, VM, VM, VM] + [ANY] * count,
        out_specs=ANY,
        out_shape=jax.ShapeDtypeStruct((3 * width, length), BF16),
        scratch_shapes=[
            pltpu.VMEM((length, depth), BF16),
            pltpu.VMEM((3 * width, depth), BF16),
            pltpu.VMEM((8, 3 * width, rows), BF16),
            pltpu.SemaphoreType.DMA((count,)),
            pltpu.SemaphoreType.DMA((parts,)),
            pltpu.SemaphoreType.DMA((8,)),
        ],
        compiler_params=params(),
        cost_estimate=cost(6 * length * depth * width, 15 * MIB),
        name="project",
    )(pos, weight, bias, cosine, sine, *arrays)


def feed(pieces, weight):
    layout, arrays = split_pieces(pieces)
    rows, depth = arrays[0].shape
    length = 8 * rows
    parts, pair_units, _ = weight.shape
    units = pair_units // 2
    count = len(arrays)

    def body(w_ref, *refs):
        piece_refs = refs[:count]
        hid_ref, slope_ref, hold, w_hold, hid, slope = refs[count : count + 6]
        sems, w_sems, h_sems, s_sems = refs[count + 6 :]
        w_copies = weight_copies(w_ref, pair_units, w_hold, w_sems)
        for copy in w_copies:
            copy.start()
        copies = start_pieces(layout, piece_refs, rows, hold, sems)
        for copy in w_copies:
            copy.wait()
        kept = []
        for core_step in range(2):
            wait_core(core_step, copies)
            for chunk in range(4 * core_step, 4 * core_step + 4):
                here = slice(chunk * rows, (chunk + 1) * rows)
                block = hold[here, :]
                gate = dot_nt(w_hold[:units, :], block)
                up = dot_nt(w_hold[units:, :], block)
                sig = 0.5 + 0.5 * jnp.tanh(0.5 * gate)
                silu = gate * sig
                hid[:, here] = (silu * up).astype(BF16)
                slope[:units, here] = (up * (sig + silu * (1.0 - sig))).astype(BF16)
                slope[units:, here] = silu.astype(BF16)
            there = pl.ds(core_step * 4 * rows, 4 * rows)
            for made, out, o_sems in ((hid, hid_ref, h_sems), (slope, slope_ref, s_sems)):
                copy = pltpu.make_async_copy(
                    made.at[:, there], out.at[:, there], o_sems.at[core_step]
                )
                copy.start()
                kept.append(copy)
        for copy in kept:
            copy.wait()

    return pl.pallas_call(
        body,
        in_specs=[ANY] * (count + 1),
        out_specs=[ANY, ANY],
        out_shape=[
            jax.ShapeDtypeStruct((units, length), BF16),
            jax.ShapeDtypeStruct((pair_units, length), BF16),
        ],
        scratch_shapes=[
            pltpu.VMEM((length, depth), BF16),
            pltpu.VMEM((pair_units, depth), BF16),
            pltpu.VMEM((units, length), BF16),
            pltpu.VMEM((pair_units, length), BF16),
            pltpu.SemaphoreType.DMA((count,)),
            pltpu.SemaphoreType.DMA((parts,)),
            pltpu.SemaphoreType.DMA((2,)),
            pltpu.SemaphoreType.DMA((2,)),
        ],
        compiler_params=params(),
        cost_estimate=cost(2 * length * depth * pair_units, 22 * MIB),
        name="feed",
    )(weight, *arrays)


def feed_back(pieces, w_down, slopes, w_gate_up):
    pieces = [pieces[number] for number in (5, 6, 7, 8, 9, 0, 1, 2, 3, 4)]
    layout, arrays = split_pieces(pieces)
    rows, depth = arrays[0].shape
    parts, pair_units, cols = w_gate_up.shape
    units = pair_units // 2
    count = len(arrays)
    half = 4 * rows

    def body(wd_ref, s_ref, wg_ref, *refs):
        piece_refs = refs[:count]
        dgu_ref, o_ref, hold, w_hold, slope, wg_hold, made = refs[count : count + 7]
        sems, w_sems, s_sems, wg_sems, d_sems, o_sems = refs[count + 7 :]
        w_copies = weight_copies(wd_ref, units, w_hold, w_sems)
        for copy in w_copies:
            copy.start()
        copies = start_pieces(layout, piece_refs, rows, hold, sems)
        s_copies = []
        for core_step in (1, 0):
            there = pl.ds(core_step * half, half)
            copy = pltpu.make_async_copy(
                s_ref.at[:, there], slope.at[:, there], s_sems.at[core_step]
            )
            copy.start()
            s_copies.append(copy)
        wg_copies = [
            pltpu.make_async_copy(wg_ref.at[part], wg_hold.at[part], wg_sems.at[part])
            for part in range(parts)
        ]
        for copy in wg_copies:
            copy.start()
        for copy in w_copies:
            copy.wait()
        kept = []
        for core_step in (1, 0):
            wait_core(core_step, copies)
            s_copies[1 - core_step].wait()
            for chunk in range(4 * core_step, 4 * core_step + 4):
                here = slice(chunk * rows, (chunk + 1) * rows)
                d_hid = dot_nt(w_hold[...], hold[here, :])
                low = slope[:units, here].astype(F32)
                high = slope[units:, here].astype(F32)
                slope[:units, here] = (d_hid * low).astype(BF16)
                slope[units:, here] = (d_hid * high).astype(BF16)
            there = pl.ds(core_step * half, half)
            copy = pltpu.make_async_copy(
                slope.at[:, there], dgu_ref.at[:, there], d_sems.at[core_step]
            )
            copy.start()
            kept.append(copy)
        for copy in wg_copies:
            copy.wait()
        left = slope[:, half:].T
        for group in range(2):
            columns = pl.ds(group * depth // 2, depth // 2)
            for part in range(group * parts // 2, (group + 1) * parts // 2):
                made[:, part * cols : (part + 1) * cols] = dot_nn(left, wg_hold[part]).astype(BF16)
            copy = pltpu.make_async_copy(
                made.at[:, columns], o_ref.at[:, columns], o_sems.at[group]
            )
            copy.start()
            kept.append(copy)
        for copy in kept:
            copy.wait()

    return pl.pallas_call(
        body,
        in_specs=[ANY] * (count + 3),
        out_specs=[ANY, ANY],
        out_shape=[
            jax.ShapeDtypeStruct((pair_units, 2 * half), BF16),
            jax.ShapeDtypeStruct((half, depth), BF16),
        ],
        scratch_shapes=[
            pltpu.VMEM((2 * half, depth), BF16),
            pltpu.VMEM((units, depth), BF16),
            pltpu.VMEM((pair_units, 2 * half), BF16),
            pltpu.VMEM((parts, pair_units, cols), BF16),
            pltpu.VMEM((half, depth), BF16),
            pltpu.SemaphoreType.DMA((count,)),
            pltpu.SemaphoreType.DMA((parts,)),
            pltpu.SemaphoreType.DMA((2,)),
            pltpu.SemaphoreType.DMA((parts,)),
            pltpu.SemaphoreType.DMA((2,)),
            pltpu.SemaphoreType.DMA((2,)),
        ],
        compiler_params=params(),
        cost_estimate=cost(0, 0),
        name="feed_back",
    )(w_down, slopes, w_gate_up, *arrays)


def unit_grads(pieces, left, parts, name, scale=1):
    layout, arrays = split_pieces(pieces)
    rows, depth = arrays[0].shape
    height, length = left.shape
    cols = depth // parts
    count = len(arrays)

    def body(l_ref, *refs):
        piece_refs = refs[:count]
        out_ref, hold, sems = refs[count:]
        step = pl.program_id(0)
        copy_columns(step, parts, cols, layout, piece_refs, rows, hold, sems)
        columns = pl.ds(pl.multiple_of(step * cols, cols), cols)
        out_ref[0] = dot_nn(l_ref[...], hold[:, columns]).astype(BF16)

    return pl.pallas_call(
        body,
        grid=(parts,),
        in_specs=[pl.BlockSpec((height, length), lambda i: (0, 0), pipeline_mode=pl.Buffered(1))]
        + [ANY] * count,
        out_specs=pl.BlockSpec((1, height, cols), lambda i: (i, 0, 0)),
        out_shape=jax.ShapeDtypeStruct((parts, height, cols), BF16),
        scratch_shapes=[
            pltpu.VMEM((length, depth), BF16),
            pltpu.SemaphoreType.DMA((parts, count)),
        ],
        compiler_params=params(),
        cost_estimate=cost(2 * height * length * depth, 20 * MIB, scale),
        name=name,
    )(left, *arrays)


def rows_scratch(half, units, parts, cols):
    return [
        pltpu.VMEM((parts, units, cols), BF16),
        pltpu.VMEM((half, parts * cols), BF16),
        pltpu.SemaphoreType.DMA,
        pltpu.SemaphoreType.DMA((parts,)),
        pltpu.SemaphoreType.DMA((2,)),
    ]


def rows_of(left_copy, left, w_ref, units, o_ref, w_hold, made, w_sems, o_sems):
    parts, _, cols = w_ref.shape
    w_copies = [
        pltpu.make_async_copy(w_ref.at[part, pl.ds(0, units)], w_hold.at[part], w_sems.at[part])
        for part in range(parts)
    ]
    for copy in w_copies:
        copy.start()
    left_copy.wait()
    block = left()
    kept = []
    for group in range(2):
        members = range(group * parts // 2, (group + 1) * parts // 2)
        for part in members:
            w_copies[part].wait()
        for part in members:
            made[:, part * cols : (part + 1) * cols] = dot_nn(block, w_hold[part]).astype(BF16)
        columns = pl.ds(members.start * cols, len(members) * cols)
        copy = pltpu.make_async_copy(made.at[:, columns], o_ref.at[:, columns], o_sems.at[group])
        copy.start()
        kept.append(copy)
    for copy in kept:
        copy.wait()


def unit_rows(left, weight, core_step, name, scale=1):
    units, length = left.shape
    half = length // 2
    parts, _, cols = weight.shape

    def body(h_ref, w_ref, o_ref, held, w_hold, made, h_sem, w_sems, o_sems):
        h_copy = pltpu.make_async_copy(h_ref.at[:, pl.ds(core_step * half, half)], held, h_sem)
        h_copy.start()
        rows_of(h_copy, lambda: held[...].T, w_ref, units, o_ref, w_hold, made, w_sems, o_sems)

    return pl.pallas_call(
        body,
        in_specs=[ANY, ANY],
        out_specs=ANY,
        out_shape=jax.ShapeDtypeStruct((half, parts * cols), BF16),
        scratch_shapes=[pltpu.VMEM((units, half), BF16)]
        + rows_scratch(half, units, parts, cols),
        compiler_params=params(),
        cost_estimate=cost(2 * half * units * parts * cols, 9 * MIB, scale),
        name=name,
    )(left, weight)


def qkv_rows(pos, d_projected, weight, core_step, scale=1):
    tall, length = d_projected.shape
    rows = length // 8
    parts, _, cols = weight.shape

    def body(pos_ref, l_ref, w_ref, o_ref, held, w_hold, made, h_sem, w_sems, o_sems):
        for number in range(4):
            pltpu.make_async_copy(
                l_ref.at[:, chunk_lanes(pos_ref, 4 * core_step + number, rows)],
                held.at[:, pl.ds(number * rows, rows)],
                h_sem,
            ).start()
        h_copy = pltpu.make_async_copy(l_ref.at[:, pl.ds(0, 4 * rows)], held, h_sem)
        rows_of(h_copy, lambda: held[...].T, w_ref, tall, o_ref, w_hold, made, w_sems, o_sems)

    return pl.pallas_call(
        body,
        in_specs=[SM, ANY, ANY],
        out_specs=ANY,
        out_shape=jax.ShapeDtypeStruct((4 * rows, parts * cols), BF16),
        scratch_shapes=[pltpu.VMEM((tall, 4 * rows), BF16)]
        + rows_scratch(4 * rows, tall, parts, cols),
        compiler_params=params(),
        cost_estimate=cost(8 * rows * tall * parts * cols, 9 * MIB, scale),
        name="d_one_rows_sibling" if core_step else "d_one_rows_own",
    )(pos, d_projected, weight)


def attention_grads(pos, token_pieces, branch_pieces, d_projected, attended, parts):
    x_layout, x_arrays = split_pieces(token_pieces)
    b_layout, b_arrays = split_pieces(branch_pieces)
    rows, depth = x_arrays[0].shape
    width, length = attended.shape
    cols = depth // parts
    x_count, b_count = len(x_arrays), len(b_arrays)

    def body(pos_ref, dp_ref, a_ref, *refs):
        x_refs = refs[:x_count]
        b_refs = refs[x_count : x_count + b_count]
        o_ref, x_hold, b_hold, x_sems, b_sems = refs[x_count + b_count :]
        step = pl.program_id(0)
        columns = pl.ds(pl.multiple_of(step * cols, cols), cols)
        copy_columns(step, parts, cols, x_layout, x_refs, rows, x_hold, x_sems, pos_ref)
        copy_columns(step, parts, cols, b_layout, b_refs, rows, b_hold, b_sems, pos_ref)
        grad = dot_nn(dp_ref[...], x_hold[:, columns])
        for kind in range(3):
            o_ref[0, kind] = grad[kind * width : (kind + 1) * width].T.astype(BF16)
        o_ref[0, 3] = dot_nn(a_ref[...], b_hold[:, columns]).T.astype(BF16)

    whole = pl.Buffered(1)
    return pl.pallas_call(
        body,
        grid_spec=pltpu.PrefetchScalarGridSpec(
            num_scalar_prefetch=1,
            grid=(parts,),
            in_specs=[
                pl.BlockSpec((3 * width, length), lambda i, p: (0, 0), pipeline_mode=whole),
                pl.BlockSpec((width, length), lambda i, p: (0, 0), pipeline_mode=whole),
            ]
            + [ANY] * (x_count + b_count),
            out_specs=pl.BlockSpec((1, 4, cols, width), lambda i, p: (i, 0, 0, 0)),
            scratch_shapes=[
                pltpu.VMEM((length, depth), BF16),
                pltpu.VMEM((length, depth), BF16),
                pltpu.SemaphoreType.DMA((parts, x_count)),
                pltpu.SemaphoreType.DMA((parts, b_count)),
            ],
        ),
        out_shape=jax.ShapeDtypeStruct((parts, 4, cols, width), BF16),
        compiler_params=params(),
        cost_estimate=cost(8 * width * length * depth, 24 * MIB, 0.1),
        name="attention_grads",
    )(pos, d_projected, attended, *x_arrays, *b_arrays)


def chunk_lanes(pos_ref, chunk, rows):
    return pl.ds(pl.multiple_of(pos_ref[chunk] * rows, rows), rows)


def allowed_pairs(first_ref, q_at, k_at, size):
    lanes = pl.ds(pl.multiple_of(q_at * size, size), size)
    k_index = k_at * size + lax.broadcasted_iota(jnp.int32, (size, size), 0)
    q_index = q_at * size + lax.broadcasted_iota(jnp.int32, (size, size), 1)
    return (k_index >= first_ref[:, lanes]) & (k_index <= q_index)


def attend(pos, qkv, doc_first, start_block, size):
    length = qkv.shape[1]
    rows = length // 8
    width = qkv.shape[0] // 3
    heads = width // HEAD_DIM

    def body(pos_ref, start_ref, qkv_ref, first_ref, out_ref, log_ref, *refs):
        block_refs, held, acc = refs[:5], refs[5], refs[6]

        def query_block(q_at, _):
            q_lanes = pl.ds(pl.multiple_of(q_at * size, size), size)
            start = start_ref[q_at]
            every = range(heads)
            queries = [qkv_ref[h * HEAD_DIM : (h + 1) * HEAD_DIM, q_lanes] for h in every]

            def held_rows(k_at):
                return pl.ds(pl.multiple_of((k_at - start) * size, size), size)

            def find_top(k_at, tops):
                k_lanes = pl.ds(pl.multiple_of(k_at * size, size), size)
                mask = allowed_pairs(first_ref, q_at, k_at, size)
                new = []
                for head in every:
                    at = width + head * HEAD_DIM
                    logits = dot_tn(qkv_ref[at : at + HEAD_DIM, k_lanes], queries[head])
                    logits = jnp.where(mask, logits, -1e30)
                    held[head, held_rows(k_at), :] = logits
                    new.append(
                        jnp.maximum(
                            tops[head], jnp.max(logits.reshape(size // 8, 8, size), axis=0)
                        )
                    )
                return tuple(new)

            tops = lax.fori_loop(
                start,
                q_at + 1,
                find_top,
                tuple(jnp.full((8, size), -1e30, F32) for _ in every),
            )
            tops = [jnp.max(top, axis=0, keepdims=True) for top in tops]
            acc[...] = jnp.zeros_like(acc)

            def add_values(k_at, totals):
                k_lanes = pl.ds(pl.multiple_of(k_at * size, size), size)
                expons = []
                new = []
                for head in every:
                    expon = jnp.exp(held[head, held_rows(k_at), :] - tops[head])
                    new.append(
                        totals[head] + jnp.sum(expon.reshape(size // 8, 8, size), axis=0)
                    )
                    expons.append(expon.astype(BF16))
                outs = []
                for head in every:
                    at = 2 * width + head * HEAD_DIM
                    outs.append(dot_nn(qkv_ref[at : at + HEAD_DIM, k_lanes], expons[head]))
                acc[...] += jnp.concatenate(outs, axis=0)
                return tuple(new)

            totals = lax.fori_loop(
                start, q_at + 1, add_values, tuple(jnp.zeros((8, size), F32) for _ in every)
            )
            for head in every:
                total = jnp.sum(totals[head], axis=0, keepdims=True)
                band = slice(head * HEAD_DIM, (head + 1) * HEAD_DIM)
                out_ref[band, q_lanes] = (acc[band, :] / total).astype(BF16)
                log_ref[head : head + 1, q_lanes] = tops[head] + jnp.log(total)
            return 0

        lax.fori_loop(0, length // size, query_block, 0)
        for chunk in range(8):
            block = out_ref[:, chunk_lanes(pos_ref, chunk, rows)]
            if chunk < 4:
                block_refs[chunk][...] = block
            else:
                block_refs[4][chunk - 4] = block

    outs = pl.pallas_call(
        body,
        out_shape=[
            jax.ShapeDtypeStruct((width, length), BF16),
            jax.ShapeDtypeStruct((heads, length), F32),
        ]
        + [jax.ShapeDtypeStruct((width, rows), BF16)] * 4
        + [jax.ShapeDtypeStruct((4, width, rows), BF16)],
        in_specs=[SM, SM, VM, VM],
        out_specs=[VM] * 7,
        scratch_shapes=[
            pltpu.VMEM((heads, length, size), F32),
            pltpu.VMEM((width, size), F32),
        ],
        compiler_params=params(),
        cost_estimate=cost(0, 0),
        name="attend",
    )(pos, start_block, qkv, doc_first)
    return outs[0], outs[1], outs[2:6], outs[6]


def attend_back(
    pos, blocks, qkv, attended, log_sums, cosine, sine, doc_first, start_block, size
):
    width, length = attended.shape
    rows = length // 8
    heads = width // HEAD_DIM
    half_rot = ROT // 2
    scale = 1.0 / math.sqrt(HEAD_DIM)

    def body(pos_ref, start_ref, qkv_ref, att_ref, log_ref, c_ref, s_ref, first_ref, *refs):
        block_refs = refs[:5]
        out_ref, bias_ref, d_att, grads, sems = refs[5:]
        copies = exchanged_copies(
            block_refs, lambda chunk: d_att.at[:, chunk_lanes(pos_ref, chunk, rows)], sems
        )
        for copy in copies:
            copy.start()
        grads[...] = jnp.zeros_like(grads)
        for copy in copies:
            copy.wait()

        def query_block(q_at, _):
            q_lanes = pl.ds(pl.multiple_of(q_at * size, size), size)
            deltas = []
            for head in range(heads):
                at = head * HEAD_DIM
                deltas.append(
                    jnp.sum(
                        d_att[at : at + HEAD_DIM, q_lanes].astype(F32)
                        * att_ref[at : at + HEAD_DIM, q_lanes].astype(F32),
                        axis=0,
                        keepdims=True,
                    )
                )

            def key_block(k_at, _):
                k_lanes = pl.ds(pl.multiple_of(k_at * size, size), size)
                mask = allowed_pairs(first_ref, q_at, k_at, size)
                made = []
                for head in range(heads):
                    at = head * HEAD_DIM
                    key_at, value_at = width + at, 2 * width + at
                    query = qkv_ref[at : at + HEAD_DIM, q_lanes]
                    key = qkv_ref[key_at : key_at + HEAD_DIM, k_lanes]
                    value = qkv_ref[value_at : value_at + HEAD_DIM, k_lanes]
                    d_out = d_att[at : at + HEAD_DIM, q_lanes]
                    logits = dot_tn(key, query)
                    prob = jnp.where(
                        mask, jnp.exp(logits - log_ref[head : head + 1, q_lanes]), 0.0
                    )
                    d_prob = dot_tn(value, d_out)
                    d_logits = (prob * (d_prob - deltas[head])).astype(BF16)
                    made.append((query, key, d_out, d_logits, prob.astype(BF16)))
                for head in range(heads):
                    at = head * HEAD_DIM
                    key_at, value_at = width + at, 2 * width + at
                    query, key, d_out, d_logits, prob = made[head]
                    grads[at : at + HEAD_DIM, q_lanes] += dot_nn(key, d_logits)
                    grads[key_at : key_at + HEAD_DIM, k_lanes] += dot_nt(query, d_logits)
                    grads[value_at : value_at + HEAD_DIM, k_lanes] += dot_nt(d_out, prob)
                return 0

            lax.fori_loop(start_ref[q_at], q_at + 1, key_block, 0)
            return 0

        lax.fori_loop(0, length // size, query_block, 0)

        bias_ref[...] = jnp.zeros_like(bias_ref)

        def finish(at, _):
            lanes = pl.ds(pl.multiple_of(at * rows, rows), rows)
            cosines, sines = c_ref[:, lanes], s_ref[:, lanes]
            for kind in range(3):
                band = grads[kind * width : (kind + 1) * width, lanes]
                if kind == 0:
                    band = band * scale
                if kind < 2:
                    bands = []
                    for first in range(0, width, HEAD_DIM):
                        g_one = band[first : first + half_rot]
                        g_two = band[first + half_rot : first + ROT]
                        bands.append(g_one * cosines + g_two * sines)
                        bands.append(g_two * cosines - g_one * sines)
                        bands.append(band[first + ROT : first + HEAD_DIM])
                    band = jnp.concatenate(bands, axis=0)
                low = band.astype(BF16)
                out_ref[kind * width : (kind + 1) * width, lanes] = low
                bias_ref[kind * width : (kind + 1) * width, :] += jnp.sum(
                    low.astype(F32), axis=1, keepdims=True
                )
            return 0

        lax.fori_loop(0, length // rows, finish, 0)

    return pl.pallas_call(
        body,
        out_shape=[
            jax.ShapeDtypeStruct((3 * width, length), BF16),
            jax.ShapeDtypeStruct((3 * width, 1), F32),
        ],
        in_specs=[SM, SM] + [VM] * 6 + [ANY] * 5,
        out_specs=[VM, VM],
        scratch_shapes=[
            pltpu.VMEM((width, length), BF16),
            pltpu.VMEM((3 * width, length), F32),
            pltpu.SemaphoreType.DMA((8,)),
        ],
        compiler_params=params(),
        cost_estimate=cost(0, 0),
        name="attend_back",
    )(
        pos,
        start_block,
        qkv,
        attended,
        log_sums,
        cosine,
        sine,
        doc_first,
        *blocks,
    )


def doc_tables(doc_lengths, seq_length):
    doc_ends = jnp.cumsum(doc_lengths)
    doc_starts = doc_ends - doc_lengths
    places = jnp.arange(seq_length, dtype=jnp.int32)
    segment = jnp.sum((places[:, None] >= doc_ends[None, :-1]).astype(jnp.int32), axis=1)
    owners = segment[:, None] == jnp.arange(doc_lengths.shape[0], dtype=jnp.int32)[None, :]
    return places, jnp.sum(jnp.where(owners, doc_starts[None, :], 0), axis=1)


def shards(
    tokens,
    lengths,
    ln1_gain,
    ln1_bias,
    qkv_weight,
    qkv_bias,
    out_weight,
    ln2_gain,
    ln2_bias,
    gate_up_weight,
    down_weight,
    cotangent,
    axes,
):
    x = tokens[0]
    cot = cotangent[0]
    rows, depth = x.shape
    length = 8 * rows
    parts = axes["gx"]
    part_rows = depth // parts
    width = qkv_weight.shape[2]
    units = gate_up_weight.shape[2]
    size = 256
    gain_one = ln1_gain.astype(F32)[None]
    shift_one = ln1_bias.astype(F32)[None]
    gain_two = ln2_gain.astype(F32)[None]
    shift_two = ln2_bias.astype(F32)[None]

    attn_weight = jnp.concatenate(
        [qkv_weight.transpose(1, 2, 0).reshape(3 * width, part_rows), out_weight.T], axis=0
    )
    w_attn = lax.all_gather(attn_weight, "gx", axis=0, tiled=False)
    w_gate_up = lax.all_gather(
        gate_up_weight.transpose(1, 2, 0).reshape(2 * units, part_rows), "gx", axis=0, tiled=False
    )
    w_down = lax.all_gather(down_weight.T, "gx", axis=0, tiled=False)

    steps = jnp.arange(8, dtype=jnp.int32)
    pos = (lax.axis_index("gy") ^ (steps % 4)) * 2 + (lax.axis_index("gz") ^ (steps // 4))
    places, doc_first = doc_tables(lengths[0], length)
    start_block = doc_first[:: size] // size
    frequency = jnp.exp(
        jnp.arange(ROT // 2, dtype=F32) * (-2.0 * math.log(10000.0) / ROT)
    )
    angles = frequency[:, None] * (places - doc_first).astype(F32)[None, :]
    cosine, sine = jnp.cos(angles), jnp.sin(angles)
    doc_first = doc_first[None]

    bias_column = qkv_bias.astype(F32).reshape(3 * width, 1)
    normed_one = norm_one(x, gain_one, shift_one)
    one_pieces = gather_plane(normed_one, bias_column, cosine, sine, doc_first, start_block)
    cot_block = after(cot, one_pieces[1][0], one_pieces[2][0])
    cot_pieces = gather_plane(cot_block)
    out_block = w_attn[:, 3 * width :].transpose(1, 0, 2).reshape(width, depth)
    out_first = gather_first(out_block)
    qkv = project(
        pos,
        one_pieces,
        w_attn,
        after(bias_column, cot_pieces[3][0], cot_pieces[4][0], out_block),
        cosine,
        sine,
    )
    qkv = after(qkv, out_first[1], out_first[2], *[piece for piece, _, _ in cot_pieces])
    attended, log_sums, *blocks = attend(pos, qkv, doc_first, start_block, size)
    exchanged = []

    def exchange(*arrived):
        exchanged.extend(exchange_second(*exchange_first(*after(tuple(blocks), *arrived))))
        return exchanged[2:]

    out_pieces = gather_second(out_first, (qkv,), exchange)
    blocks = exchanged
    middle, normed_two = middle_norm(
        after(x, *[piece for piece, _, _ in cot_pieces]), blocks, out_pieces, gain_two, shift_two
    )

    two_pieces = gather_plane(normed_two)
    hidden, slopes = feed(two_pieces, w_gate_up)
    down_grad = unit_grads(cot_pieces, hidden, parts, "down_grads")
    down_grad_sum = lax.psum_scatter(down_grad, "gx", scatter_dimension=0, tiled=False)
    d_gate_up, d_two_sib = feed_back(cot_pieces, w_down, after(slopes, down_grad), w_gate_up)
    d_two_own = unit_rows(after(d_gate_up, d_two_sib), w_gate_up, 0, "d_two_rows_own", 0.3)
    came, sent = scatter_first(d_two_own, d_two_sib, rows)
    gate_up_grad = unit_grads(two_pieces, after(d_gate_up, *sent), parts, "gate_up_grads", 0.05)
    gate_up_grad_sum = lax.psum_scatter(gate_up_grad, "gx", scatter_dimension=0, tiled=False)
    sent, arrived = scatter_second(d_two_own, came, sent, rows, gate_up_grad, down_grad_sum)
    mlp_sib = unit_rows(
        after(hidden, gate_up_grad, *sent), w_down, 1, "mlp_rows_sibling", 0.1
    )
    d_two = scatter_last(d_two_own, came, sent, arrived)

    d_branch, norm_two_sums, d_middle, own_blocks, other_blocks = norm_two_back(
        after(middle, mlp_sib), cot, d_two, gain_two, out_pieces
    )
    blocks = exchange_second(*exchange_first(own_blocks, other_blocks))
    d_projected, bias_sums = attend_back(
        pos, blocks, qkv, attended, log_sums, cosine, sine, doc_first, start_block, size
    )
    branch_pieces = gather_plane(after(d_branch, *blocks[2:]), d_projected)
    d_one_sib = qkv_rows(
        pos, after(d_projected, branch_pieces[1][0], branch_pieces[2][0]), w_attn, 1, 0.1
    )
    d_one_own = qkv_rows(pos, after(d_projected, d_one_sib), w_attn, 0, 0.1)
    came, sent = scatter_first(d_one_own, d_one_sib, rows)
    attn_grads = attention_grads(
        pos, one_pieces, branch_pieces, d_projected, after(attended, *sent), parts
    )
    attn_grads_sum = lax.psum_scatter(attn_grads, "gx", scatter_dimension=0, tiled=False)
    sent, arrived = scatter_second(d_one_own, came, sent, rows, attn_grads)
    mlp_own = unit_rows(after(hidden, *sent), w_down, 0, "mlp_rows_own")
    mlp_came, mlp_sent = scatter_first(mlp_own, after(mlp_sib, *sent), rows)
    d_one = scatter_last(d_one_own, came, sent, arrived)
    gate_up_out = gate_up_grad_sum.astype(F32).reshape(2, units, part_rows).transpose(2, 0, 1)
    down_out = down_grad_sum.astype(F32).T
    input_grad, norm_one_sums = norm_one_back(
        after(x, gate_up_out, down_out), d_middle, d_one, gain_one
    )

    mlp_sent = after(mlp_sent, input_grad)
    mlp_sent, mlp_arrived = scatter_second(mlp_own, mlp_came, mlp_sent, rows)
    mlp = scatter_last(mlp_own, mlp_came, mlp_sent, mlp_arrived)
    half = rows // 2
    total = mlp[0][:rows].astype(F32) + mlp[1][:rows].astype(F32)
    total = total + jnp.concatenate(
        [
            mlp[2][half:].astype(F32) + mlp[4].astype(F32),
            mlp[3].astype(F32) + mlp[5][half:].astype(F32),
        ],
        axis=0,
    )
    activations = (middle + total).astype(BF16)

    bias_row = jnp.pad(bias_sums.reshape(1, 3 * width), ((0, 0), (0, depth - 3 * width)))
    small = jnp.concatenate([norm_one_sums, norm_two_sums, bias_row], axis=0)
    small = sum_all(small, [("gx", axes["gx"])])
    bias_sum = small[4, : 3 * width].reshape(3, width)
    norm_sums = sum_all(small[:4], [("gz", axes["gz"]), ("gy", axes["gy"])])
    attn_grads_sum = after(attn_grads_sum, activations, norm_sums, bias_sum).astype(F32)
    return (
        activations[None],
        input_grad[None],
        norm_sums[0],
        norm_sums[1],
        attn_grads_sum[:3].transpose(1, 0, 2),
        bias_sum,
        attn_grads_sum[3],
        norm_sums[2],
        norm_sums[3],
        gate_up_out,
        down_out,
    )


def solution(mesh):
    axes = dict(mesh.shape)
    placed = (
        P("gx", ("gy", "gz"), None),
        P("gx", None),
        P(),
        P(),
        P("gx", None, ("gy", "gz")),
        P(None, ("gy", "gz")),
        P("gx", ("gy", "gz")),
        P(),
        P(),
        P("gx", None, ("gy", "gz")),
        P("gx", ("gy", "gz")),
        P("gx", ("gy", "gz"), None),
    )
    return jax.shard_map(
        lambda *args: shards(*args, axes),
        mesh=mesh,
        in_specs=placed,
        out_specs=(
            P("gx", ("gy", "gz"), None),
            P("gx", ("gy", "gz"), None),
            P(),
            P(),
            P("gx", None, ("gy", "gz")),
            P(None, ("gy", "gz")),
            P("gx", ("gy", "gz")),
            P(),
            P(),
            P("gx", None, ("gy", "gz")),
            P("gx", ("gy", "gz")),
        ),
        check_vma=False,
    )
```

profile of v0, /device:TPU:0, one launch (start us, length us, event | category | flops | bytes accessed | tf_op | source)
XLA Modules:
  0.0 552.0 jit_solution(8460656807221160061)
XLA Ops:
  12.8 3.0 norm_one.1.refs_0_
  16.3 2.5 collective-permute-start.1
  22.3 20.5 %collective-permute-done.1.refs_2_ = bf16[256,2048]{1,0:T(8,128)(2,1)S(1)} collective-permute-done((bf16[256,2048]{1,0:T(8,128)(2,1)}, bf16[256,2048]{1,0:T(8,128)(2,1)S(1)}, u32[]{:S(2)}, u32[]{:S(2)}) %collective-permute-start.1) | collective-permute-done | bytes 1048608 | tf_op jit(solution)/shard_map/ppermute | solution.py:28
  49.1 8.7 %collective-permute-done.13.refs_3_ = bf16[128,2048]{1,0:T(8,128)(2,1)S(1)} collective-permute-done((bf16[128,2048]{1,0:T(8,128)(2,1)S(1)}, bf16[128,2048]{1,0:T(8,128)(2,1)S(1)}, u32[]{:S(2)}, u32[]{:S(2)}) %collective-permute-start.13) | collective-permute-done | bytes 524320 | tf_op jit(solution)/shard_map/ppermute | solution.py:24
  57.7 22.8 %collective-permute-done.14.refs_4_ = bf16[128,2048]{1,0:T(8,128)(2,1)S(1)} collective-permute-done((bf16[128,2048]{1,0:T(8,128)(2,1)S(1)}, bf16[128,2048]{1,0:T(8,128)(2,1)S(1)}, u32[]{:S(2)}, u32[]{:S(2)}) %collective-permute-start.14) | collective-permute-done | bytes 524320 | tf_op jit(solution)/shard_map/ppermute | solution.py:28
  88.4 6.0 %all-gather.8.cloned.1.call-done = bf16[4096,512]{1,0:T(8,128)(2,1)} async-done(((bf16[1024,512]{1,0:T(8,128)(2,1)}), bf16[4096,512]{1,0:T(8,128)(2,1)}) %all-gather.8.cloned.1.call-update) | async-done | bytes 4194320 | tf_op jit(solution)/shard_map/all_gather | solution.py:1076
  97.0 3.0 collective-permute-done.4.refs_3_.refs_8_
  104.6 13.6 %project.1.qkv_ref = bf16[768,2048]{1,0:T(8,128)(2,1)} custom-call(s32[8]{0:T(128)} %fusion.4.pos_ref, bf16[4,1024,512]{2,1,0:T(8,128)(2,1)} %bitcast.64, f32[768,1]{1,0:T(8,128)} %copy.47.b_ref, f32[8,2048]{1,0:T(8,128)} %get-tuple-element.195.c_ref, f32[8,2048]{1,0:T(8,128)} %get-tuple-element.194.s_ref, bf16[256,2048]{1,0:T(8,128)(2,1)} %norm_one.1.refs_0_, ...), custom_call_target="tpu_custom_call" | custom-call | flops 6442450944 | bytes 15728640 | tf_op jit(solution)/shard_map/project/pallas_call | solution.py:461
  118.2 6.5 %collective-permute-done.12.refs_2_.refs_9_ = bf16[256,2048]{1,0:T(8,128)(2,1)S(1)} collective-permute-done((bf16[256,2048]{1,0:T(8,128)(2,1)S(1)}, bf16[256,2048]{1,0:T(8,128)(2,1)S(1)}, u32[]{:S(2)}, u32[]{:S(2)}) %collective-permute-start.12) | collective-permute-done | bytes 1048608 | tf_op jit(solution)/shard_map/ppermute | solution.py:28
  128.6 15.6 %attend.1 = (bf16[256,2048]{1,0:T(8,128)(2,1)}, f32[4,2048]{1,0:T(4,128)}, bf16[256,256]{1,0:T(8,128)(2,1)}, bf16[256,256]{1,0:T(8,128)(2,1)}, bf16[256,256]{1,0...) custom-call(s32[8]{0:T(128)} %fusion.4.pos_ref, s32[8]{0:T(128)} %and_select_fusion.start_ref, ...), custom_call_target="tpu_custom_call" | custom-call | tf_op jit(solution)/shard_map/attend/pallas_call | solution.py:891
  152.7 5.7 %collective-permute-done.24.refs_12_ = bf16[2,256,256]{2,1,0:T(8,128)(2,1)S(1)} collective-permute-done((bf16[2,256,256]{2,1,0:T(8,128)(2,1)S(1)}, bf16[2,256,256]{2,1,0:T(8,128)(2,1)S(1)}, u32[]{:S(2)}, u32[]{:S(2)}) %collective-permute-start.24) | collective-permute-done | bytes 262176 | tf_op jit(solution)/shard_map/ppermute | solution.py:24
  158.3 5.1 collective-permute-done.25.refs_13_
  169.5 9.2 %middle_norm.1 = (f32[256,2048]{1,0:T(8,128)}, bf16[256,2048]{1,0:T(8,128)(2,1)}) custom-call(bf16[256,2048]{1,0:T(8,128)(2,1)} %bitcast.71, f32[1,2048]{1,0:T(1,128)} %bitcast.97, f32[1,2048]{1,0:T(1,128)} %bitcast.99, bf16[256,2048]{1,0:T(8,128)(2,1)} %copy-done.1, bf16[256,2048]{1,0:T(8,128)(2,1)} %copy-done.4, bf16[256,2048]{1,0:T(8,128)(2,1)} %copy-done.3, ...), custom_call_target="tpu_custom_call" | custom-call | flops 2147483648 | bytes 14680064 | tf_op jit(solution)/shard_map/middle_norm/pallas_call | solution.py:224
  180.8 23.4 %collective-permute-done.32.refs_2_ = bf16[256,2048]{1,0:T(8,128)(2,1)S(1)} collective-permute-done((bf16[256,2048]{1,0:T(8,128)(2,1)}, bf16[256,2048]{1,0:T(8,128)(2,1)S(1)}, u32[]{:S(2)}, u32[]{:S(2)}) %collective-permute-start.32) | collective-permute-done | bytes 1048608 | tf_op jit(solution)/shard_map/ppermute | solution.py:28
  206.9 10.6 %collective-permute-done.33.refs_3_ = bf16[128,2048]{1,0:T(8,128)(2,1)} collective-permute-done((bf16[128,2048]{1,0:T(8,128)(2,1)S(1)}, bf16[128,2048]{1,0:T(8,128)(2,1)}, u32[]{:S(2)}, u32[]{:S(2)}) %collective-permute-start.33) | collective-permute-done | bytes 524320 | tf_op jit(solution)/shard_map/ppermute | solution.py:24
  217.5 2.9 collective-permute-done.34.refs_4_
  222.7 21.3 %feed.1 = (bf16[704,2048]{1,0:T(8,128)(2,1)}, bf16[1408,2048]{1,0:T(8,128)(2,1)}) custom-call(bf16[4,1408,512]{2,1,0:T(8,128)(2,1)} %all-gather.6.cloned.1.call-done.w_ref.wg_ref, bf16[256,2048]{1,0:T(8,128)(2,1)} %get-tuple-element.114.refs_0_, bf16[256,2048]{1,0:T(8,128)(2,1)} %copy-done.10, bf16[256,2048]{1,0:T(8,128)(2,1)} %copy-done.9, ...), custom_call_target="tpu_custom_call" | custom-call | flops 11811160064 | bytes 23068672 | tf_op jit(solution)/shard_map/feed/pallas_call | solution.py:521
  244.0 11.4 %down_grads.1 = bf16[4,704,512]{2,1,0:T(8,128)(2,1)} custom-call(bf16[704,2048]{1,0:T(8,128)(2,1)} %get-tuple-element.149.l_ref.h_ref, bf16[256,2048]{1,0:T(8,128)(2,1)} %bitcast.74, bf16[256,2048]{1,0:T(8,128)(2,1)} %copy-done.8, bf16[256,2048]{1,0:T(8,128)(2,1)} %collective-permute-done.3.refs_2_.refs_7_, ...), custom_call_target="tpu_custom_call" | custom-call | flops 5905580032 | bytes 20971520 | tf_op jit(solution)/shard_map/down_grads/pallas_call | solution.py:652
  255.4 4.9 all-gather.10.cloned.1.call-done
  260.4 21.1 %feed_back.1 = (bf16[1408,2048]{1,0:T(8,128)(2,1)}, bf16[1024,2048]{1,0:T(8,128)(2,1)}) custom-call(bf16[4,704,512]{2,1,0:T(8,128)(2,1)} %bitcast.67, bf16[1408,2048]{1,0:T(8,128)(2,1)} %get-tuple-element.119.s_ref, bf16[4,1408,512]{2,1,0:T(8,128)(2,1)} %all-gather.6.cloned.1.call-done.w_ref.wg_ref, ...), custom_call_target="tpu_custom_call" | custom-call | tf_op jit(solution)/shard_map/feed_back/pallas_call | solution.py:610
  281.8 12.2 %d_two_rows_own.1.refs_0_ = bf16[1024,2048]{1,0:T(8,128)(2,1)} custom-call(bf16[1408,2048]{1,0:T(8,128)(2,1)} %get-tuple-element.124.h_ref.l_ref, bf16[4,1408,512]{2,1,0:T(8,128)(2,1)} %all-gather.6.cloned.1.call-done.w_ref.wg_ref), custom_call_target="tpu_custom_call" | custom-call | flops 1771673984 | bytes 2831155 | tf_op jit(solution)/shard_map/d_two_rows_own/pallas_call | solution.py:714
  294.0 2.9 add_convert_fusion.15
  301.1 18.4 %gate_up_grads.1 = bf16[4,1408,512]{2,1,0:T(8,128)(2,1)} custom-call(bf16[1408,2048]{1,0:T(8,128)(2,1)} %get-tuple-element.124.h_ref.l_ref, bf16[256,2048]{1,0:T(8,128)(2,1)} %get-tuple-element.114.refs_0_, bf16[256,2048]{1,0:T(8,128)(2,1)} %copy-done.10, bf16[256,2048]{1,0:T(8,128)(2,1)} %copy-done.9, bf16[128,2048]{1,0:T(8,128)(2,1)} %collective-permute-done.33.refs_3_, ...), custom_call_target="tpu_custom_call" | custom-call | flops 590558016 | bytes 1048576 | tf_op jit(solution)/shard_map/gate_up_grads/pallas_call | solution.py:652
  319.9 4.1 collective-permute-done.41.refs_2_
  324.9 2.4 add_convert_fusion.12
  329.8 7.5 %mlp_rows_sibling.1 = bf16[1024,2048]{1,0:T(8,128)(2,1)} custom-call(bf16[704,2048]{1,0:T(8,128)(2,1)} %get-tuple-element.149.l_ref.h_ref, bf16[4,704,512]{2,1,0:T(8,128)(2,1)} %bitcast.68), custom_call_target="tpu_custom_call" | custom-call | flops 295279008 | bytes 943718 | tf_op jit(solution)/shard_map/mlp_rows_sibling/pallas_call | solution.py:714
  337.3 3.5 collective-permute-done.43.refs_3_
  342.5 10.6 %norm_two_back.1 = (bf16[256,2048]{1,0:T(8,128)(2,1)}, f32[2,2048]{1,0:T(2,128)}, f32[256,2048]{1,0:T(8,128)}, bf16[256,256]{1,0:T(8,128)(2,1)}, bf16[256,256]{1...) custom-call(f32[256,2048]{1,0:T(8,128)} %get-tuple-element.128.v_ref, ...), custom_call_target="tpu_custom_call" | custom-call | tf_op jit(solution)/shard_map/norm_two_back/pallas_call | solution.py:286
  361.5 5.7 %collective-permute-done.46.refs_2_ = bf16[2,256,256]{2,1,0:T(8,128)(2,1)S(1)} collective-permute-done((bf16[2,256,256]{2,1,0:T(8,128)(2,1)S(1)}, bf16[2,256,256]{2,1,0:T(8,128)(2,1)S(1)}, u32[]{:S(2)}, u32[]{:S(2)}) %collective-permute-start.46) | collective-permute-done | bytes 262176 | tf_op jit(solution)/shard_map/ppermute | solution.py:24
  367.2 4.3 collective-permute-done.47.refs_3_
  375.0 23.1 %attend_back.1 = (bf16[768,2048]{1,0:T(8,128)(2,1)}, f32[768,1]{1,0:T(8,128)}) custom-call(s32[8]{0:T(128)} %fusion.4.pos_ref, s32[8]{0:T(128)} %and_select_fusion.start_ref, bf16[768,2048]{1,0:T(8,128)(2,1)} %project.1.qkv_ref, bf16[256,2048]{1,0:T(8,128)(2,1)} %get-tuple-element.144.att_ref.a_ref, f32[4,2048]{1,0:T(4,128)} %get-tuple-element.117.log_ref, ...), custom_call_target="tpu_custom_call" | custom-call | tf_op jit(solution)/shard_map/attend_back/pallas_call | solution.py:1006
  399.1 8.2 %d_one_rows_sibling.1 = bf16[1024,2048]{1,0:T(8,128)(2,1)} custom-call(s32[8]{0:T(128)} %fusion.4.pos_ref, bf16[768,2048]{1,0:T(8,128)(2,1)} %get-tuple-element.141.l_ref.dp_ref, bf16[4,1024,512]{2,1,0:T(8,128)(2,1)} %bitcast.65), custom_call_target="tpu_custom_call" | custom-call | flops 322122560 | bytes 943718 | tf_op jit(solution)/shard_map/d_one_rows_sibling/pallas_call | solution.py:742
  412.1 8.2 %d_one_rows_own.1.refs_0_ = bf16[1024,2048]{1,0:T(8,128)(2,1)} custom-call(s32[8]{0:T(128)} %fusion.4.pos_ref, bf16[768,2048]{1,0:T(8,128)(2,1)} %get-tuple-element.141.l_ref.dp_ref, bf16[4,1024,512]{2,1,0:T(8,128)(2,1)} %bitcast.66), custom_call_target="tpu_custom_call" | custom-call | flops 322122560 | bytes 943718 | tf_op jit(solution)/shard_map/d_one_rows_own/pallas_call | solution.py:742
  420.3 2.5 collective-permute-done.54.refs_13_
  423.4 3.5 add_convert_fusion.9
  433.6 19.0 %attention_grads.1 = bf16[4,4,512,256]{3,2,1,0:T(8,128)(2,1)} custom-call(s32[8]{0:T(128)} %fusion.4.pos_ref, bf16[768,2048]{1,0:T(8,128)(2,1)} %get-tuple-element.141.l_ref.dp_ref, bf16[256,2048]{1,0:T(8,128)(2,1)} %get-tuple-element.144.att_ref.a_ref, bf16[256,2048]{1,0:T(8,128)(2,1)} %norm_one.1.refs_0_, bf16[256,2048]{1,0:T(8,128)(2,1)} %collective-permute-done.refs_1_, ...), custom_call_target="tpu_custom_call" | custom-call | flops 858993472 | bytes 2516582 | tf_op jit(solution)/shard_map/attention_grads/pallas_call | solution.py:777
  455.6 3.0 add_convert_fusion.6
  458.7 2.5 convert_bitcast_fusion.1
  463.1 7.5 %mlp_rows_own.1 = bf16[1024,2048]{1,0:T(8,128)(2,1)} custom-call(bf16[704,2048]{1,0:T(8,128)(2,1)} %get-tuple-element.149.l_ref.h_ref, bf16[4,704,512]{2,1,0:T(8,128)(2,1)} %bitcast.69), custom_call_target="tpu_custom_call" | custom-call | flops 2952790016 | bytes 9437184 | tf_op jit(solution)/shard_map/mlp_rows_own/pallas_call | solution.py:714
  470.6 3.3 convert_bitcast_fusion
  477.1 6.5 %norm_one_back.1 = (bf16[256,2048]{1,0:T(8,128)(2,1)}, f32[2,2048]{1,0:T(2,128)}) custom-call(bf16[256,2048]{1,0:T(8,128)(2,1)} %bitcast.72, f32[256,2048]{1,0:T(8,128)} %get-tuple-element.154.u_ref, bf16[1024,2048]{1,0:T(8,128)(2,1)} %d_one_rows_own.1.refs_0_, bf16[1024,2048]{1,0:T(8,128)(2,1)} %copy-done, bf16[256,2048]{1,0:T(8,128)(2,1)} %copy-done.13, ...), custom_call_target="tpu_custom_call" | custom-call | bytes 8388608 | tf_op jit(solution)/shard_map/norm_one_back/pallas_call | solution.py:324
  484.4 5.1 collective-permute-start.69
  490.1 2.3 add_convert_fusion.3
  497.6 2.8 collective-permute-done.68
  505.2 12.4 %collective-permute-done.64 = bf16[256,2048]{1,0:T(8,128)(2,1)} collective-permute-done((bf16[256,2048]{1,0:T(8,128)(2,1)S(1)}, bf16[256,2048]{1,0:T(8,128)(2,1)}, u32[]{:S(2)}, u32[]{:S(2)}) %collective-permute-start.64) | collective-permute-done | bytes 1048608 | tf_op jit(solution)/shard_map/ppermute | solution.py:24
  523.0 9.0 %collective-permute-done.66 = bf16[128,2048]{1,0:T(8,128)(2,1)S(1)} collective-permute-done((bf16[128,2048]{1,0:T(8,128)(2,1)S(1)}, bf16[128,2048]{1,0:T(8,128)(2,1)S(1)}, u32[]{:S(2)}, u32[]{:S(2)}) %collective-permute-start.66) | collective-permute-done | bytes 524320 | tf_op jit(solution)/shard_map/ppermute | solution.py:28
  533.3 3.1 fusion.1
  536.4 4.8 reduce-scatter.8.cloned.1.call-done
  (306 shorter events, 120.3 us)
Async XLA Ops:
  7.2 87.3 %all-gather.8.cloned.1.call-start = ((), (), s32[]{:S(2)}) async-start(), calls=%async_computation.7 | async-start | bytes 5242880 | tf_op jit(solution)/shard_map/all_gather | solution.py:1076
  10.8 209.6 %all-gather.6.cloned.1.call-start = ((), (), s32[]{:S(2)}) async-start(), calls=%async_computation.3 | async-start | bytes 7208960 | tf_op jit(solution)/shard_map/all_gather | solution.py:1077
  11.6 248.8 %all-gather.10.cloned.1.call-start = ((), (), s32[]{:S(2)}) async-start(), calls=%async_computation.8 | async-start | bytes 3604480 | tf_op jit(solution)/shard_map/all_gather | solution.py:1080
  15.8 33.3 %collective-permute-start.15 = (bf16[256,2048]{1,0:T(8,128)(2,1)}, bf16[256,2048]{1,0:T(8,128)(2,1)}, u32[]{:S(2)}, u32[]{:S(2)}) collective-permute-start(bf16[256,2048]{1,0:T(8,128)(2,1)} %norm_one.1.refs_0_), channel_id=1, source_target_pairs={{0,1},{1,0},{2,3},{3,2},{4,5},{5,4},{6,7},{7,6},{8,9},{9,8},{10,11... | collective-permute-start | bytes 3145736 | tf_op jit(solution)/shard_map/ppermute | solution.py:40
  16.3 26.6 %collective-permute-start.1 = (bf16[256,2048]{1,0:T(8,128)(2,1)}, bf16[256,2048]{1,0:T(8,128)(2,1)S(1)}, u32[]{:S(2)}, u32[]{:S(2)}) collective-permute-start(bf16[256,2048]{1,0:T(8,128)(2,1)} %norm_one.1.refs_0_), channel_id=1, source_target_pairs={{0,4},{4,0},{2,6},{6,2},{1,5},{5,1},{3,7},{7,3},{8,12},{12,8},{10,... | collective-permute-start | bytes 3145736 | tf_op jit(solution)/shard_map/ppermute | solution.py:28
  18.8 25.9 %collective-permute-start = (bf16[256,2048]{1,0:T(8,128)(2,1)}, bf16[256,2048]{1,0:T(8,128)(2,1)}, u32[]{:S(2)}, u32[]{:S(2)}) collective-permute-start(bf16[256,2048]{1,0:T(8,128)(2,1)} %norm_one.1.refs_0_), channel_id=1, source_target_pairs={{0,2},{2,0},{4,6},{6,4},{1,3},{3,1},{5,7},{7,5},{8,10},{10,8},{12,... | collective-permute-start | bytes 3145736 | tf_op jit(solution)/shard_map/ppermute | solution.py:24
  42.9 14.8 %collective-permute-start.13 = (bf16[128,2048]{1,0:T(8,128)(2,1)S(1)}, bf16[128,2048]{1,0:T(8,128)(2,1)S(1)}, u32[]{:S(2)}, u32[]{:S(2)}) collective-permute-start(bf16[128,2048]{1,0:T(8,128)(2,1)S(1)} %slice.305), channel_id=1, source_target_pairs={{0,2},{2,0},{4,6},{6,4},{1,3},{3,1},{5,7},{7,5},{8,10},{10,8},{12,... | collective-permute-start | bytes 1572872 | tf_op jit(solution)/shard_map/ppermute | solution.py:24
  44.7 36.4 %collective-permute-start.3 = (bf16[256,2048]{1,0:T(8,128)(2,1)S(1)}, bf16[256,2048]{1,0:T(8,128)(2,1)}, u32[]{:S(2)}, u32[]{:S(2)}) collective-permute-start(bf16[256,2048]{1,0:T(8,128)(2,1)S(1)} %bitcast.77), channel_id=1, source_target_pairs={{0,4},{4,0},{2,6},{6,2},{1,5},{5,1},{3,7},{7,3},{8,12},{12,8},{10,... | collective-permute-start | bytes 3145736 | tf_op jit(solution)/shard_map/ppermute | solution.py:28
  46.2 34.9 %collective-permute-start.2 = (bf16[256,2048]{1,0:T(8,128)(2,1)S(1)}, bf16[256,2048]{1,0:T(8,128)(2,1)S(1)}, u32[]{:S(2)}, u32[]{:S(2)}) collective-permute-start(bf16[256,2048]{1,0:T(8,128)(2,1)S(1)} %bitcast.78), channel_id=1, source_target_pairs={{0,2},{2,0},{4,6},{6,4},{1,3},{3,1},{5,7},{7,5},{8,10},{10,8},{12,... | collective-permute-start | bytes 3145736 | tf_op jit(solution)/shard_map/ppermute | solution.py:24
  47.8 32.7 %collective-permute-start.14 = (bf16[128,2048]{1,0:T(8,128)(2,1)S(1)}, bf16[128,2048]{1,0:T(8,128)(2,1)S(1)}, u32[]{:S(2)}, u32[]{:S(2)}) collective-permute-start(bf16[128,2048]{1,0:T(8,128)(2,1)S(1)} %slice.306), channel_id=1, source_target_pairs={{0,4},{4,0},{2,6},{6,2},{1,5},{5,1},{3,7},{7,3},{8,12},{12,8},{10,... | collective-permute-start | bytes 1572872 | tf_op jit(solution)/shard_map/ppermute | solution.py:28
  49.1 35.5 %collective-permute-start.17 = (bf16[256,2048]{1,0:T(8,128)(2,1)S(1)}, bf16[256,2048]{1,0:T(8,128)(2,1)S(1)}, u32[]{:S(2)}, u32[]{:S(2)}) collective-permute-start(bf16[256,2048]{1,0:T(8,128)(2,1)S(1)} %collective-permute-done.1.refs_2_), channel_id=1, source_target_pairs={{0,1},{1,0},{2,3},{3,2},{4,5},{5,4},{6,7},{7,6},{8,9},{9,8},{10,11... | collective-permute-start | bytes 3145736 | tf_op jit(solution)/shard_map/ppermute | solution.py:40
  57.7 22.8 %collective-permute-start.18 = (bf16[128,2048]{1,0:T(8,128)(2,1)S(1)}, bf16[128,2048]{1,0:T(8,128)(2,1)S(1)}, u32[]{:S(2)}, u32[]{:S(2)}) collective-permute-start(bf16[128,2048]{1,0:T(8,128)(2,1)S(1)} %collective-permute-done.13.refs_3_), channel_id=1, source_target_pairs={{0,1},{1,0},{2,3},{3,2},{4,5},{5,4},{6,7},{7,6},{8,9},{9,8},{10,11... | collective-permute-start | bytes 1572872 | tf_op jit(solution)/shard_map/ppermute | solution.py:40
  80.5 16.4 %collective-permute-start.6 = (bf16[256,2048]{1,0:T(8,128)(2,1)S(1)}, bf16[256,2048]{1,0:T(8,128)(2,1)}, u32[]{:S(2)}, u32[]{:S(2)}) collective-permute-start(bf16[256,2048]{1,0:T(8,128)(2,1)S(1)} %bitcast.79), channel_id=1, source_target_pairs={{0,1},{1,0},{2,3},{3,2},{4,5},{5,4},{6,7},{7,6},{8,9},{9,8},{10,11... | collective-permute-start | bytes 3145736 | tf_op jit(solution)/shard_map/ppermute | solution.py:40
  81.0 23.1 %collective-permute-start.16 = (bf16[256,2048]{1,0:T(8,128)(2,1)}, bf16[256,2048]{1,0:T(8,128)(2,1)}, u32[]{:S(2)}, u32[]{:S(2)}) collective-permute-start(bf16[256,2048]{1,0:T(8,128)(2,1)} %collective-permute-done.refs_1_), channel_id=1, source_target_pairs={{0,1},{1,0},{2,3},{3,2},{4,5},{5,4},{6,7},{7,6},{8,9},{9,8},{10,11... | collective-permute-start | bytes 3145736 | tf_op jit(solution)/shard_map/ppermute | solution.py:40
  81.4 22.8 %collective-permute-start.8 = (bf16[256,2048]{1,0:T(8,128)(2,1)}, bf16[256,2048]{1,0:T(8,128)(2,1)}, u32[]{:S(2)}, u32[]{:S(2)}) collective-permute-start(bf16[256,2048]{1,0:T(8,128)(2,1)} %collective-permute-done.3.refs_2_.refs_7_), channel_id=1, source_target_pairs={{0,1},{1,0},{2,3},{3,2},{4,5},{5,4},{6,7},{7,6},{8,9},{9,8},{10,11... | collective-permute-start | bytes 3145736 | tf_op jit(solution)/shard_map/ppermute | solution.py:40
  85.5 14.5 %collective-permute-start.4 = (bf16[128,2048]{1,0:T(8,128)(2,1)}, bf16[128,2048]{1,0:T(8,128)(2,1)}, u32[]{:S(2)}, u32[]{:S(2)}) collective-permute-start(bf16[128,2048]{1,0:T(8,128)(2,1)} %slice.301), channel_id=1, source_target_pairs={{0,2},{2,0},{4,6},{6,4},{1,3},{3,1},{5,7},{7,5},{8,10},{10,8},{12,... | collective-permute-start | bytes 1572872 | tf_op jit(solution)/shard_map/ppermute | solution.py:24
  87.5 14.2 %collective-permute-start.5 = (bf16[128,2048]{1,0:T(8,128)(2,1)}, bf16[128,2048]{1,0:T(8,128)(2,1)}, u32[]{:S(2)}, u32[]{:S(2)}) collective-permute-start(bf16[128,2048]{1,0:T(8,128)(2,1)} %slice.302), channel_id=1, source_target_pairs={{0,4},{4,0},{2,6},{6,2},{1,5},{5,1},{3,7},{7,3},{8,12},{12,8},{10,... | collective-permute-start | bytes 1572872 | tf_op jit(solution)/shard_map/ppermute | solution.py:28
  97.0 21.2 %collective-permute-start.7 = (bf16[256,2048]{1,0:T(8,128)(2,1)}, bf16[256,2048]{1,0:T(8,128)(2,1)}, u32[]{:S(2)}, u32[]{:S(2)}) collective-permute-start(bf16[256,2048]{1,0:T(8,128)(2,1)} %copy-done.8), channel_id=1, source_target_pairs={{0,1},{1,0},{2,3},{3,2},{4,5},{5,4},{6,7},{7,6},{8,9},{9,8},{10,11... | collective-permute-start | bytes 3145736 | tf_op jit(solution)/shard_map/ppermute | solution.py:40
  100.1 24.6 %collective-permute-start.12 = (bf16[256,2048]{1,0:T(8,128)(2,1)S(1)}, bf16[256,2048]{1,0:T(8,128)(2,1)S(1)}, u32[]{:S(2)}, u32[]{:S(2)}) collective-permute-start(bf16[256,2048]{1,0:T(8,128)(2,1)S(1)} %copy.49.refs_0_.refs_7_), channel_id=1, source_target_pairs={{0,4},{4,0},{2,6},{6,2},{1,5},{5,1},{3,7},{7,3},{8,12},{12,8},{10,... | collective-permute-start | bytes 3145736 | tf_op jit(solution)/shard_map/ppermute | solution.py:28
  101.7 24.3 %collective-permute-start.11 = (bf16[256,2048]{1,0:T(8,128)(2,1)S(1)}, bf16[256,2048]{1,0:T(8,128)(2,1)S(1)}, u32[]{:S(2)}, u32[]{:S(2)}) collective-permute-start(bf16[256,2048]{1,0:T(8,128)(2,1)S(1)} %copy.49.refs_0_.refs_7_), channel_id=1, source_target_pairs={{0,2},{2,0},{4,6},{6,4},{1,3},{3,1},{5,7},{7,5},{8,10},{10,8},{12,... | collective-permute-start | bytes 3145736 | tf_op jit(solution)/shard_map/ppermute | solution.py:24
  126.1 18.2 %collective-permute-start.20 = (bf16[128,2048]{1,0:T(8,128)(2,1)S(1)}, bf16[128,2048]{1,0:T(8,128)(2,1)}, u32[]{:S(2)}, u32[]{:S(2)}) collective-permute-start(bf16[128,2048]{1,0:T(8,128)(2,1)S(1)} %slice.304), channel_id=1, source_target_pairs={{0,2},{2,0},{4,6},{6,4},{1,3},{3,1},{5,7},{7,5},{8,10},{10,8},{12,... | collective-permute-start | bytes 1572872 | tf_op jit(solution)/shard_map/ppermute | solution.py:24
  127.1 17.2 %collective-permute-start.21 = (bf16[128,2048]{1,0:T(8,128)(2,1)S(1)}, bf16[128,2048]{1,0:T(8,128)(2,1)}, u32[]{:S(2)}, u32[]{:S(2)}) collective-permute-start(bf16[128,2048]{1,0:T(8,128)(2,1)S(1)} %slice.307), channel_id=1, source_target_pairs={{0,4},{4,0},{2,6},{6,2},{1,5},{5,1},{3,7},{7,3},{8,12},{12,8},{10,... | collective-permute-start | bytes 1572872 | tf_op jit(solution)/shard_map/ppermute | solution.py:28
  164.7 294.0 %reduce-scatter.4.cloned.1.call-start = ((), (), s32[]{:S(2)}) async-start(), calls=%async_computation.4 | async-start | bytes 3604480 | tf_op jit(solution)/shard_map/reduce_scatter | solution.py:1125
  178.7 25.5 %collective-permute-start.32 = (bf16[256,2048]{1,0:T(8,128)(2,1)}, bf16[256,2048]{1,0:T(8,128)(2,1)S(1)}, u32[]{:S(2)}, u32[]{:S(2)}) collective-permute-start(bf16[256,2048]{1,0:T(8,128)(2,1)} %get-tuple-element.114.refs_0_), channel_id=1, source_target_pairs={{0,4},{4,0},{2,6},{6,2},{1,5},{5,1},{3,7},{7,3},{8,12},{12,8},{10,... | collective-permute-start | bytes 3145736 | tf_op jit(solution)/shard_map/ppermute | solution.py:28
  179.9 25.9 %collective-permute-start.31 = (bf16[256,2048]{1,0:T(8,128)(2,1)}, bf16[256,2048]{1,0:T(8,128)(2,1)S(1)}, u32[]{:S(2)}, u32[]{:S(2)}) collective-permute-start(bf16[256,2048]{1,0:T(8,128)(2,1)} %get-tuple-element.114.refs_0_), channel_id=1, source_target_pairs={{0,2},{2,0},{4,6},{6,4},{1,3},{3,1},{5,7},{7,5},{8,10},{10,8},{12,... | collective-permute-start | bytes 3145736 | tf_op jit(solution)/shard_map/ppermute | solution.py:24
  180.7 39.7 %collective-permute-start.35 = (bf16[256,2048]{1,0:T(8,128)(2,1)}, bf16[256,2048]{1,0:T(8,128)(2,1)S(1)}, u32[]{:S(2)}, u32[]{:S(2)}) collective-permute-start(bf16[256,2048]{1,0:T(8,128)(2,1)} %get-tuple-element.114.refs_0_), channel_id=1, source_target_pairs={{0,1},{1,0},{2,3},{3,2},{4,5},{5,4},{6,7},{7,6},{8,9},{9,8},{10,11... | collective-permute-start | bytes 3145736 | tf_op jit(solution)/shard_map/ppermute | solution.py:40
  205.8 14.6 %collective-permute-start.37 = (bf16[256,2048]{1,0:T(8,128)(2,1)S(1)}, bf16[256,2048]{1,0:T(8,128)(2,1)}, u32[]{:S(2)}, u32[]{:S(2)}) collective-permute-start(bf16[256,2048]{1,0:T(8,128)(2,1)S(1)} %collective-permute-done.32.refs_2_), channel_id=1, source_target_pairs={{0,1},{1,0},{2,3},{3,2},{4,5},{5,4},{6,7},{7,6},{8,9},{9,8},{10,11... | collective-permute-start | bytes 3145736 | tf_op jit(solution)/shard_map/ppermute | solution.py:40
  205.9 14.5 %collective-permute-start.36 = (bf16[256,2048]{1,0:T(8,128)(2,1)S(1)}, bf16[256,2048]{1,0:T(8,128)(2,1)}, u32[]{:S(2)}, u32[]{:S(2)}) collective-permute-start(bf16[256,2048]{1,0:T(8,128)(2,1)S(1)} %collective-permute-done.31.refs_1_), channel_id=1, source_target_pairs={{0,1},{1,0},{2,3},{3,2},{4,5},{5,4},{6,7},{7,6},{8,9},{9,8},{10,11... | collective-permute-start | bytes 3145736 | tf_op jit(solution)/shard_map/ppermute | solution.py:40
  281.6 189.0 %reduce-scatter.6.cloned.1.call-start = ((), (), s32[]{:S(2)}) async-start(), calls=%async_computation.5 | async-start | bytes 7208960 | tf_op jit(solution)/shard_map/reduce_scatter | solution.py:1130
  298.2 25.8 %collective-permute-start.41 = (bf16[256,2048]{1,0:T(8,128)(2,1)}, bf16[256,2048]{1,0:T(8,128)(2,1)S(1)}, u32[]{:S(2)}, u32[]{:S(2)}) collective-permute-start(bf16[256,2048]{1,0:T(8,128)(2,1)} %pad_maximum_fusion.1), channel_id=1, source_target_pairs={{0,2},{2,0},{4,6},{6,4},{1,3},{3,1},{5,7},{7,5},{8,10},{10,8},{12,... | collective-permute-start | bytes 3145736 | tf_op jit(solution)/shard_map/ppermute | solution.py:24
  299.7 25.3 %collective-permute-start.42 = (bf16[256,2048]{1,0:T(8,128)(2,1)S(1)}, bf16[256,2048]{1,0:T(8,128)(2,1)S(1)}, u32[]{:S(2)}, u32[]{:S(2)}) collective-permute-start(bf16[256,2048]{1,0:T(8,128)(2,1)S(1)} %pad_maximum_fusion.2), channel_id=1, source_target_pairs={{0,4},{4,0},{2,6},{6,2},{1,5},{5,1},{3,7},{7,3},{8,12},{12,8},{10,... | collective-permute-start | bytes 3145736 | tf_op jit(solution)/shard_map/ppermute | solution.py:28
  319.6 221.6 %reduce-scatter.8.cloned.1.call-start = ((), (), s32[]{:S(2)}) async-start(), calls=%async_computation.6 | async-start | bytes 5242880 | tf_op jit(solution)/shard_map/reduce_scatter | solution.py:1153
  372.6 25.5 %collective-permute-start.50 = (bf16[256,2048]{1,0:T(8,128)(2,1)S(1)}, bf16[256,2048]{1,0:T(8,128)(2,1)S(1)}, u32[]{:S(2)}, u32[]{:S(2)}) collective-permute-start(bf16[256,2048]{1,0:T(8,128)(2,1)S(1)} %copy-done.17), channel_id=1, source_target_pairs={{0,4},{4,0},{2,6},{6,2},{1,5},{5,1},{3,7},{7,3},{8,12},{12,8},{10,... | collective-permute-start | bytes 3145736 | tf_op jit(solution)/shard_map/ppermute | solution.py:28
  374.0 24.1 %collective-permute-start.49 = (bf16[256,2048]{1,0:T(8,128)(2,1)S(1)}, bf16[256,2048]{1,0:T(8,128)(2,1)S(1)}, u32[]{:S(2)}, u32[]{:S(2)}) collective-permute-start(bf16[256,2048]{1,0:T(8,128)(2,1)S(1)} %copy-done.17), channel_id=1, source_target_pairs={{0,2},{2,0},{4,6},{6,4},{1,3},{3,1},{5,7},{7,5},{8,10},{10,8},{12,... | collective-permute-start | bytes 3145736 | tf_op jit(solution)/shard_map/ppermute | solution.py:24
  407.4 15.5 %collective-permute-start.51 = (bf16[1024,2048]{1,0:T(8,128)(2,1)}, bf16[1024,2048]{1,0:T(8,128)(2,1)S(1)}, u32[]{:S(2)}, u32[]{:S(2)}) collective-permute-start(bf16[1024,2048]{1,0:T(8,128)(2,1)} %d_one_rows_sibling.1), channel_id=1, source_target_pairs={{0,1},{1,0},{2,3},{3,2},{4,5},{5,4},{6,7},{7,6},{8,9},{9,8},{10,11... | collective-permute-start | bytes 12582920 | tf_op jit(solution)/shard_map/ppermute | solution.py:40
  408.3 14.5 %collective-permute-start.54 = (bf16[128,2048]{1,0:T(8,128)(2,1)}, bf16[128,2048]{1,0:T(8,128)(2,1)S(1)}, u32[]{:S(2)}, u32[]{:S(2)}) collective-permute-start(bf16[128,2048]{1,0:T(8,128)(2,1)} %slice.340), channel_id=1, source_target_pairs={{0,2},{2,0},{4,6},{6,4},{1,3},{3,1},{5,7},{7,5},{8,10},{10,8},{12,... | collective-permute-start | bytes 1572872 | tf_op jit(solution)/shard_map/ppermute | solution.py:24
  409.4 19.5 %collective-permute-start.56 = (bf16[256,2048]{1,0:T(8,128)(2,1)}, bf16[256,2048]{1,0:T(8,128)(2,1)}, u32[]{:S(2)}, u32[]{:S(2)}) collective-permute-start(bf16[256,2048]{1,0:T(8,128)(2,1)} %get-tuple-element.139.refs_10_), channel_id=1, source_target_pairs={{0,1},{1,0},{2,3},{3,2},{4,5},{5,4},{6,7},{7,6},{8,9},{9,8},{10,11... | collective-permute-start | bytes 3145736 | tf_op jit(solution)/shard_map/ppermute | solution.py:40
  411.5 18.6 %collective-permute-start.55 = (bf16[128,2048]{1,0:T(8,128)(2,1)}, bf16[128,2048]{1,0:T(8,128)(2,1)}, u32[]{:S(2)}, u32[]{:S(2)}) collective-permute-start(bf16[128,2048]{1,0:T(8,128)(2,1)} %slice.341), channel_id=1, source_target_pairs={{0,4},{4,0},{2,6},{6,2},{1,5},{5,1},{3,7},{7,3},{8,12},{12,8},{10,... | collective-permute-start | bytes 1572872 | tf_op jit(solution)/shard_map/ppermute | solution.py:28
  412.1 18.6 %collective-permute-start.58 = (bf16[256,2048]{1,0:T(8,128)(2,1)S(1)}, bf16[256,2048]{1,0:T(8,128)(2,1)}, u32[]{:S(2)}, u32[]{:S(2)}) collective-permute-start(bf16[256,2048]{1,0:T(8,128)(2,1)S(1)} %collective-permute-done.50.refs_12_), channel_id=1, source_target_pairs={{0,1},{1,0},{2,3},{3,2},{4,5},{5,4},{6,7},{7,6},{8,9},{9,8},{10,11... | collective-permute-start | bytes 3145736 | tf_op jit(solution)/shard_map/ppermute | solution.py:40
  429.0 25.6 %collective-permute-start.52 = (bf16[256,2048]{1,0:T(8,128)(2,1)}, bf16[256,2048]{1,0:T(8,128)(2,1)S(1)}, u32[]{:S(2)}, u32[]{:S(2)}) collective-permute-start(bf16[256,2048]{1,0:T(8,128)(2,1)} %pad_maximum_fusion.3), channel_id=1, source_target_pairs={{0,2},{2,0},{4,6},{6,4},{1,3},{3,1},{5,7},{7,5},{8,10},{10,8},{12,... | collective-permute-start | bytes 3145736 | tf_op jit(solution)/shard_map/ppermute | solution.py:24
  430.1 25.5 %collective-permute-start.53 = (bf16[256,2048]{1,0:T(8,128)(2,1)}, bf16[256,2048]{1,0:T(8,128)(2,1)}, u32[]{:S(2)}, u32[]{:S(2)}) collective-permute-start(bf16[256,2048]{1,0:T(8,128)(2,1)} %pad_maximum_fusion.4), channel_id=1, source_target_pairs={{0,4},{4,0},{2,6},{6,2},{1,5},{5,1},{3,7},{7,3},{8,12},{12,8},{10,... | collective-permute-start | bytes 3145736 | tf_op jit(solution)/shard_map/ppermute | solution.py:28
  458.6 31.5 %collective-permute-start.61 = (bf16[1024,2048]{1,0:T(8,128)(2,1)}, bf16[1024,2048]{1,0:T(8,128)(2,1)}, u32[]{:S(2)}, u32[]{:S(2)}) collective-permute-start(bf16[1024,2048]{1,0:T(8,128)(2,1)} %mlp_rows_sibling.1), channel_id=1, source_target_pairs={{0,1},{1,0},{2,3},{3,2},{4,5},{5,4},{6,7},{7,6},{8,9},{9,8},{10,11... | collective-permute-start | bytes 12582920 | tf_op jit(solution)/shard_map/ppermute | solution.py:40
  461.3 14.6 %collective-permute-start.62 = (bf16[128,2048]{1,0:T(8,128)(2,1)}, bf16[128,2048]{1,0:T(8,128)(2,1)S(1)}, u32[]{:S(2)}, u32[]{:S(2)}) collective-permute-start(bf16[128,2048]{1,0:T(8,128)(2,1)} %get-tuple-element.170), channel_id=1, source_target_pairs={{0,2},{2,0},{4,6},{6,4},{1,3},{3,1},{5,7},{7,5},{8,10},{10,8},{12,... | collective-permute-start | bytes 1572872 | tf_op jit(solution)/shard_map/ppermute | solution.py:24
  492.6 25.1 %collective-permute-start.64 = (bf16[256,2048]{1,0:T(8,128)(2,1)S(1)}, bf16[256,2048]{1,0:T(8,128)(2,1)}, u32[]{:S(2)}, u32[]{:S(2)}) collective-permute-start(bf16[256,2048]{1,0:T(8,128)(2,1)S(1)} %pad_maximum_fusion.5), channel_id=1, source_target_pairs={{0,2},{2,0},{4,6},{6,4},{1,3},{3,1},{5,7},{7,5},{8,10},{10,8},{12,... | collective-permute-start | bytes 3145736 | tf_op jit(solution)/shard_map/ppermute | solution.py:24
  493.9 24.8 %collective-permute-start.65 = (bf16[256,2048]{1,0:T(8,128)(2,1)S(1)}, bf16[256,2048]{1,0:T(8,128)(2,1)S(1)}, u32[]{:S(2)}, u32[]{:S(2)}) collective-permute-start(bf16[256,2048]{1,0:T(8,128)(2,1)S(1)} %pad_maximum_fusion.6), channel_id=1, source_target_pairs={{0,4},{4,0},{2,6},{6,2},{1,5},{5,1},{3,7},{7,3},{8,12},{12,8},{10,... | collective-permute-start | bytes 3145736 | tf_op jit(solution)/shard_map/ppermute | solution.py:28
  501.7 19.5 %collective-permute-start.74 = (f32[4,2048]{1,0:T(4,128)S(1)}, f32[4,2048]{1,0:T(4,128)S(1)}, u32[]{:S(2)}, u32[]{:S(2)}) collective-permute-start(f32[4,2048]{1,0:T(4,128)S(1)} %slice_add_fusion), channel_id=1, source_target_pairs={{0,6},{2,4},{4,2},{6,0},{1,7},{3,5},{5,3},{7,1},{8,14},{10,12},{12... | collective-permute-start | bytes 98312 | tf_op jit(solution)/shard_map/ppermute | solution.py:168
  503.7 17.5 %collective-permute-start.73 = (f32[4,2048]{1,0:T(4,128)S(1)}, f32[4,2048]{1,0:T(4,128)S(1)}, u32[]{:S(2)}, u32[]{:S(2)}) collective-permute-start(f32[4,2048]{1,0:T(4,128)S(1)} %slice_add_fusion), channel_id=1, source_target_pairs={{0,4},{2,6},{4,0},{6,2},{1,5},{3,7},{5,1},{7,3},{8,12},{10,14},{12... | collective-permute-start | bytes 98312 | tf_op jit(solution)/shard_map/ppermute | solution.py:168
  504.6 16.6 %collective-permute-start.72 = (f32[4,2048]{1,0:T(4,128)S(1)}, f32[4,2048]{1,0:T(4,128)S(1)}, u32[]{:S(2)}, u32[]{:S(2)}) collective-permute-start(f32[4,2048]{1,0:T(4,128)S(1)} %slice_add_fusion), channel_id=1, source_target_pairs={{0,2},{2,0},{4,6},{6,4},{1,3},{3,1},{5,7},{7,5},{8,10},{10,8},{12,... | collective-permute-start | bytes 98312 | tf_op jit(solution)/shard_map/ppermute | solution.py:168
  (82 other events, 909.5 us)
Sparse Core Ops, SparseCore 0:
  10.9 83.4 all-gather.7
  96.0 105.2 all-gather.5
  202.9 57.4 all-gather.9
  281.7 55.0 reduce-scatter.3
  339.0 102.0 reduce-scatter.5
  458.7 82.3 reduce-scatter.7
where the time goes:
time: 561 us; the launch traced here: 552 us
  Pallas kernels  216 us (39%)
  waiting for transfers between devices  196 us (35%)
  starting transfers between devices  58.4 us (10%)
  other arithmetic  42.2 us (8%)
  local copies, waits for them, and re-layouts  24 us (4%)
  between operations  15.5 us (3%)
    ppermute x18, waiting for transfers between devices, to_y(): return lax.ppermute(values, 'gy', SWAP_Y)  98.7 us
    ppermute x18, waiting for transfers between devices, to_x(): return lax.ppermute(values, 'gy', SWAP_X)  61.4 us
    pallas_call x2, Pallas kernels, unit_grads(): pl.pallas_call(body, grid=(parts,), in_specs=[pl.BlockSpec((height, lengt...  29.9 us
    pallas_call x3, Pallas kernels, unit_rows(): pl.pallas_call(body, in_specs=[ANY, ANY], out_specs=ANY, out_shape=jax.Sh...  27.1 us
    pallas_call x1, Pallas kernels, attend_back(): pl.pallas_call(body, out_shape=[jax.ShapeDtypeStruct((3 * width, length),...  23.1 us
    pallas_call x1, Pallas kernels, feed(): pl.pallas_call(body, in_specs=[ANY] * (count + 1), out_specs=[ANY, ANY],...  21.3 us
    pallas_call x1, Pallas kernels, feed_back(): pl.pallas_call(body, in_specs=[ANY] * (count + 3), out_specs=[ANY, ANY],...  21.1 us
    ppermute x18, starting transfers between devices, to_y(): return lax.ppermute(values, 'gy', SWAP_Y)  20.5 us
  transfers between devices with their start and end apart: 81, of which 40 were waited for; matrix products, arithmetic and copies ran while one was open for 10% of the time, Pallas kernels for 35%

commit v1 on v0

--- a/solution.py
+++ b/solution.py
@@ -97,27 +97,18 @@
     ]
 
 
-def exchange_first(own, sibling):
-    came = to_core(sibling)
-    sent = tuple(jnp.stack([own[step], came[step]]) for step in range(1, 4))
-    return own[0], came[0], lax.optimization_barrier(sent)
-
-
-def exchange_second(own, came, sent):
-    return [own, came, to_x(sent[0]), to_y(sent[1]), to_far(sent[2])]
+def exchange_plane(blocks):
+    got = [blocks[0], to_x(blocks[1]), to_y(blocks[2]), to_far(blocks[3])]
+    return got, to_core(jnp.stack([block[1] for block in got]))
 
 
 def exchanged_copies(refs, hold_of, sems):
-    copies = [
-        pltpu.make_async_copy(refs[0], hold_of(0), sems.at[0]),
-        pltpu.make_async_copy(refs[1], hold_of(4), sems.at[4]),
-    ]
-    for step in range(1, 4):
-        for core in range(2):
-            chunk = step + 4 * core
-            copies.append(
-                pltpu.make_async_copy(refs[step + 1].at[core], hold_of(chunk), sems.at[chunk])
-            )
+    copies = []
+    for step in range(4):
+        copies.append(pltpu.make_async_copy(refs[step].at[0], hold_of(step), sems.at[step]))
+        copies.append(
+            pltpu.make_async_copy(refs[4].at[step], hold_of(step + 4), sems.at[step + 4])
+        )
     return copies
 
 
@@ -201,7 +192,7 @@
 def middle_norm(tokens, blocks, weight_pieces, gain, shift):
     rows, depth = tokens.shape
     layout, arrays = split_pieces(weight_pieces)
-    width = blocks[0].shape[0]
+    width = blocks[0].shape[1]
     count = len(arrays)
 
     def body(t_ref, g_ref, b_ref, *refs):
@@ -272,24 +263,19 @@
             copy.wait()
         for chunk in range(8):
             block = dot_nt(hold[chunk * width : (chunk + 1) * width, :], low_ref[...]).astype(BF16)
-            if chunk < 4:
-                out_refs[chunk][...] = block
-            else:
-                out_refs[4][chunk - 4] = block
+            out_refs[chunk % 4][chunk // 4] = block
 
     whole = pl.BlockSpec((rows, depth), lambda i: (0, 0))
     line = pl.BlockSpec((1, depth), lambda i: (0, 0))
     two = pl.BlockSpec((2, depth), lambda i: (0, 0))
     half = pl.BlockSpec((rows // 2, depth), lambda i: (0, 0))
     second = pl.BlockSpec((rows // 2, depth), lambda i: (1, 0))
-    block = pl.BlockSpec((width, rows), lambda i: (0, 0))
+    block = pl.BlockSpec((2, width, rows), lambda i: (0, 0, 0))
     outs = pl.pallas_call(
         body,
         grid=(1,),
         in_specs=[whole, whole, whole, whole, second, half, half, second, line] + [ANY] * count,
-        out_specs=[whole, two, whole]
-        + [block] * 4
-        + [pl.BlockSpec((4, width, rows), lambda i: (0, 0, 0))],
+        out_specs=[whole, two, whole] + [block] * 4,
         scratch_shapes=[
             pltpu.VMEM((8 * width, depth), BF16),
             pltpu.SemaphoreType.DMA((count,)),
@@ -299,13 +285,12 @@
             jax.ShapeDtypeStruct((2, depth), F32),
             jax.ShapeDtypeStruct((rows, depth), F32),
         ]
-        + [jax.ShapeDtypeStruct((width, rows), BF16)] * 4
-        + [jax.ShapeDtypeStruct((4, width, rows), BF16)],
+        + [jax.ShapeDtypeStruct((2, width, rows), BF16)] * 4,
         compiler_params=params(),
         cost_estimate=cost(0, 0),
         name="norm_two_back",
     )(middle, cotangent, *parts, gain, *arrays)
-    return outs[0], outs[1], outs[2], outs[3:7], outs[7]
+    return outs[0], outs[1], outs[2], outs[3:]
 
 
 def norm_one_back(tokens, d_middle, parts, gain):
@@ -331,7 +316,7 @@
         in_specs=[whole, whole, whole, whole, second, half, half, second, line],
         out_specs=[whole, two],
         compiler_params=params(),
-        cost_estimate=cost(0, 8 * MIB),
+        cost_estimate=cost(0, 0),
         name="norm_one_back",
     )(tokens, d_middle, *parts, gain)
 
@@ -369,24 +354,6 @@
             )
         )
     return copies
-
-
-def copy_columns(step, parts, cols, layout, piece_refs, rows, hold, sems, pos_ref=None):
-    def copies(part):
-        return column_copies(part, cols, layout, piece_refs, rows, hold, sems, pos_ref)
-
-    @pl.when(step == 0)
-    def _():
-        for part in range(parts):
-            for copy in copies(part):
-                copy.start()
-
-    for part in range(parts):
-
-        @pl.when(step == part)
-        def _(part=part):
-            for copy in copies(part):
-                copy.wait()
 
 
 def weight_copies(w_ref, height, w_hold, w_sems):
@@ -542,128 +509,139 @@
     )(weight, *arrays)
 
 
-def feed_back(pieces, w_down, slopes, w_gate_up):
-    pieces = [pieces[number] for number in (5, 6, 7, 8, 9, 0, 1, 2, 3, 4)]
+def feed_back(pieces, w_down, slopes, w_gate_up, core_step, d_gate_up=None):
+    pieces = [
+        (piece, chunk - 4 * core_step, first)
+        for piece, chunk, first in pieces
+        if chunk // 4 == core_step
+    ]
     layout, arrays = split_pieces(pieces)
     rows, depth = arrays[0].shape
     parts, pair_units, cols = w_gate_up.shape
     units = pair_units // 2
     count = len(arrays)
     half = 4 * rows
+    given = [] if d_gate_up is None else [d_gate_up]
 
     def body(wd_ref, s_ref, wg_ref, *refs):
         piece_refs = refs[:count]
-        dgu_ref, o_ref, hold, w_hold, slope, wg_hold, made = refs[count : count + 7]
-        sems, w_sems, s_sems, wg_sems, d_sems, o_sems = refs[count + 7 :]
-        w_copies = weight_copies(wd_ref, units, w_hold, w_sems)
-        for copy in w_copies:
+        refs = refs[count + len(given) :]
+        dgu_ref, o_ref, hold, wd_hold, slope, w_hold, made = refs[:7]
+        sems, wd_sems, s_sem, w_sems, d_sem, o_sems = refs[7:]
+        there = pl.ds(core_step * half, half)
+        wd_copies = weight_copies(wd_ref, units, wd_hold, wd_sems)
+        for copy in wd_copies:
             copy.start()
         copies = start_pieces(layout, piece_refs, rows, hold, sems)
-        s_copies = []
-        for core_step in (1, 0):
-            there = pl.ds(core_step * half, half)
-            copy = pltpu.make_async_copy(
-                s_ref.at[:, there], slope.at[:, there], s_sems.at[core_step]
-            )
-            copy.start()
-            s_copies.append(copy)
-        wg_copies = [
-            pltpu.make_async_copy(wg_ref.at[part], wg_hold.at[part], wg_sems.at[part])
-            for part in range(parts)
-        ]
-        for copy in wg_copies:
-            copy.start()
-        for copy in w_copies:
+        s_copy = pltpu.make_async_copy(s_ref.at[:, there], slope, s_sem)
+        s_copy.start()
+        for copy in wd_copies:
             copy.wait()
-        kept = []
-        for core_step in (1, 0):
-            wait_core(core_step, copies)
-            s_copies[1 - core_step].wait()
-            for chunk in range(4 * core_step, 4 * core_step + 4):
+        for _, copy in copies:
+            copy.wait()
+        kept = pltpu.make_async_copy(slope, dgu_ref.at[:, there], d_sem)
+
+        def left():
+            for chunk in range(4):
                 here = slice(chunk * rows, (chunk + 1) * rows)
-                d_hid = dot_nt(w_hold[...], hold[here, :])
+                d_hid = dot_nt(wd_hold[...], hold[here, :])
                 low = slope[:units, here].astype(F32)
                 high = slope[units:, here].astype(F32)
                 slope[:units, here] = (d_hid * low).astype(BF16)
                 slope[units:, here] = (d_hid * high).astype(BF16)
-            there = pl.ds(core_step * half, half)
-            copy = pltpu.make_async_copy(
-                slope.at[:, there], dgu_ref.at[:, there], d_sems.at[core_step]
-            )
-            copy.start()
-            kept.append(copy)
-        for copy in wg_copies:
-            copy.wait()
-        left = slope[:, half:].T
-        for group in range(2):
-            columns = pl.ds(group * depth // 2, depth // 2)
-            for part in range(group * parts // 2, (group + 1) * parts // 2):
-                made[:, part * cols : (part + 1) * cols] = dot_nn(left, wg_hold[part]).astype(BF16)
-            copy = pltpu.make_async_copy(
-                made.at[:, columns], o_ref.at[:, columns], o_sems.at[group]
-            )
-            copy.start()
-            kept.append(copy)
-        for copy in kept:
-            copy.wait()
+            kept.start()
+            return slope[...].T
+
+        rows_of(s_copy, left, wg_ref, pair_units, o_ref, w_hold, made, w_sems, o_sems)
+        kept.wait()
 
     return pl.pallas_call(
         body,
-        in_specs=[ANY] * (count + 3),
+        in_specs=[ANY] * (count + 3 + len(given)),
         out_specs=[ANY, ANY],
         out_shape=[
             jax.ShapeDtypeStruct((pair_units, 2 * half), BF16),
             jax.ShapeDtypeStruct((half, depth), BF16),
         ],
         scratch_shapes=[
-            pltpu.VMEM((2 * half, depth), BF16),
+            pltpu.VMEM((half, depth), BF16),
             pltpu.VMEM((units, depth), BF16),
-            pltpu.VMEM((pair_units, 2 * half), BF16),
+            pltpu.VMEM((pair_units, half), BF16),
             pltpu.VMEM((parts, pair_units, cols), BF16),
             pltpu.VMEM((half, depth), BF16),
             pltpu.SemaphoreType.DMA((count,)),
             pltpu.SemaphoreType.DMA((parts,)),
+            pltpu.SemaphoreType.DMA,
+            pltpu.SemaphoreType.DMA((parts,)),
+            pltpu.SemaphoreType.DMA,
             pltpu.SemaphoreType.DMA((2,)),
-            pltpu.SemaphoreType.DMA((parts,)),
-            pltpu.SemaphoreType.DMA((2,)),
-            pltpu.SemaphoreType.DMA((2,)),
-        ],
+        ],
+        input_output_aliases={3 + count: 0} if given else {},
         compiler_params=params(),
-        cost_estimate=cost(0, 0),
-        name="feed_back",
-    )(w_down, slopes, w_gate_up, *arrays)
-
-
-def unit_grads(pieces, left, parts, name, scale=1):
+        cost_estimate=cost(2 * half * depth * units, 10 * MIB, 0.1),
+        name="feed_back_sibling" if core_step else "feed_back_own",
+    )(w_down, slopes, w_gate_up, *arrays, *given)
+
+
+def grads_of(left, pieces, parts, name, pos=None, kinds=0, scale=1):
     layout, arrays = split_pieces(pieces)
     rows, depth = arrays[0].shape
     height, length = left.shape
     cols = depth // parts
     count = len(arrays)
-
-    def body(l_ref, *refs):
+    shape = (kinds, cols, height // kinds) if kinds else (height, cols)
+
+    def body(pos_ref, l_ref, *refs):
         piece_refs = refs[:count]
-        out_ref, hold, sems = refs[count:]
-        step = pl.program_id(0)
-        copy_columns(step, parts, cols, layout, piece_refs, rows, hold, sems)
-        columns = pl.ds(pl.multiple_of(step * cols, cols), cols)
-        out_ref[0] = dot_nn(l_ref[...], hold[:, columns]).astype(BF16)
+        out_ref, l_hold, hold, made, l_sem, sems, o_sems = refs[count:]
+        l_copy = pltpu.make_async_copy(l_ref, l_hold, l_sem)
+        l_copy.start()
+        order = None if pos is None else pos_ref
+        groups = [
+            column_copies(group, depth // 2, layout, piece_refs, rows, hold, sems, order)
+            for group in range(2)
+        ]
+        for group in groups:
+            for copy in group:
+                copy.start()
+        l_copy.wait()
+        kept = []
+        for group in range(2):
+            for copy in groups[group]:
+                copy.wait()
+            members = range(group * parts // 2, (group + 1) * parts // 2)
+            for part in members:
+                grad = dot_nn(l_hold[...], hold[:, part * cols : (part + 1) * cols])
+                if kinds:
+                    for kind in range(kinds):
+                        band = grad[kind * shape[2] : (kind + 1) * shape[2]]
+                        made[part, kind] = band.T.astype(BF16)
+                else:
+                    made[part] = grad.astype(BF16)
+            there = pl.ds(members.start, len(members))
+            copy = pltpu.make_async_copy(made.at[there], out_ref.at[there], o_sems.at[group])
+            copy.start()
+            kept.append(copy)
+        for copy in kept:
+            copy.wait()
 
     return pl.pallas_call(
         body,
-        grid=(parts,),
-        in_specs=[pl.BlockSpec((height, length), lambda i: (0, 0), pipeline_mode=pl.Buffered(1))]
-        + [ANY] * count,
-        out_specs=pl.BlockSpec((1, height, cols), lambda i: (i, 0, 0)),
-        out_shape=jax.ShapeDtypeStruct((parts, height, cols), BF16),
+        in_specs=[SM] + [ANY] * (count + 1),
+        out_specs=ANY,
+        out_shape=jax.ShapeDtypeStruct((parts, *shape), BF16),
         scratch_shapes=[
+            pltpu.VMEM((height, length), BF16),
             pltpu.VMEM((length, depth), BF16),
-            pltpu.SemaphoreType.DMA((parts, count)),
+            pltpu.VMEM((parts, *shape), BF16),
+            pltpu.SemaphoreType.DMA,
+            pltpu.SemaphoreType.DMA((2, count)),
+            pltpu.SemaphoreType.DMA((2,)),
         ],
         compiler_params=params(),
         cost_estimate=cost(2 * height * length * depth, 20 * MIB, scale),
         name=name,
-    )(left, *arrays)
+    )(jnp.zeros((8,), jnp.int32) if pos is None else pos, left, *arrays)
 
 
 def rows_scratch(half, units, parts, cols):
@@ -752,53 +730,6 @@
     )(pos, d_projected, weight)
 
 
-def attention_grads(pos, token_pieces, branch_pieces, d_projected, attended, parts):
-    x_layout, x_arrays = split_pieces(token_pieces)
-    b_layout, b_arrays = split_pieces(branch_pieces)
-    rows, depth = x_arrays[0].shape
-    width, length = attended.shape
-    cols = depth // parts
-    x_count, b_count = len(x_arrays), len(b_arrays)
-
-    def body(pos_ref, dp_ref, a_ref, *refs):
-        x_refs = refs[:x_count]
-        b_refs = refs[x_count : x_count + b_count]
-        o_ref, x_hold, b_hold, x_sems, b_sems = refs[x_count + b_count :]
-        step = pl.program_id(0)
-        columns = pl.ds(pl.multiple_of(step * cols, cols), cols)
-        copy_columns(step, parts, cols, x_layout, x_refs, rows, x_hold, x_sems, pos_ref)
-        copy_columns(step, parts, cols, b_layout, b_refs, rows, b_hold, b_sems, pos_ref)
-        grad = dot_nn(dp_ref[...], x_hold[:, columns])
-        for kind in range(3):
-            o_ref[0, kind] = grad[kind * width : (kind + 1) * width].T.astype(BF16)
-        o_ref[0, 3] = dot_nn(a_ref[...], b_hold[:, columns]).T.astype(BF16)
-
-    whole = pl.Buffered(1)
-    return pl.pallas_call(
-        body,
-        grid_spec=pltpu.PrefetchScalarGridSpec(
-            num_scalar_prefetch=1,
-            grid=(parts,),
-            in_specs=[
-                pl.BlockSpec((3 * width, length), lambda i, p: (0, 0), pipeline_mode=whole),
-                pl.BlockSpec((width, length), lambda i, p: (0, 0), pipeline_mode=whole),
-            ]
-            + [ANY] * (x_count + b_count),
-            out_specs=pl.BlockSpec((1, 4, cols, width), lambda i, p: (i, 0, 0, 0)),
-            scratch_shapes=[
-                pltpu.VMEM((length, depth), BF16),
-                pltpu.VMEM((length, depth), BF16),
-                pltpu.SemaphoreType.DMA((parts, x_count)),
-                pltpu.SemaphoreType.DMA((parts, b_count)),
-            ],
-        ),
-        out_shape=jax.ShapeDtypeStruct((parts, 4, cols, width), BF16),
-        compiler_params=params(),
-        cost_estimate=cost(8 * width * length * depth, 24 * MIB, 0.1),
-        name="attention_grads",
-    )(pos, d_projected, attended, *x_arrays, *b_arrays)
-
-
 def chunk_lanes(pos_ref, chunk, rows):
     return pl.ds(pl.multiple_of(pos_ref[chunk] * rows, rows), rows)
 
@@ -817,7 +748,7 @@
     heads = width // HEAD_DIM
 
     def body(pos_ref, start_ref, qkv_ref, first_ref, out_ref, log_ref, *refs):
-        block_refs, held, acc = refs[:5], refs[5], refs[6]
+        block_refs, held, acc = refs[:4], refs[4], refs[5]
 
         def query_block(q_at, _):
             q_lanes = pl.ds(pl.multiple_of(q_at * size, size), size)
@@ -883,10 +814,7 @@
         lax.fori_loop(0, length // size, query_block, 0)
         for chunk in range(8):
             block = out_ref[:, chunk_lanes(pos_ref, chunk, rows)]
-            if chunk < 4:
-                block_refs[chunk][...] = block
-            else:
-                block_refs[4][chunk - 4] = block
+            block_refs[chunk % 4][chunk // 4] = block
 
     outs = pl.pallas_call(
         body,
@@ -894,10 +822,9 @@
             jax.ShapeDtypeStruct((width, length), BF16),
             jax.ShapeDtypeStruct((heads, length), F32),
         ]
-        + [jax.ShapeDtypeStruct((width, rows), BF16)] * 4
-        + [jax.ShapeDtypeStruct((4, width, rows), BF16)],
+        + [jax.ShapeDtypeStruct((2, width, rows), BF16)] * 4,
         in_specs=[SM, SM, VM, VM],
-        out_specs=[VM] * 7,
+        out_specs=[VM] * 6,
         scratch_shapes=[
             pltpu.VMEM((heads, length, size), F32),
             pltpu.VMEM((width, size), F32),
@@ -906,7 +833,7 @@
         cost_estimate=cost(0, 0),
         name="attend",
     )(pos, start_block, qkv, doc_first)
-    return outs[0], outs[1], outs[2:6], outs[6]
+    return outs[0], outs[1], outs[2:]
 
 
 def attend_back(
@@ -1106,12 +1033,13 @@
         sine,
     )
     qkv = after(qkv, out_first[1], out_first[2], *[piece for piece, _, _ in cot_pieces])
-    attended, log_sums, *blocks = attend(pos, qkv, doc_first, start_block, size)
+    attended, log_sums, blocks = attend(pos, qkv, doc_first, start_block, size)
     exchanged = []
 
     def exchange(*arrived):
-        exchanged.extend(exchange_second(*exchange_first(*after(tuple(blocks), *arrived))))
-        return exchanged[2:]
+        got, other = exchange_plane(after(tuple(blocks), *arrived))
+        exchanged.extend([*got, other])
+        return exchanged[1:]
 
     out_pieces = gather_second(out_first, (qkv,), exchange)
     blocks = exchanged
@@ -1121,48 +1049,66 @@
 
     two_pieces = gather_plane(normed_two)
     hidden, slopes = feed(two_pieces, w_gate_up)
-    down_grad = unit_grads(cot_pieces, hidden, parts, "down_grads")
+    down_grad = grads_of(hidden, cot_pieces, parts, "down_grads", scale=0.1)
     down_grad_sum = lax.psum_scatter(down_grad, "gx", scatter_dimension=0, tiled=False)
-    d_gate_up, d_two_sib = feed_back(cot_pieces, w_down, after(slopes, down_grad), w_gate_up)
-    d_two_own = unit_rows(after(d_gate_up, d_two_sib), w_gate_up, 0, "d_two_rows_own", 0.3)
+    d_gate_up, d_two_sib = feed_back(cot_pieces, w_down, after(slopes, down_grad), w_gate_up, 1)
+    d_gate_up, d_two_own = feed_back(
+        cot_pieces, w_down, after(slopes, d_two_sib), w_gate_up, 0, d_gate_up
+    )
     came, sent = scatter_first(d_two_own, d_two_sib, rows)
-    gate_up_grad = unit_grads(two_pieces, after(d_gate_up, *sent), parts, "gate_up_grads", 0.05)
-    gate_up_grad_sum = lax.psum_scatter(gate_up_grad, "gx", scatter_dimension=0, tiled=False)
-    sent, arrived = scatter_second(d_two_own, came, sent, rows, gate_up_grad, down_grad_sum)
+    gate_up_grad = grads_of(after(d_gate_up, *sent), two_pieces, parts, "gate_up_grads", scale=0.05)
+    sent, arrived = scatter_second(d_two_own, came, sent, rows, gate_up_grad)
+    gate_up_grad_sum = lax.psum_scatter(
+        after(gate_up_grad, *sent), "gx", scatter_dimension=0, tiled=False
+    )
     mlp_sib = unit_rows(
         after(hidden, gate_up_grad, *sent), w_down, 1, "mlp_rows_sibling", 0.1
     )
     d_two = scatter_last(d_two_own, came, sent, arrived)
 
-    d_branch, norm_two_sums, d_middle, own_blocks, other_blocks = norm_two_back(
+    d_branch, norm_two_sums, d_middle, blocks = norm_two_back(
         after(middle, mlp_sib), cot, d_two, gain_two, out_pieces
     )
-    blocks = exchange_second(*exchange_first(own_blocks, other_blocks))
+    got, other = exchange_plane(blocks)
+    blocks = [*got, other]
     d_projected, bias_sums = attend_back(
-        pos, blocks, qkv, attended, log_sums, cosine, sine, doc_first, start_block, size
-    )
-    branch_pieces = gather_plane(after(d_branch, *blocks[2:]), d_projected)
-    d_one_sib = qkv_rows(
-        pos, after(d_projected, branch_pieces[1][0], branch_pieces[2][0]), w_attn, 1, 0.1
-    )
-    d_one_own = qkv_rows(pos, after(d_projected, d_one_sib), w_attn, 0, 0.1)
+        pos,
+        blocks,
+        qkv,
+        after(attended, down_grad_sum),
+        log_sums,
+        cosine,
+        sine,
+        doc_first,
+        start_block,
+        size,
+    )
+    branch_pieces = gather_plane(after(d_branch, *blocks[1:]), d_projected)
+    far_pieces = (branch_pieces[3][0], branch_pieces[4][0])
+    qkv_grad = grads_of(
+        after(d_projected, branch_pieces[1][0], branch_pieces[2][0]),
+        one_pieces,
+        parts,
+        "qkv_grads",
+        pos,
+        kinds=3,
+        scale=0,
+    )
+    qkv_grad = after(qkv_grad, *far_pieces)
+    qkv_grad_sum = lax.psum_scatter(qkv_grad, "gx", scatter_dimension=0, tiled=False)
+    d_one_sib = qkv_rows(pos, after(d_projected, qkv_grad), w_attn, 1, 0)
+    d_one_own = qkv_rows(pos, after(d_projected, d_one_sib), w_attn, 0, 0)
     came, sent = scatter_first(d_one_own, d_one_sib, rows)
-    attn_grads = attention_grads(
-        pos, one_pieces, branch_pieces, d_projected, after(attended, *sent), parts
-    )
-    attn_grads_sum = lax.psum_scatter(attn_grads, "gx", scatter_dimension=0, tiled=False)
-    sent, arrived = scatter_second(d_one_own, came, sent, rows, attn_grads)
-    mlp_own = unit_rows(after(hidden, *sent), w_down, 0, "mlp_rows_own")
-    mlp_came, mlp_sent = scatter_first(mlp_own, after(mlp_sib, *sent), rows)
+    out_grad = grads_of(
+        after(attended, *sent), branch_pieces, parts, "out_grads", pos, kinds=1, scale=0
+    )
+    out_grad_sum = lax.psum_scatter(out_grad, "gx", scatter_dimension=0, tiled=False)
+    mlp_own = unit_rows(after(hidden, out_grad), w_down, 0, "mlp_rows_own", 0)
+    mlp_came, mlp_sent = scatter_first(mlp_own, after(mlp_sib, d_branch), rows)
+    sent, arrived = scatter_second(d_one_own, came, sent, rows, *mlp_sent)
     d_one = scatter_last(d_one_own, came, sent, arrived)
-    gate_up_out = gate_up_grad_sum.astype(F32).reshape(2, units, part_rows).transpose(2, 0, 1)
-    down_out = down_grad_sum.astype(F32).T
-    input_grad, norm_one_sums = norm_one_back(
-        after(x, gate_up_out, down_out), d_middle, d_one, gain_one
-    )
-
-    mlp_sent = after(mlp_sent, input_grad)
-    mlp_sent, mlp_arrived = scatter_second(mlp_own, mlp_came, mlp_sent, rows)
+    mlp_sent, mlp_arrived = scatter_second(mlp_own, mlp_came, after(mlp_sent, *sent), rows)
+
     mlp = scatter_last(mlp_own, mlp_came, mlp_sent, mlp_arrived)
     half = rows // 2
     total = mlp[0][:rows].astype(F32) + mlp[1][:rows].astype(F32)
@@ -1174,21 +1120,27 @@
         axis=0,
     )
     activations = (middle + total).astype(BF16)
+    input_grad, norm_one_sums = norm_one_back(x, d_middle, d_one, gain_one)
+    gate_up_grad_sum, down_grad_sum = after((gate_up_grad_sum, down_grad_sum), *mlp_sent)
+    gate_up_out = gate_up_grad_sum.astype(F32).reshape(2, units, part_rows).transpose(2, 0, 1)
+    down_out = down_grad_sum.astype(F32).T
 
     bias_row = jnp.pad(bias_sums.reshape(1, 3 * width), ((0, 0), (0, depth - 3 * width)))
     small = jnp.concatenate([norm_one_sums, norm_two_sums, bias_row], axis=0)
     small = sum_all(small, [("gx", axes["gx"])])
     bias_sum = small[4, : 3 * width].reshape(3, width)
     norm_sums = sum_all(small[:4], [("gz", axes["gz"]), ("gy", axes["gy"])])
-    attn_grads_sum = after(attn_grads_sum, activations, norm_sums, bias_sum).astype(F32)
+    qkv_grad_sum, out_grad_sum = after(
+        (qkv_grad_sum, out_grad_sum[0]), activations, norm_sums, bias_sum, gate_up_out, down_out
+    )
     return (
         activations[None],
         input_grad[None],
         norm_sums[0],
         norm_sums[1],
-        attn_grads_sum[:3].transpose(1, 0, 2),
+        qkv_grad_sum.astype(F32).transpose(1, 0, 2),
         bias_sum,
-        attn_grads_sum[3],
+        out_grad_sum.astype(F32),
         norm_sums[2],
         norm_sums[3],
         gate_up_out,

time: 561 us -> 558 us (level)
  waiting for transfers between devices: 196 us -> 180 us
  Pallas kernels: 216 us -> 225 us
    pallas_call x4 -> x6, Pallas kernels: 70 us -> 86.7 us  [the longest x4 54.8 us: grads_of(): pl.pallas_call(body, in_specs=[SM] + [ANY] * (count + 1), out_specs=ANY,...]
    pallas_call x3 -> x2, Pallas kernels: 27.1 us -> 15 us  [unit_rows(): pl.pallas_call(body, in_specs=[ANY, ANY], out_specs=ANY, out_shape=jax.Sh...]
    ppermute x18, waiting for transfers between devices: 98.7 us -> 92.8 us  [to_y(): return lax.ppermute(values, 'gy', SWAP_Y)]
  transfers between devices with their start and end apart: 81 -> 82, of which waited for: 40 -> 38; matrix products, arithmetic and copies ran while one was open for 10% -> 9% of each run, Pallas kernels for 35% -> 38%
where the time goes in v1:
time: 558 us; the launch traced here: 548 us
  Pallas kernels  225 us (40%)
  waiting for transfers between devices  180 us (32%)
  starting transfers between devices  62.2 us (11%)
  other arithmetic  40.9 us (7%)
  local copies, waits for them, and re-layouts  24.6 us (4%)
  between operations  15.3 us (3%)
    ppermute x18, waiting for transfers between devices, to_y(): return lax.ppermute(values, 'gy', SWAP_Y)  92.8 us
    ppermute x18, waiting for transfers between devices, to_x(): return lax.ppermute(values, 'gy', SWAP_X)  58.7 us
    pallas_call x4, Pallas kernels, grads_of(): pl.pallas_call(body, in_specs=[SM] + [ANY] * (count + 1), out_specs=ANY,...  54.8 us
    pallas_call x2, Pallas kernels, feed_back(): pl.pallas_call(body, in_specs=[ANY] * (count + 3 + len(given)), out_specs...  31.8 us
    pallas_call x1, Pallas kernels, attend_back(): pl.pallas_call(body, out_shape=[jax.ShapeDtypeStruct((3 * width, length),...  25.8 us
    ppermute x18, starting transfers between devices, to_y(): return lax.ppermute(values, 'gy', SWAP_Y)  24.7 us
    pallas_call x1, Pallas kernels, feed(): pl.pallas_call(body, in_specs=[ANY] * (count + 1), out_specs=[ANY, ANY],...  21.4 us
    ppermute x18, starting transfers between devices, to_x(): return lax.ppermute(values, 'gy', SWAP_X)  21 us
  transfers between devices with their start and end apart: 82, of which 38 were waited for; matrix products, arithmetic and copies ran while one was open for 9% of the time, Pallas kernels for 38%

profile of v1, /device:TPU:0, one launch (start us, length us, event | category | flops | bytes accessed | tf_op | source)
XLA Modules:
  0.0 548.5 jit_solution(9137188656273278462)
XLA Ops:
  12.8 3.0 norm_one.1.refs_0_
  16.3 2.5 collective-permute-start.1
  22.3 20.5 %collective-permute-done.1.refs_2_ = bf16[256,2048]{1,0:T(8,128)(2,1)S(1)} collective-permute-done((bf16[256,2048]{1,0:T(8,128)(2,1)}, bf16[256,2048]{1,0:T(8,128)(2,1)S(1)}, u32[]{:S(2)}, u32[]{:S(2)}) %collective-permute-start.1) | collective-permute-done | bytes 1048608 | tf_op jit(solution)/shard_map/ppermute | solution.py:28
  49.9 7.8 %collective-permute-done.13.refs_3_ = bf16[128,2048]{1,0:T(8,128)(2,1)S(1)} collective-permute-done((bf16[128,2048]{1,0:T(8,128)(2,1)S(1)}, bf16[128,2048]{1,0:T(8,128)(2,1)S(1)}, u32[]{:S(2)}, u32[]{:S(2)}) %collective-permute-start.13) | collective-permute-done | bytes 524320 | tf_op jit(solution)/shard_map/ppermute | solution.py:24
  57.7 23.8 %collective-permute-done.14.refs_4_ = bf16[128,2048]{1,0:T(8,128)(2,1)S(1)} collective-permute-done((bf16[128,2048]{1,0:T(8,128)(2,1)S(1)}, bf16[128,2048]{1,0:T(8,128)(2,1)S(1)}, u32[]{:S(2)}, u32[]{:S(2)}) %collective-permute-start.14) | collective-permute-done | bytes 524320 | tf_op jit(solution)/shard_map/ppermute | solution.py:28
  88.4 6.1 %all-gather.8.cloned.1.call-done = bf16[4096,512]{1,0:T(8,128)(2,1)} async-done(((bf16[1024,512]{1,0:T(8,128)(2,1)}), bf16[4096,512]{1,0:T(8,128)(2,1)}) %all-gather.8.cloned.1.call-update) | async-done | bytes 4194320 | tf_op jit(solution)/shard_map/all_gather | solution.py:1003
  94.4 2.3 slice_bitcast_fusion
  105.7 13.5 %project.1.qkv_ref = bf16[768,2048]{1,0:T(8,128)(2,1)} custom-call(s32[8]{0:T(128)} %fusion.4.pos_ref, bf16[4,1024,512]{2,1,0:T(8,128)(2,1)} %bitcast.57, f32[768,1]{1,0:T(8,128)} %copy.48.b_ref, f32[8,2048]{1,0:T(8,128)} %get-tuple-element.186.c_ref, f32[8,2048]{1,0:T(8,128)} %get-tuple-element.185.s_ref, bf16[256,2048]{1,0:T(8,128)(2,1)} %norm_one.1.refs_0_, ...), custom_call_target="tpu_custom_call" | custom-call | flops 6442450944 | bytes 15728640 | tf_op jit(solution)/shard_map/project/pallas_call | solution.py:428
  119.2 6.9 %collective-permute-done.12.refs_2_.refs_9_ = bf16[256,2048]{1,0:T(8,128)(2,1)S(1)} collective-permute-done((bf16[256,2048]{1,0:T(8,128)(2,1)S(1)}, bf16[256,2048]{1,0:T(8,128)(2,1)S(1)}, u32[]{:S(2)}, u32[]{:S(2)}) %collective-permute-start.12) | collective-permute-done | bytes 1048608 | tf_op jit(solution)/shard_map/ppermute | solution.py:28
  130.8 17.5 %attend.1 = (bf16[256,2048]{1,0:T(8,128)(2,1)}, f32[4,2048]{1,0:T(4,128)}, bf16[2,256,256]{2,1,0:T(8,128)(2,1)}, bf16[2,256,256]{2,1,0:T(8,128)(2,1)}, bf16[2,25...) custom-call(s32[8]{0:T(128)} %fusion.4.pos_ref, s32[8]{0:T(128)} %and_select_fusion.start_ref, ...), custom_call_target="tpu_custom_call" | custom-call | tf_op jit(solution)/shard_map/attend/pallas_call | solution.py:819
  152.9 5.1 collective-permute-done.23.refs_11_
  158.3 3.9 collective-permute-done.25.refs_13_
  167.1 2.6 collective-permute-done.29.refs_8_.refs_15_
  171.2 9.1 %middle_norm.1 = (f32[256,2048]{1,0:T(8,128)}, bf16[256,2048]{1,0:T(8,128)(2,1)}) custom-call(bf16[256,2048]{1,0:T(8,128)(2,1)} %bitcast.61, f32[1,2048]{1,0:T(1,128)} %bitcast.83, f32[1,2048]{1,0:T(1,128)} %bitcast.86, bf16[256,2048]{1,0:T(8,128)(2,1)} %copy-done.1, bf16[256,2048]{1,0:T(8,128)(2,1)} %collective-permute-done.11.refs_1_.refs_8_, ...), custom_call_target="tpu_custom_call" | custom-call | flops 2147483648 | bytes 14680064 | tf_op jit(solution)/shard_map/middle_norm/pallas_call | solution.py:215
  182.8 23.0 %collective-permute-done.32.refs_2_ = bf16[256,2048]{1,0:T(8,128)(2,1)S(1)} collective-permute-done((bf16[256,2048]{1,0:T(8,128)(2,1)}, bf16[256,2048]{1,0:T(8,128)(2,1)S(1)}, u32[]{:S(2)}, u32[]{:S(2)}) %collective-permute-start.32) | collective-permute-done | bytes 1048608 | tf_op jit(solution)/shard_map/ppermute | solution.py:28
  209.0 10.2 %collective-permute-done.33.refs_3_ = bf16[128,2048]{1,0:T(8,128)(2,1)} collective-permute-done((bf16[128,2048]{1,0:T(8,128)(2,1)S(1)}, bf16[128,2048]{1,0:T(8,128)(2,1)}, u32[]{:S(2)}, u32[]{:S(2)}) %collective-permute-start.33) | collective-permute-done | bytes 524320 | tf_op jit(solution)/shard_map/ppermute | solution.py:24
  219.2 2.7 collective-permute-done.34.refs_4_
  224.2 21.4 %feed.1 = (bf16[704,2048]{1,0:T(8,128)(2,1)}, bf16[1408,2048]{1,0:T(8,128)(2,1)}) custom-call(bf16[4,1408,512]{2,1,0:T(8,128)(2,1)} %all-gather.6.cloned.1.call-done.w_ref.wg_ref, bf16[256,2048]{1,0:T(8,128)(2,1)} %get-tuple-element.108.refs_0_, bf16[256,2048]{1,0:T(8,128)(2,1)} %copy-done.10, bf16[256,2048]{1,0:T(8,128)(2,1)} %copy-done.9, ...), custom_call_target="tpu_custom_call" | custom-call | flops 11811160064 | bytes 23068672 | tf_op jit(solution)/shard_map/feed/pallas_call | solution.py:488
  246.1 12.5 %down_grads.1 = bf16[4,704,512]{2,1,0:T(8,128)(2,1)} custom-call(s32[8]{0:T(128)} %jit_remainder_.5.pos_ref, bf16[704,2048]{1,0:T(8,128)(2,1)} %get-tuple-element.143.l_ref.h_ref, bf16[256,2048]{1,0:T(8,128)(2,1)} %bitcast.63, bf16[256,2048]{1,0:T(8,128)(2,1)} %copy-done.4, bf16[256,2048]{1,0:T(8,128)(2,1)} %copy-done.3, ...), custom_call_target="tpu_custom_call" | custom-call | flops 590558016 | bytes 2097152 | tf_op jit(solution)/shard_map/down_grads/pallas_call | solution.py:628
  260.4 15.9 %feed_back_sibling.1 = (bf16[1408,2048]{1,0:T(8,128)(2,1)}, bf16[1024,2048]{1,0:T(8,128)(2,1)}) custom-call(bf16[4,704,512]{2,1,0:T(8,128)(2,1)} %bitcast.52, bf16[1408,2048]{1,0:T(8,128)(2,1)} %get-tuple-element.116.s_ref, bf16[4,1408,512]{2,1,0:T(8,128)(2,1)} %all-gather.6.cloned.1.call-done.w_ref.wg_ref, ...), custom_call_target="tpu_custom_call" | custom-call | flops 295279008 | bytes 1048576 | tf_op jit(solution)/shard_map/feed_back_sibling/pallas_call | solution.py:558
  276.6 15.9 %feed_back_own.1 = (bf16[1408,2048]{1,0:T(8,128)(2,1)}, bf16[1024,2048]{1,0:T(8,128)(2,1)}) custom-call(bf16[4,704,512]{2,1,0:T(8,128)(2,1)} %bitcast.53, bf16[1408,2048]{1,0:T(8,128)(2,1)} %get-tuple-element.116.s_ref, bf16[4,1408,512]{2,1,0:T(8,128)(2,1)} %all-gather.6.cloned.1.call-done.w_ref.wg_ref, ...), custom_call_target="tpu_custom_call", output_to_operand_aliasing={{0}: (8, {})} | custom-call | flops 295279008 | bytes 1048576 | tf_op jit(solution)/shard_map/feed_back_own/pallas_call | solution.py:558
  292.6 3.0 add_convert_fusion.15
  299.7 20.1 %gate_up_grads.1 = bf16[4,1408,512]{2,1,0:T(8,128)(2,1)} custom-call(s32[8]{0:T(128)} %jit_remainder_.5.pos_ref, bf16[1408,2048]{1,0:T(8,128)(2,1)} %get-tuple-element.122.l_ref, bf16[256,2048]{1,0:T(8,128)(2,1)} %get-tuple-element.108.refs_0_, bf16[256,2048]{1,0:T(8,128)(2,1)} %copy-done.10, bf16[256,2048]{1,0:T(8,128)(2,1)} %copy-done.9, ...), custom_call_target="tpu_custom_call" | custom-call | flops 590558016 | bytes 1048576 | tf_op jit(solution)/shard_map/gate_up_grads/pallas_call | solution.py:628
  319.8 2.7 collective-permute-done.41.refs_2_
  323.5 2.4 add_convert_fusion.12
  328.4 7.5 %mlp_rows_sibling.1 = bf16[1024,2048]{1,0:T(8,128)(2,1)} custom-call(bf16[704,2048]{1,0:T(8,128)(2,1)} %get-tuple-element.143.l_ref.h_ref, bf16[4,704,512]{2,1,0:T(8,128)(2,1)} %bitcast.54), custom_call_target="tpu_custom_call" | custom-call | flops 295279008 | bytes 943718 | tf_op jit(solution)/shard_map/mlp_rows_sibling/pallas_call | solution.py:692
  335.9 3.4 collective-permute-done.43.refs_3_
  341.1 10.0 %norm_two_back.1 = (bf16[256,2048]{1,0:T(8,128)(2,1)}, f32[2,2048]{1,0:T(2,128)}, f32[256,2048]{1,0:T(8,128)}, bf16[2,256,256]{2,1,0:T(8,128)(2,1)}, bf16[2,256,...) custom-call(f32[256,2048]{1,0:T(8,128)} %get-tuple-element.126.v_ref, ...), custom_call_target="tpu_custom_call" | custom-call | tf_op jit(solution)/shard_map/norm_two_back/pallas_call | solution.py:274
  355.6 5.0 collective-permute-done.45.refs_1_
  360.7 5.1 collective-permute-done.46.refs_2_
  370.7 25.8 %attend_back.1 = (bf16[768,2048]{1,0:T(8,128)(2,1)}, f32[768,1]{1,0:T(8,128)}) custom-call(s32[8]{0:T(128)} %fusion.4.pos_ref, s32[8]{0:T(128)} %and_select_fusion.start_ref, bf16[768,2048]{1,0:T(8,128)(2,1)} %project.1.qkv_ref, bf16[256,2048]{1,0:T(8,128)(2,1)} %get-tuple-element.142.att_ref.l_ref, f32[4,2048]{1,0:T(4,128)} %get-tuple-element.112.log_ref, ...), custom_call_target="tpu_custom_call" | custom-call | tf_op jit(solution)/shard_map/attend_back/pallas_call | solution.py:933
  399.8 13.5 %qkv_grads.1 = bf16[4,3,512,256]{3,2,1,0:T(8,128)(2,1)} custom-call(s32[8]{0:T(128)} %fusion.4.pos_ref, bf16[768,2048]{1,0:T(8,128)(2,1)} %get-tuple-element.139.l_ref, bf16[256,2048]{1,0:T(8,128)(2,1)} %norm_one.1.refs_0_, bf16[256,2048]{1,0:T(8,128)(2,1)} %copy-done.8, bf16[256,2048]{1,0:T(8,128)(2,1)} %copy-done.7, bf16[128,2048]{1,0:T(8,128)(2,1)} %copy-done.35, ...), custom_call_target="tpu_custom_call" | custom-call | tf_op jit(solution)/shard_map/qkv_grads/pallas_call | solution.py:628
  413.4 8.2 %d_one_rows_sibling.1 = bf16[1024,2048]{1,0:T(8,128)(2,1)} custom-call(s32[8]{0:T(128)} %fusion.4.pos_ref, bf16[768,2048]{1,0:T(8,128)(2,1)} %get-tuple-element.139.l_ref, bf16[4,1024,512]{2,1,0:T(8,128)(2,1)} %bitcast.58), custom_call_target="tpu_custom_call" | custom-call | tf_op jit(solution)/shard_map/d_one_rows_sibling/pallas_call | solution.py:720
  423.1 8.2 %d_one_rows_own.1.refs_0_ = bf16[1024,2048]{1,0:T(8,128)(2,1)} custom-call(s32[8]{0:T(128)} %fusion.4.pos_ref, bf16[768,2048]{1,0:T(8,128)(2,1)} %get-tuple-element.139.l_ref, bf16[4,1024,512]{2,1,0:T(8,128)(2,1)} %bitcast.59), custom_call_target="tpu_custom_call" | custom-call | tf_op jit(solution)/shard_map/d_one_rows_own/pallas_call | solution.py:720
  432.4 2.9 add_convert_fusion.9
  441.2 8.7 %out_grads.1 = bf16[4,1,512,256]{3,2,1,0:T(8,128)(2,1)} custom-call(s32[8]{0:T(128)} %fusion.4.pos_ref, bf16[256,2048]{1,0:T(8,128)(2,1)} %get-tuple-element.142.att_ref.l_ref, bf16[256,2048]{1,0:T(8,128)(2,1)} %get-tuple-element.133.refs_0_, bf16[256,2048]{1,0:T(8,128)(2,1)} %collective-permute-done.49.refs_1_, bf16[256,2048]{1,0:T(8,128)(2,1)} %copy-done.13, ...), custom_call_target="tpu_custom_call" | custom-call | tf_op jit(solution)/shard_map/out_grads/pallas_call | solution.py:628
  449.9 7.5 %mlp_rows_own.1 = bf16[1024,2048]{1,0:T(8,128)(2,1)} custom-call(bf16[704,2048]{1,0:T(8,128)(2,1)} %get-tuple-element.143.l_ref.h_ref, bf16[4,704,512]{2,1,0:T(8,128)(2,1)} %bitcast.55), custom_call_target="tpu_custom_call" | custom-call | tf_op jit(solution)/shard_map/mlp_rows_own/pallas_call | solution.py:692
  457.4 2.9 add_convert_fusion.5
  463.7 3.4 add_convert_fusion.2
  469.7 10.6 %collective-permute-done.66.refs_3_ = bf16[128,2048]{1,0:T(8,128)(2,1)S(1)} collective-permute-done((bf16[128,2048]{1,0:T(8,128)(2,1)}, bf16[128,2048]{1,0:T(8,128)(2,1)S(1)}, u32[]{:S(2)}, u32[]{:S(2)}) %collective-permute-start.66) | collective-permute-done | bytes 524320 | tf_op jit(solution)/shard_map/ppermute | solution.py:24
  481.7 6.7 %norm_one_back.1 = (bf16[256,2048]{1,0:T(8,128)(2,1)}, f32[2,2048]{1,0:T(2,128)}) custom-call(bf16[256,2048]{1,0:T(8,128)(2,1)} %bitcast.62, f32[256,2048]{1,0:T(8,128)} %get-tuple-element.153.u_ref, bf16[1024,2048]{1,0:T(8,128)(2,1)} %d_one_rows_own.1.refs_0_, bf16[1024,2048]{1,0:T(8,128)(2,1)} %collective-permute-done.53.refs_1_, ...), custom_call_target="tpu_custom_call" | custom-call | tf_op jit(solution)/shard_map/norm_one_back/pallas_call | solution.py:309
  489.3 3.4 collective-permute-start.68
  495.1 3.6 collective-permute-done.69
  501.4 2.3 collective-permute-start.74
  505.0 10.8 %collective-permute-done.62 = bf16[256,2048]{1,0:T(8,128)(2,1)} collective-permute-done((bf16[256,2048]{1,0:T(8,128)(2,1)S(1)}, bf16[256,2048]{1,0:T(8,128)(2,1)}, u32[]{:S(2)}, u32[]{:S(2)}) %collective-permute-start.62) | collective-permute-done | bytes 1048608 | tf_op jit(solution)/shard_map/ppermute | solution.py:24
  522.1 6.3 %collective-permute-done.64 = bf16[128,2048]{1,0:T(8,128)(2,1)S(1)} collective-permute-done((bf16[128,2048]{1,0:T(8,128)(2,1)S(1)}, bf16[128,2048]{1,0:T(8,128)(2,1)S(1)}, u32[]{:S(2)}, u32[]{:S(2)}) %collective-permute-start.64) | collective-permute-done | bytes 524320 | tf_op jit(solution)/shard_map/ppermute | solution.py:28
  530.2 3.2 fusion.1
  539.0 2.4 convert_bitcast_fusion.1
  (324 shorter events, 117.2 us)
Async XLA Ops:
  7.2 87.3 %all-gather.8.cloned.1.call-start = ((), (), s32[]{:S(2)}) async-start(), calls=%async_computation.9 | async-start | bytes 5242880 | tf_op jit(solution)/shard_map/all_gather | solution.py:1003
  10.8 211.1 %all-gather.6.cloned.1.call-start = ((), (), s32[]{:S(2)}) async-start(), calls=%async_computation.4 | async-start | bytes 7208960 | tf_op jit(solution)/shard_map/all_gather | solution.py:1004
  11.6 248.8 %all-gather.10.cloned.1.call-start = ((), (), s32[]{:S(2)}) async-start(), calls=%async_computation.10 | async-start | bytes 3604480 | tf_op jit(solution)/shard_map/all_gather | solution.py:1007
  15.8 34.1 %collective-permute-start.15 = (bf16[256,2048]{1,0:T(8,128)(2,1)}, bf16[256,2048]{1,0:T(8,128)(2,1)}, u32[]{:S(2)}, u32[]{:S(2)}) collective-permute-start(bf16[256,2048]{1,0:T(8,128)(2,1)} %norm_one.1.refs_0_), channel_id=1, source_target_pairs={{0,1},{1,0},{2,3},{3,2},{4,5},{5,4},{6,7},{7,6},{8,9},{9,8},{10,11... | collective-permute-start | bytes 3145736 | tf_op jit(solution)/shard_map/ppermute | solution.py:40
  16.3 26.6 %collective-permute-start.1 = (bf16[256,2048]{1,0:T(8,128)(2,1)}, bf16[256,2048]{1,0:T(8,128)(2,1)S(1)}, u32[]{:S(2)}, u32[]{:S(2)}) collective-permute-start(bf16[256,2048]{1,0:T(8,128)(2,1)} %norm_one.1.refs_0_), channel_id=1, source_target_pairs={{0,4},{4,0},{2,6},{6,2},{1,5},{5,1},{3,7},{7,3},{8,12},{12,8},{10,... | collective-permute-start | bytes 3145736 | tf_op jit(solution)/shard_map/ppermute | solution.py:28
  18.8 25.9 %collective-permute-start = (bf16[256,2048]{1,0:T(8,128)(2,1)}, bf16[256,2048]{1,0:T(8,128)(2,1)S(1)}, u32[]{:S(2)}, u32[]{:S(2)}) collective-permute-start(bf16[256,2048]{1,0:T(8,128)(2,1)} %norm_one.1.refs_0_), channel_id=1, source_target_pairs={{0,2},{2,0},{4,6},{6,4},{1,3},{3,1},{5,7},{7,5},{8,10},{10,8},{12,... | collective-permute-start | bytes 3145736 | tf_op jit(solution)/shard_map/ppermute | solution.py:24
  42.9 14.8 %collective-permute-start.13 = (bf16[128,2048]{1,0:T(8,128)(2,1)S(1)}, bf16[128,2048]{1,0:T(8,128)(2,1)S(1)}, u32[]{:S(2)}, u32[]{:S(2)}) collective-permute-start(bf16[128,2048]{1,0:T(8,128)(2,1)S(1)} %slice.297), channel_id=1, source_target_pairs={{0,2},{2,0},{4,6},{6,4},{1,3},{3,1},{5,7},{7,5},{8,10},{10,8},{12,... | collective-permute-start | bytes 1572872 | tf_op jit(solution)/shard_map/ppermute | solution.py:24
  45.6 36.4 %collective-permute-start.3 = (bf16[256,2048]{1,0:T(8,128)(2,1)S(1)}, bf16[256,2048]{1,0:T(8,128)(2,1)S(1)}, u32[]{:S(2)}, u32[]{:S(2)}) collective-permute-start(bf16[256,2048]{1,0:T(8,128)(2,1)S(1)} %bitcast.66), channel_id=1, source_target_pairs={{0,4},{4,0},{2,6},{6,2},{1,5},{5,1},{3,7},{7,3},{8,12},{12,8},{10,... | collective-permute-start | bytes 3145736 | tf_op jit(solution)/shard_map/ppermute | solution.py:28
  47.2 34.9 %collective-permute-start.2 = (bf16[256,2048]{1,0:T(8,128)(2,1)S(1)}, bf16[256,2048]{1,0:T(8,128)(2,1)S(1)}, u32[]{:S(2)}, u32[]{:S(2)}) collective-permute-start(bf16[256,2048]{1,0:T(8,128)(2,1)S(1)} %bitcast.67), channel_id=1, source_target_pairs={{0,2},{2,0},{4,6},{6,4},{1,3},{3,1},{5,7},{7,5},{8,10},{10,8},{12,... | collective-permute-start | bytes 3145736 | tf_op jit(solution)/shard_map/ppermute | solution.py:24
  48.8 32.7 %collective-permute-start.14 = (bf16[128,2048]{1,0:T(8,128)(2,1)S(1)}, bf16[128,2048]{1,0:T(8,128)(2,1)S(1)}, u32[]{:S(2)}, u32[]{:S(2)}) collective-permute-start(bf16[128,2048]{1,0:T(8,128)(2,1)S(1)} %slice.298), channel_id=1, source_target_pairs={{0,4},{4,0},{2,6},{6,2},{1,5},{5,1},{3,7},{7,3},{8,12},{12,8},{10,... | collective-permute-start | bytes 1572872 | tf_op jit(solution)/shard_map/ppermute | solution.py:28
  49.9 34.6 %collective-permute-start.17 = (bf16[256,2048]{1,0:T(8,128)(2,1)}, bf16[256,2048]{1,0:T(8,128)(2,1)}, u32[]{:S(2)}, u32[]{:S(2)}) collective-permute-start(bf16[256,2048]{1,0:T(8,128)(2,1)} %copy-done.7), channel_id=1, source_target_pairs={{0,1},{1,0},{2,3},{3,2},{4,5},{5,4},{6,7},{7,6},{8,9},{9,8},{10,11... | collective-permute-start | bytes 3145736 | tf_op jit(solution)/shard_map/ppermute | solution.py:40
  57.7 23.8 %collective-permute-start.18 = (bf16[128,2048]{1,0:T(8,128)(2,1)S(1)}, bf16[128,2048]{1,0:T(8,128)(2,1)S(1)}, u32[]{:S(2)}, u32[]{:S(2)}) collective-permute-start(bf16[128,2048]{1,0:T(8,128)(2,1)S(1)} %collective-permute-done.13.refs_3_), channel_id=1, source_target_pairs={{0,1},{1,0},{2,3},{3,2},{4,5},{5,4},{6,7},{7,6},{8,9},{9,8},{10,11... | collective-permute-start | bytes 1572872 | tf_op jit(solution)/shard_map/ppermute | solution.py:40
  81.5 19.0 %collective-permute-start.6 = (bf16[256,2048]{1,0:T(8,128)(2,1)S(1)}, bf16[256,2048]{1,0:T(8,128)(2,1)}, u32[]{:S(2)}, u32[]{:S(2)}) collective-permute-start(bf16[256,2048]{1,0:T(8,128)(2,1)S(1)} %bitcast.68), channel_id=1, source_target_pairs={{0,1},{1,0},{2,3},{3,2},{4,5},{5,4},{6,7},{7,6},{8,9},{9,8},{10,11... | collective-permute-start | bytes 3145736 | tf_op jit(solution)/shard_map/ppermute | solution.py:40
  82.0 23.1 %collective-permute-start.16 = (bf16[256,2048]{1,0:T(8,128)(2,1)}, bf16[256,2048]{1,0:T(8,128)(2,1)}, u32[]{:S(2)}, u32[]{:S(2)}) collective-permute-start(bf16[256,2048]{1,0:T(8,128)(2,1)} %copy-done.8), channel_id=1, source_target_pairs={{0,1},{1,0},{2,3},{3,2},{4,5},{5,4},{6,7},{7,6},{8,9},{9,8},{10,11... | collective-permute-start | bytes 3145736 | tf_op jit(solution)/shard_map/ppermute | solution.py:40
  82.4 22.8 %collective-permute-start.8 = (bf16[256,2048]{1,0:T(8,128)(2,1)S(1)}, bf16[256,2048]{1,0:T(8,128)(2,1)}, u32[]{:S(2)}, u32[]{:S(2)}) collective-permute-start(bf16[256,2048]{1,0:T(8,128)(2,1)S(1)} %collective-permute-done.3.refs_2_), channel_id=1, source_target_pairs={{0,1},{1,0},{2,3},{3,2},{4,5},{5,4},{6,7},{7,6},{8,9},{9,8},{10,11... | collective-permute-start | bytes 3145736 | tf_op jit(solution)/shard_map/ppermute | solution.py:40
  84.5 16.1 %collective-permute-start.4 = (bf16[128,2048]{1,0:T(8,128)(2,1)}, bf16[128,2048]{1,0:T(8,128)(2,1)}, u32[]{:S(2)}, u32[]{:S(2)}) collective-permute-start(bf16[128,2048]{1,0:T(8,128)(2,1)} %slice.293), channel_id=1, source_target_pairs={{0,2},{2,0},{4,6},{6,4},{1,3},{3,1},{5,7},{7,5},{8,10},{10,8},{12,... | collective-permute-start | bytes 1572872 | tf_op jit(solution)/shard_map/ppermute | solution.py:24
  86.8 15.3 %collective-permute-start.5 = (bf16[128,2048]{1,0:T(8,128)(2,1)}, bf16[128,2048]{1,0:T(8,128)(2,1)}, u32[]{:S(2)}, u32[]{:S(2)}) collective-permute-start(bf16[128,2048]{1,0:T(8,128)(2,1)} %slice.294), channel_id=1, source_target_pairs={{0,4},{4,0},{2,6},{6,2},{1,5},{5,1},{3,7},{7,3},{8,12},{12,8},{10,... | collective-permute-start | bytes 1572872 | tf_op jit(solution)/shard_map/ppermute | solution.py:28
  100.5 18.7 %collective-permute-start.7 = (bf16[256,2048]{1,0:T(8,128)(2,1)}, bf16[256,2048]{1,0:T(8,128)(2,1)}, u32[]{:S(2)}, u32[]{:S(2)}) collective-permute-start(bf16[256,2048]{1,0:T(8,128)(2,1)} %copy-done.4), channel_id=1, source_target_pairs={{0,1},{1,0},{2,3},{3,2},{4,5},{5,4},{6,7},{7,6},{8,9},{9,8},{10,11... | collective-permute-start | bytes 3145736 | tf_op jit(solution)/shard_map/ppermute | solution.py:40
  100.6 25.6 %collective-permute-start.12 = (bf16[256,2048]{1,0:T(8,128)(2,1)S(1)}, bf16[256,2048]{1,0:T(8,128)(2,1)S(1)}, u32[]{:S(2)}, u32[]{:S(2)}) collective-permute-start(bf16[256,2048]{1,0:T(8,128)(2,1)S(1)} %copy.50.refs_0_.refs_7_), channel_id=1, source_target_pairs={{0,4},{4,0},{2,6},{6,2},{1,5},{5,1},{3,7},{7,3},{8,12},{12,8},{10,... | collective-permute-start | bytes 3145736 | tf_op jit(solution)/shard_map/ppermute | solution.py:28
  102.2 25.3 %collective-permute-start.11 = (bf16[256,2048]{1,0:T(8,128)(2,1)S(1)}, bf16[256,2048]{1,0:T(8,128)(2,1)}, u32[]{:S(2)}, u32[]{:S(2)}) collective-permute-start(bf16[256,2048]{1,0:T(8,128)(2,1)S(1)} %copy.50.refs_0_.refs_7_), channel_id=1, source_target_pairs={{0,2},{2,0},{4,6},{6,4},{1,3},{3,1},{5,7},{7,5},{8,10},{10,8},{12,... | collective-permute-start | bytes 3145736 | tf_op jit(solution)/shard_map/ppermute | solution.py:24
  128.6 19.7 %collective-permute-start.20 = (bf16[128,2048]{1,0:T(8,128)(2,1)S(1)}, bf16[128,2048]{1,0:T(8,128)(2,1)S(1)}, u32[]{:S(2)}, u32[]{:S(2)}) collective-permute-start(bf16[128,2048]{1,0:T(8,128)(2,1)S(1)} %slice.296), channel_id=1, source_target_pairs={{0,2},{2,0},{4,6},{6,4},{1,3},{3,1},{5,7},{7,5},{8,10},{10,8},{12,... | collective-permute-start | bytes 1572872 | tf_op jit(solution)/shard_map/ppermute | solution.py:24
  130.2 18.1 %collective-permute-start.21 = (bf16[128,2048]{1,0:T(8,128)(2,1)S(1)}, bf16[128,2048]{1,0:T(8,128)(2,1)S(1)}, u32[]{:S(2)}, u32[]{:S(2)}) collective-permute-start(bf16[128,2048]{1,0:T(8,128)(2,1)S(1)} %slice.299), channel_id=1, source_target_pairs={{0,4},{4,0},{2,6},{6,2},{1,5},{5,1},{3,7},{7,3},{8,12},{12,8},{10,... | collective-permute-start | bytes 1572872 | tf_op jit(solution)/shard_map/ppermute | solution.py:28
  165.0 205.7 %reduce-scatter.5.cloned.1.call-start = ((), (), s32[]{:S(2)}) async-start(), calls=%async_computation.5 | async-start | bytes 3604480 | tf_op jit(solution)/shard_map/reduce_scatter | solution.py:1053
  180.4 25.5 %collective-permute-start.32 = (bf16[256,2048]{1,0:T(8,128)(2,1)}, bf16[256,2048]{1,0:T(8,128)(2,1)S(1)}, u32[]{:S(2)}, u32[]{:S(2)}) collective-permute-start(bf16[256,2048]{1,0:T(8,128)(2,1)} %get-tuple-element.108.refs_0_), channel_id=1, source_target_pairs={{0,4},{4,0},{2,6},{6,2},{1,5},{5,1},{3,7},{7,3},{8,12},{12,8},{10,... | collective-permute-start | bytes 3145736 | tf_op jit(solution)/shard_map/ppermute | solution.py:28
  181.4 25.8 %collective-permute-start.31 = (bf16[256,2048]{1,0:T(8,128)(2,1)}, bf16[256,2048]{1,0:T(8,128)(2,1)S(1)}, u32[]{:S(2)}, u32[]{:S(2)}) collective-permute-start(bf16[256,2048]{1,0:T(8,128)(2,1)} %get-tuple-element.108.refs_0_), channel_id=1, source_target_pairs={{0,2},{2,0},{4,6},{6,4},{1,3},{3,1},{5,7},{7,5},{8,10},{10,8},{12,... | collective-permute-start | bytes 3145736 | tf_op jit(solution)/shard_map/ppermute | solution.py:24
  182.8 39.1 %collective-permute-start.35 = (bf16[256,2048]{1,0:T(8,128)(2,1)}, bf16[256,2048]{1,0:T(8,128)(2,1)S(1)}, u32[]{:S(2)}, u32[]{:S(2)}) collective-permute-start(bf16[256,2048]{1,0:T(8,128)(2,1)} %get-tuple-element.108.refs_0_), channel_id=1, source_target_pairs={{0,1},{1,0},{2,3},{3,2},{4,5},{5,4},{6,7},{7,6},{8,9},{9,8},{10,11... | collective-permute-start | bytes 3145736 | tf_op jit(solution)/shard_map/ppermute | solution.py:40
  207.3 14.6 %collective-permute-start.37 = (bf16[256,2048]{1,0:T(8,128)(2,1)S(1)}, bf16[256,2048]{1,0:T(8,128)(2,1)}, u32[]{:S(2)}, u32[]{:S(2)}) collective-permute-start(bf16[256,2048]{1,0:T(8,128)(2,1)S(1)} %collective-permute-done.32.refs_2_), channel_id=1, source_target_pairs={{0,1},{1,0},{2,3},{3,2},{4,5},{5,4},{6,7},{7,6},{8,9},{9,8},{10,11... | collective-permute-start | bytes 3145736 | tf_op jit(solution)/shard_map/ppermute | solution.py:40
  207.4 14.5 %collective-permute-start.36 = (bf16[256,2048]{1,0:T(8,128)(2,1)S(1)}, bf16[256,2048]{1,0:T(8,128)(2,1)}, u32[]{:S(2)}, u32[]{:S(2)}) collective-permute-start(bf16[256,2048]{1,0:T(8,128)(2,1)S(1)} %collective-permute-done.31.refs_1_), channel_id=1, source_target_pairs={{0,1},{1,0},{2,3},{3,2},{4,5},{5,4},{6,7},{7,6},{8,9},{9,8},{10,11... | collective-permute-start | bytes 3145736 | tf_op jit(solution)/shard_map/ppermute | solution.py:40
  276.3 16.3 %collective-permute-start.40 = (bf16[1024,2048]{1,0:T(8,128)(2,1)}, bf16[1024,2048]{1,0:T(8,128)(2,1)}, u32[]{:S(2)}, u32[]{:S(2)}) collective-permute-start(bf16[1024,2048]{1,0:T(8,128)(2,1)} %get-tuple-element.115), channel_id=1, source_target_pairs={{0,1},{1,0},{2,3},{3,2},{4,5},{5,4},{6,7},{7,6},{8,9},{9,8},{10,11... | collective-permute-start | bytes 12582920 | tf_op jit(solution)/shard_map/ppermute | solution.py:40
  276.4 257.0 %reduce-scatter.11.cloned.1.call-start = ((), (), s32[]{:S(2)}) async-start(), calls=%async_computation.8 | async-start | bytes 7208960 | tf_op jit(solution)/shard_map/reduce_scatter | solution.py:1061
  296.8 25.8 %collective-permute-start.41 = (bf16[256,2048]{1,0:T(8,128)(2,1)}, bf16[256,2048]{1,0:T(8,128)(2,1)S(1)}, u32[]{:S(2)}, u32[]{:S(2)}) collective-permute-start(bf16[256,2048]{1,0:T(8,128)(2,1)} %get-tuple-element.120), channel_id=1, source_target_pairs={{0,2},{2,0},{4,6},{6,4},{1,3},{3,1},{5,7},{7,5},{8,10},{10,8},{12,... | collective-permute-start | bytes 3145736 | tf_op jit(solution)/shard_map/ppermute | solution.py:24
  298.2 25.3 %collective-permute-start.42 = (bf16[256,2048]{1,0:T(8,128)(2,1)S(1)}, bf16[256,2048]{1,0:T(8,128)(2,1)S(1)}, u32[]{:S(2)}, u32[]{:S(2)}) collective-permute-start(bf16[256,2048]{1,0:T(8,128)(2,1)S(1)} %get-tuple-element.121), channel_id=1, source_target_pairs={{0,4},{4,0},{2,6},{6,2},{1,5},{5,1},{3,7},{7,3},{8,12},{12,8},{10,... | collective-permute-start | bytes 3145736 | tf_op jit(solution)/shard_map/ppermute | solution.py:28
  326.0 211.3 %reduce-scatter.7.cloned.1.call-start = ((), (), s32[]{:S(2)}) async-start(), calls=%async_computation.6 | async-start | bytes 3932160 | tf_op jit(solution)/shard_map/reduce_scatter | solution.py:1098
  368.7 27.9 %collective-permute-start.50 = (bf16[256,2048]{1,0:T(8,128)(2,1)S(1)}, bf16[256,2048]{1,0:T(8,128)(2,1)S(1)}, u32[]{:S(2)}, u32[]{:S(2)}) collective-permute-start(bf16[256,2048]{1,0:T(8,128)(2,1)S(1)} %copy-done.25), channel_id=1, source_target_pairs={{0,4},{4,0},{2,6},{6,2},{1,5},{5,1},{3,7},{7,3},{8,12},{12,8},{10,... | collective-permute-start | bytes 3145736 | tf_op jit(solution)/shard_map/ppermute | solution.py:28
  370.1 28.0 %collective-permute-start.49 = (bf16[256,2048]{1,0:T(8,128)(2,1)S(1)}, bf16[256,2048]{1,0:T(8,128)(2,1)}, u32[]{:S(2)}, u32[]{:S(2)}) collective-permute-start(bf16[256,2048]{1,0:T(8,128)(2,1)S(1)} %copy-done.25), channel_id=1, source_target_pairs={{0,2},{2,0},{4,6},{6,4},{1,3},{3,1},{5,7},{7,5},{8,10},{10,8},{12,... | collective-permute-start | bytes 3145736 | tf_op jit(solution)/shard_map/ppermute | solution.py:24
  396.6 16.8 %collective-permute-start.51 = (bf16[128,2048]{1,0:T(8,128)(2,1)S(1)}, bf16[128,2048]{1,0:T(8,128)(2,1)}, u32[]{:S(2)}, u32[]{:S(2)}) collective-permute-start(bf16[128,2048]{1,0:T(8,128)(2,1)S(1)} %slice.314), channel_id=1, source_target_pairs={{0,2},{2,0},{4,6},{6,4},{1,3},{3,1},{5,7},{7,5},{8,10},{10,8},{12,... | collective-permute-start | bytes 1572872 | tf_op jit(solution)/shard_map/ppermute | solution.py:24
  399.2 14.2 %collective-permute-start.52 = (bf16[128,2048]{1,0:T(8,128)(2,1)S(1)}, bf16[128,2048]{1,0:T(8,128)(2,1)}, u32[]{:S(2)}, u32[]{:S(2)}) collective-permute-start(bf16[128,2048]{1,0:T(8,128)(2,1)S(1)} %slice.315), channel_id=1, source_target_pairs={{0,4},{4,0},{2,6},{6,2},{1,5},{5,1},{3,7},{7,3},{8,12},{12,8},{10,... | collective-permute-start | bytes 1572872 | tf_op jit(solution)/shard_map/ppermute | solution.py:28
  421.7 35.7 %collective-permute-start.59 = (bf16[1024,2048]{1,0:T(8,128)(2,1)}, bf16[1024,2048]{1,0:T(8,128)(2,1)}, u32[]{:S(2)}, u32[]{:S(2)}) collective-permute-start(bf16[1024,2048]{1,0:T(8,128)(2,1)} %mlp_rows_sibling.1), channel_id=1, source_target_pairs={{0,1},{1,0},{2,3},{3,2},{4,5},{5,4},{6,7},{7,6},{8,9},{9,8},{10,11... | collective-permute-start | bytes 12582920 | tf_op jit(solution)/shard_map/ppermute | solution.py:40
  422.2 115.0 %reduce-scatter.9.cloned.1.call-start = ((), (), s32[]{:S(2)}) async-start(), calls=%async_computation.7 | async-start | bytes 1310720 | tf_op jit(solution)/shard_map/reduce_scatter | solution.py:1105
  422.6 16.0 %collective-permute-start.56 = (bf16[256,2048]{1,0:T(8,128)(2,1)S(1)}, bf16[256,2048]{1,0:T(8,128)(2,1)S(1)}, u32[]{:S(2)}, u32[]{:S(2)}) collective-permute-start(bf16[256,2048]{1,0:T(8,128)(2,1)S(1)} %collective-permute-done.50.refs_2_), channel_id=1, source_target_pairs={{0,1},{1,0},{2,3},{3,2},{4,5},{5,4},{6,7},{7,6},{8,9},{9,8},{10,11... | collective-permute-start | bytes 3145736 | tf_op jit(solution)/shard_map/ppermute | solution.py:40
  423.0 18.2 %collective-permute-start.55 = (bf16[256,2048]{1,0:T(8,128)(2,1)}, bf16[256,2048]{1,0:T(8,128)(2,1)}, u32[]{:S(2)}, u32[]{:S(2)}) collective-permute-start(bf16[256,2048]{1,0:T(8,128)(2,1)} %collective-permute-done.49.refs_1_), channel_id=1, source_target_pairs={{0,1},{1,0},{2,3},{3,2},{4,5},{5,4},{6,7},{7,6},{8,9},{9,8},{10,11... | collective-permute-start | bytes 3145736 | tf_op jit(solution)/shard_map/ppermute | solution.py:40
  437.4 25.4 %collective-permute-start.60 = (bf16[256,2048]{1,0:T(8,128)(2,1)}, bf16[256,2048]{1,0:T(8,128)(2,1)S(1)}, u32[]{:S(2)}, u32[]{:S(2)}) collective-permute-start(bf16[256,2048]{1,0:T(8,128)(2,1)} %pad_maximum_fusion.3), channel_id=1, source_target_pairs={{0,2},{2,0},{4,6},{6,4},{1,3},{3,1},{5,7},{7,5},{8,10},{10,8},{12,... | collective-permute-start | bytes 3145736 | tf_op jit(solution)/shard_map/ppermute | solution.py:24
  438.5 25.1 %collective-permute-start.61 = (bf16[256,2048]{1,0:T(8,128)(2,1)}, bf16[256,2048]{1,0:T(8,128)(2,1)S(1)}, u32[]{:S(2)}, u32[]{:S(2)}) collective-permute-start(bf16[256,2048]{1,0:T(8,128)(2,1)} %pad_maximum_fusion.4), channel_id=1, source_target_pairs={{0,4},{4,0},{2,6},{6,2},{1,5},{5,1},{3,7},{7,3},{8,12},{12,8},{10,... | collective-permute-start | bytes 3145736 | tf_op jit(solution)/shard_map/ppermute | solution.py:28
  492.7 23.1 %collective-permute-start.62 = (bf16[256,2048]{1,0:T(8,128)(2,1)S(1)}, bf16[256,2048]{1,0:T(8,128)(2,1)}, u32[]{:S(2)}, u32[]{:S(2)}) collective-permute-start(bf16[256,2048]{1,0:T(8,128)(2,1)S(1)} %copy-done.24), channel_id=1, source_target_pairs={{0,2},{2,0},{4,6},{6,4},{1,3},{3,1},{5,7},{7,5},{8,10},{10,8},{12,... | collective-permute-start | bytes 3145736 | tf_op jit(solution)/shard_map/ppermute | solution.py:24
  493.8 22.7 %collective-permute-start.63 = (bf16[256,2048]{1,0:T(8,128)(2,1)S(1)}, bf16[256,2048]{1,0:T(8,128)(2,1)S(1)}, u32[]{:S(2)}, u32[]{:S(2)}) collective-permute-start(bf16[256,2048]{1,0:T(8,128)(2,1)S(1)} %pad_maximum_fusion.6), channel_id=1, source_target_pairs={{0,4},{4,0},{2,6},{6,2},{1,5},{5,1},{3,7},{7,3},{8,12},{12,8},{10,... | collective-permute-start | bytes 3145736 | tf_op jit(solution)/shard_map/ppermute | solution.py:28
  501.4 19.3 %collective-permute-start.74 = (f32[4,2048]{1,0:T(4,128)S(1)}, f32[4,2048]{1,0:T(4,128)S(1)}, u32[]{:S(2)}, u32[]{:S(2)}) collective-permute-start(f32[4,2048]{1,0:T(4,128)S(1)} %slice_add_fusion), channel_id=1, source_target_pairs={{0,6},{2,4},{4,2},{6,0},{1,7},{3,5},{5,3},{7,1},{8,14},{10,12},{12... | collective-permute-start | bytes 98312 | tf_op jit(solution)/shard_map/ppermute | solution.py:159
  503.7 16.9 %collective-permute-start.73 = (f32[4,2048]{1,0:T(4,128)S(1)}, f32[4,2048]{1,0:T(4,128)S(1)}, u32[]{:S(2)}, u32[]{:S(2)}) collective-permute-start(f32[4,2048]{1,0:T(4,128)S(1)} %slice_add_fusion), channel_id=1, source_target_pairs={{0,4},{2,6},{4,0},{6,2},{1,5},{3,7},{5,1},{7,3},{8,12},{10,14},{12... | collective-permute-start | bytes 98312 | tf_op jit(solution)/shard_map/ppermute | solution.py:159
  504.3 16.4 %collective-permute-start.72 = (f32[4,2048]{1,0:T(4,128)S(1)}, f32[4,2048]{1,0:T(4,128)S(1)}, u32[]{:S(2)}, u32[]{:S(2)}) collective-permute-start(f32[4,2048]{1,0:T(4,128)S(1)} %slice_add_fusion), channel_id=1, source_target_pairs={{0,2},{2,0},{4,6},{6,4},{1,3},{3,1},{5,7},{7,5},{8,10},{10,8},{12,... | collective-permute-start | bytes 98312 | tf_op jit(solution)/shard_map/ppermute | solution.py:159
  (89 other events, 901.2 us)
Sparse Core Ops, SparseCore 0:
  10.9 83.4 all-gather.7
  96.0 105.2 all-gather.5
  202.9 57.4 all-gather.9
  276.5 54.9 reduce-scatter.4
  333.7 102.0 reduce-scatter.10
  438.0 64.9 reduce-scatter.6
  505.3 27.2 reduce-scatter.8

commit v2 on v1

--- a/solution.py
+++ b/solution.py
@@ -1120,10 +1120,12 @@
         axis=0,
     )
     activations = (middle + total).astype(BF16)
-    input_grad, norm_one_sums = norm_one_back(x, d_middle, d_one, gain_one)
-    gate_up_grad_sum, down_grad_sum = after((gate_up_grad_sum, down_grad_sum), *mlp_sent)
+    gate_up_grad_sum, down_grad_sum = after((gate_up_grad_sum, down_grad_sum), *sent)
     gate_up_out = gate_up_grad_sum.astype(F32).reshape(2, units, part_rows).transpose(2, 0, 1)
     down_out = down_grad_sum.astype(F32).T
+    input_grad, norm_one_sums = norm_one_back(
+        after(x, gate_up_out, down_out), d_middle, d_one, gain_one
+    )
 
     bias_row = jnp.pad(bias_sums.reshape(1, 3 * width), ((0, 0), (0, depth - 3 * width)))
     small = jnp.concatenate([norm_one_sums, norm_two_sums, bias_row], axis=0)

time: 558 us -> 563 us (level)
  waiting for transfers between devices: 180 us -> 193 us
    ppermute x18, waiting for transfers between devices: 92.8 us -> 99.4 us  [to_y(): return lax.ppermute(values, 'gy', SWAP_Y)]
  transfers between devices with their start and end apart: 82 -> 82, of which waited for: 38 -> 37; matrix products, arithmetic and copies ran while one was open for 9% -> 10% of each run, Pallas kernels for 38% -> 37%
where the time goes in v2:
time: 563 us; the launch traced here: 554 us
  Pallas kernels  220 us (39%)
  waiting for transfers between devices  193 us (34%)
  starting transfers between devices  60.8 us (11%)
  other arithmetic  42.5 us (8%)
  local copies, waits for them, and re-layouts  22.4 us (4%)
  between operations  15.3 us (3%)
    ppermute x18, waiting for transfers between devices, to_y(): return lax.ppermute(values, 'gy', SWAP_Y)  99.4 us
    ppermute x18, waiting for transfers between devices, to_x(): return lax.ppermute(values, 'gy', SWAP_X)  60.6 us
    pallas_call x4, Pallas kernels, grads_of(): pl.pallas_call(body, in_specs=[SM] + [ANY] * (count + 1), out_specs=ANY,...  54.1 us
    pallas_call x2, Pallas kernels, feed_back(): pl.pallas_call(body, in_specs=[ANY] * (count + 3 + len(given)), out_specs...  31.9 us
    pallas_call x1, Pallas kernels, attend_back(): pl.pallas_call(body, out_shape=[jax.ShapeDtypeStruct((3 * width, length),...  23.2 us
    ppermute x18, starting transfers between devices, to_y(): return lax.ppermute(values, 'gy', SWAP_Y)  23.2 us
    pallas_call x1, Pallas kernels, feed(): pl.pallas_call(body, in_specs=[ANY] * (count + 1), out_specs=[ANY, ANY],...  21.4 us
    ppermute x18, starting transfers between devices, to_x(): return lax.ppermute(values, 'gy', SWAP_X)  21.2 us
  transfers between devices with their start and end apart: 82, of which 37 were waited for; matrix products, arithmetic and copies ran while one was open for 10% of the time, Pallas kernels for 37%

profile of v2, /device:TPU:0, one launch (start us, length us, event | category | flops | bytes accessed | tf_op | source)
XLA Modules:
  0.0 553.7 jit_solution(2505490820186457459)
XLA Ops:
  12.8 3.0 norm_one.1.refs_0_
  16.3 2.5 collective-permute-start.1
  22.4 20.4 %collective-permute-done.1.refs_2_ = bf16[256,2048]{1,0:T(8,128)(2,1)S(1)} collective-permute-done((bf16[256,2048]{1,0:T(8,128)(2,1)}, bf16[256,2048]{1,0:T(8,128)(2,1)S(1)}, u32[]{:S(2)}, u32[]{:S(2)}) %collective-permute-start.1) | collective-permute-done | bytes 1048608 | tf_op jit(solution)/shard_map/ppermute | solution.py:28
  49.9 7.8 %collective-permute-done.13.refs_3_ = bf16[128,2048]{1,0:T(8,128)(2,1)S(1)} collective-permute-done((bf16[128,2048]{1,0:T(8,128)(2,1)S(1)}, bf16[128,2048]{1,0:T(8,128)(2,1)S(1)}, u32[]{:S(2)}, u32[]{:S(2)}) %collective-permute-start.13) | collective-permute-done | bytes 524320 | tf_op jit(solution)/shard_map/ppermute | solution.py:24
  57.7 23.8 %collective-permute-done.14.refs_4_ = bf16[128,2048]{1,0:T(8,128)(2,1)S(1)} collective-permute-done((bf16[128,2048]{1,0:T(8,128)(2,1)S(1)}, bf16[128,2048]{1,0:T(8,128)(2,1)S(1)}, u32[]{:S(2)}, u32[]{:S(2)}) %collective-permute-start.14) | collective-permute-done | bytes 524320 | tf_op jit(solution)/shard_map/ppermute | solution.py:28
  88.4 6.1 %all-gather.8.cloned.1.call-done = bf16[4096,512]{1,0:T(8,128)(2,1)} async-done(((bf16[1024,512]{1,0:T(8,128)(2,1)}), bf16[4096,512]{1,0:T(8,128)(2,1)}) %all-gather.8.cloned.1.call-update) | async-done | bytes 4194320 | tf_op jit(solution)/shard_map/all_gather | solution.py:1003
  105.6 13.5 %project.1.qkv_ref = bf16[768,2048]{1,0:T(8,128)(2,1)} custom-call(s32[8]{0:T(128)} %fusion.4.pos_ref, bf16[4,1024,512]{2,1,0:T(8,128)(2,1)} %bitcast.57, f32[768,1]{1,0:T(8,128)} %copy.48.b_ref, f32[8,2048]{1,0:T(8,128)} %get-tuple-element.188.c_ref, f32[8,2048]{1,0:T(8,128)} %get-tuple-element.187.s_ref, bf16[256,2048]{1,0:T(8,128)(2,1)} %norm_one.1.refs_0_, ...), custom_call_target="tpu_custom_call" | custom-call | flops 6442450944 | bytes 15728640 | tf_op jit(solution)/shard_map/project/pallas_call | solution.py:428
  119.2 7.0 %collective-permute-done.12.refs_2_.refs_9_ = bf16[256,2048]{1,0:T(8,128)(2,1)S(1)} collective-permute-done((bf16[256,2048]{1,0:T(8,128)(2,1)S(1)}, bf16[256,2048]{1,0:T(8,128)(2,1)S(1)}, u32[]{:S(2)}, u32[]{:S(2)}) %collective-permute-start.12) | collective-permute-done | bytes 1048608 | tf_op jit(solution)/shard_map/ppermute | solution.py:28
  130.7 15.6 %attend.1 = (bf16[256,2048]{1,0:T(8,128)(2,1)}, f32[4,2048]{1,0:T(4,128)}, bf16[2,256,256]{2,1,0:T(8,128)(2,1)}, bf16[2,256,256]{2,1,0:T(8,128)(2,1)}, bf16[2,25...) custom-call(s32[8]{0:T(128)} %fusion.4.pos_ref, s32[8]{0:T(128)} %and_select_fusion.start_ref, ...), custom_call_target="tpu_custom_call" | custom-call | tf_op jit(solution)/shard_map/attend/pallas_call | solution.py:819
  150.9 5.1 collective-permute-done.23.refs_11_
  156.4 3.7 collective-permute-done.25.refs_13_
  165.1 2.6 collective-permute-done.29.refs_8_.refs_15_
  169.3 9.2 %middle_norm.1 = (f32[256,2048]{1,0:T(8,128)}, bf16[256,2048]{1,0:T(8,128)(2,1)}) custom-call(bf16[256,2048]{1,0:T(8,128)(2,1)} %bitcast.61, f32[1,2048]{1,0:T(1,128)} %bitcast.83, f32[1,2048]{1,0:T(1,128)} %bitcast.86, bf16[256,2048]{1,0:T(8,128)(2,1)} %copy-done.1, bf16[256,2048]{1,0:T(8,128)(2,1)} %collective-permute-done.11.refs_1_.refs_8_, ...), custom_call_target="tpu_custom_call" | custom-call | flops 2147483648 | bytes 14680064 | tf_op jit(solution)/shard_map/middle_norm/pallas_call | solution.py:215
  180.9 23.0 %collective-permute-done.32.refs_2_ = bf16[256,2048]{1,0:T(8,128)(2,1)S(1)} collective-permute-done((bf16[256,2048]{1,0:T(8,128)(2,1)}, bf16[256,2048]{1,0:T(8,128)(2,1)S(1)}, u32[]{:S(2)}, u32[]{:S(2)}) %collective-permute-start.32) | collective-permute-done | bytes 1048608 | tf_op jit(solution)/shard_map/ppermute | solution.py:28
  207.0 10.2 %collective-permute-done.33.refs_3_ = bf16[128,2048]{1,0:T(8,128)(2,1)} collective-permute-done((bf16[128,2048]{1,0:T(8,128)(2,1)S(1)}, bf16[128,2048]{1,0:T(8,128)(2,1)}, u32[]{:S(2)}, u32[]{:S(2)}) %collective-permute-start.33) | collective-permute-done | bytes 524320 | tf_op jit(solution)/shard_map/ppermute | solution.py:24
  217.3 2.7 collective-permute-done.34.refs_4_
  222.2 21.4 %feed.1 = (bf16[704,2048]{1,0:T(8,128)(2,1)}, bf16[1408,2048]{1,0:T(8,128)(2,1)}) custom-call(bf16[4,1408,512]{2,1,0:T(8,128)(2,1)} %all-gather.6.cloned.1.call-done.w_ref.wg_ref, bf16[256,2048]{1,0:T(8,128)(2,1)} %get-tuple-element.109.refs_0_, bf16[256,2048]{1,0:T(8,128)(2,1)} %copy-done.10, bf16[256,2048]{1,0:T(8,128)(2,1)} %copy-done.9, ...), custom_call_target="tpu_custom_call" | custom-call | flops 11811160064 | bytes 23068672 | tf_op jit(solution)/shard_map/feed/pallas_call | solution.py:488
  244.1 12.5 %down_grads.1 = bf16[4,704,512]{2,1,0:T(8,128)(2,1)} custom-call(s32[8]{0:T(128)} %jit_remainder_.5.pos_ref, bf16[704,2048]{1,0:T(8,128)(2,1)} %get-tuple-element.144.l_ref.h_ref, bf16[256,2048]{1,0:T(8,128)(2,1)} %bitcast.63, bf16[256,2048]{1,0:T(8,128)(2,1)} %copy-done.4, bf16[256,2048]{1,0:T(8,128)(2,1)} %copy-done.3, ...), custom_call_target="tpu_custom_call" | custom-call | flops 590558016 | bytes 2097152 | tf_op jit(solution)/shard_map/down_grads/pallas_call | solution.py:628
  256.7 3.7 all-gather.10.cloned.1.call-done
  260.4 15.9 %feed_back_sibling.1 = (bf16[1408,2048]{1,0:T(8,128)(2,1)}, bf16[1024,2048]{1,0:T(8,128)(2,1)}) custom-call(bf16[4,704,512]{2,1,0:T(8,128)(2,1)} %bitcast.52, bf16[1408,2048]{1,0:T(8,128)(2,1)} %get-tuple-element.117.s_ref, bf16[4,1408,512]{2,1,0:T(8,128)(2,1)} %all-gather.6.cloned.1.call-done.w_ref.wg_ref, ...), custom_call_target="tpu_custom_call" | custom-call | flops 295279008 | bytes 1048576 | tf_op jit(solution)/shard_map/feed_back_sibling/pallas_call | solution.py:558
  276.6 16.0 %feed_back_own.1 = (bf16[1408,2048]{1,0:T(8,128)(2,1)}, bf16[1024,2048]{1,0:T(8,128)(2,1)}) custom-call(bf16[4,704,512]{2,1,0:T(8,128)(2,1)} %bitcast.53, bf16[1408,2048]{1,0:T(8,128)(2,1)} %get-tuple-element.117.s_ref, bf16[4,1408,512]{2,1,0:T(8,128)(2,1)} %all-gather.6.cloned.1.call-done.w_ref.wg_ref, ...), custom_call_target="tpu_custom_call", output_to_operand_aliasing={{0}: (8, {})} | custom-call | flops 295279008 | bytes 1048576 | tf_op jit(solution)/shard_map/feed_back_own/pallas_call | solution.py:558
  292.6 3.0 add_convert_fusion.15
  299.7 20.1 %gate_up_grads.1 = bf16[4,1408,512]{2,1,0:T(8,128)(2,1)} custom-call(s32[8]{0:T(128)} %jit_remainder_.5.pos_ref, bf16[1408,2048]{1,0:T(8,128)(2,1)} %get-tuple-element.123.l_ref, bf16[256,2048]{1,0:T(8,128)(2,1)} %get-tuple-element.109.refs_0_, bf16[256,2048]{1,0:T(8,128)(2,1)} %copy-done.10, bf16[256,2048]{1,0:T(8,128)(2,1)} %copy-done.9, ...), custom_call_target="tpu_custom_call" | custom-call | flops 590558016 | bytes 1048576 | tf_op jit(solution)/shard_map/gate_up_grads/pallas_call | solution.py:628
  319.8 2.7 collective-permute-done.41.refs_2_
  328.5 7.5 %mlp_rows_sibling.1 = bf16[1024,2048]{1,0:T(8,128)(2,1)} custom-call(bf16[704,2048]{1,0:T(8,128)(2,1)} %get-tuple-element.144.l_ref.h_ref, bf16[4,704,512]{2,1,0:T(8,128)(2,1)} %bitcast.54), custom_call_target="tpu_custom_call" | custom-call | flops 295279008 | bytes 943718 | tf_op jit(solution)/shard_map/mlp_rows_sibling/pallas_call | solution.py:692
  336.0 3.4 collective-permute-done.43.refs_3_
  341.2 10.0 %norm_two_back.1 = (bf16[256,2048]{1,0:T(8,128)(2,1)}, f32[2,2048]{1,0:T(2,128)}, f32[256,2048]{1,0:T(8,128)}, bf16[2,256,256]{2,1,0:T(8,128)(2,1)}, bf16[2,256,...) custom-call(f32[256,2048]{1,0:T(8,128)} %get-tuple-element.127.v_ref, ...), custom_call_target="tpu_custom_call" | custom-call | tf_op jit(solution)/shard_map/norm_two_back/pallas_call | solution.py:274
  355.7 5.0 collective-permute-done.45.refs_1_
  360.8 5.0 collective-permute-done.46.refs_2_
  370.0 23.2 %attend_back.1 = (bf16[768,2048]{1,0:T(8,128)(2,1)}, f32[768,1]{1,0:T(8,128)}) custom-call(s32[8]{0:T(128)} %fusion.4.pos_ref, s32[8]{0:T(128)} %and_select_fusion.start_ref, bf16[768,2048]{1,0:T(8,128)(2,1)} %project.1.qkv_ref, bf16[256,2048]{1,0:T(8,128)(2,1)} %get-tuple-element.143.att_ref.l_ref, f32[4,2048]{1,0:T(4,128)} %get-tuple-element.113.log_ref, ...), custom_call_target="tpu_custom_call" | custom-call | tf_op jit(solution)/shard_map/attend_back/pallas_call | solution.py:933
  396.5 13.4 %qkv_grads.1 = bf16[4,3,512,256]{3,2,1,0:T(8,128)(2,1)} custom-call(s32[8]{0:T(128)} %fusion.4.pos_ref, bf16[768,2048]{1,0:T(8,128)(2,1)} %get-tuple-element.140.l_ref, bf16[256,2048]{1,0:T(8,128)(2,1)} %norm_one.1.refs_0_, bf16[256,2048]{1,0:T(8,128)(2,1)} %copy-done.8, bf16[256,2048]{1,0:T(8,128)(2,1)} %copy-done.7, bf16[128,2048]{1,0:T(8,128)(2,1)} %copy-done.33, ...), custom_call_target="tpu_custom_call" | custom-call | tf_op jit(solution)/shard_map/qkv_grads/pallas_call | solution.py:628
  409.9 8.2 %d_one_rows_sibling.1 = bf16[1024,2048]{1,0:T(8,128)(2,1)} custom-call(s32[8]{0:T(128)} %fusion.4.pos_ref, bf16[768,2048]{1,0:T(8,128)(2,1)} %get-tuple-element.140.l_ref, bf16[4,1024,512]{2,1,0:T(8,128)(2,1)} %bitcast.58), custom_call_target="tpu_custom_call" | custom-call | tf_op jit(solution)/shard_map/d_one_rows_sibling/pallas_call | solution.py:720
  419.6 8.2 %d_one_rows_own.1.refs_0_ = bf16[1024,2048]{1,0:T(8,128)(2,1)} custom-call(s32[8]{0:T(128)} %fusion.4.pos_ref, bf16[768,2048]{1,0:T(8,128)(2,1)} %get-tuple-element.140.l_ref, bf16[4,1024,512]{2,1,0:T(8,128)(2,1)} %bitcast.59), custom_call_target="tpu_custom_call" | custom-call | tf_op jit(solution)/shard_map/d_one_rows_own/pallas_call | solution.py:720
  428.9 2.9 add_convert_fusion.9
  437.7 8.1 %out_grads.1 = bf16[4,1,512,256]{3,2,1,0:T(8,128)(2,1)} custom-call(s32[8]{0:T(128)} %fusion.4.pos_ref, bf16[256,2048]{1,0:T(8,128)(2,1)} %get-tuple-element.143.att_ref.l_ref, bf16[256,2048]{1,0:T(8,128)(2,1)} %get-tuple-element.134.refs_0_, bf16[256,2048]{1,0:T(8,128)(2,1)} %collective-permute-done.49.refs_1_, bf16[256,2048]{1,0:T(8,128)(2,1)} %copy-done.13, ...), custom_call_target="tpu_custom_call" | custom-call | tf_op jit(solution)/shard_map/out_grads/pallas_call | solution.py:628
  445.8 7.5 %mlp_rows_own.1 = bf16[1024,2048]{1,0:T(8,128)(2,1)} custom-call(bf16[704,2048]{1,0:T(8,128)(2,1)} %get-tuple-element.144.l_ref.h_ref, bf16[4,704,512]{2,1,0:T(8,128)(2,1)} %bitcast.55), custom_call_target="tpu_custom_call" | custom-call | tf_op jit(solution)/shard_map/mlp_rows_own/pallas_call | solution.py:692
  453.3 2.9 add_convert_fusion.5
  456.4 2.9 collective-permute-done.60.refs_2_
  460.4 3.5 add_convert_fusion.2
  466.1 22.0 %collective-permute-done.62 = bf16[256,2048]{1,0:T(8,128)(2,1)S(1)} collective-permute-done((bf16[256,2048]{1,0:T(8,128)(2,1)S(1)}, bf16[256,2048]{1,0:T(8,128)(2,1)S(1)}, u32[]{:S(2)}, u32[]{:S(2)}) %collective-permute-start.62) | collective-permute-done | bytes 1048608 | tf_op jit(solution)/shard_map/ppermute | solution.py:24
  488.9 2.8 add_convert_fusion.1
  496.0 10.6 %collective-permute-done.64 = bf16[128,2048]{1,0:T(8,128)(2,1)} collective-permute-done((bf16[128,2048]{1,0:T(8,128)(2,1)S(1)}, bf16[128,2048]{1,0:T(8,128)(2,1)}, u32[]{:S(2)}, u32[]{:S(2)}) %collective-permute-start.64) | collective-permute-done | bytes 524320 | tf_op jit(solution)/shard_map/ppermute | solution.py:28
  507.9 3.4 convert_bitcast_fusion
  512.6 2.6 collective-permute-done.67.refs_4_
  515.2 6.6 %norm_one_back.1 = (bf16[256,2048]{1,0:T(8,128)(2,1)}, f32[2,2048]{1,0:T(2,128)}) custom-call(bf16[256,2048]{1,0:T(8,128)(2,1)} %bitcast.62, f32[256,2048]{1,0:T(8,128)} %get-tuple-element.158.u_ref, bf16[1024,2048]{1,0:T(8,128)(2,1)} %d_one_rows_own.1.refs_0_, bf16[1024,2048]{1,0:T(8,128)(2,1)} %collective-permute-done.53.refs_1_, ...), custom_call_target="tpu_custom_call" | custom-call | tf_op jit(solution)/shard_map/norm_one_back/pallas_call | solution.py:309
  527.5 4.0 collective-permute-done.69
  531.6 3.1 fusion.1
  534.7 2.6 collective-permute-start.74
  (318 shorter events, 117.2 us)
Async XLA Ops:
  7.2 87.3 %all-gather.8.cloned.1.call-start = ((), (), s32[]{:S(2)}) async-start(), calls=%async_computation.9 | async-start | bytes 5242880 | tf_op jit(solution)/shard_map/all_gather | solution.py:1003
  10.8 209.1 %all-gather.6.cloned.1.call-start = ((), (), s32[]{:S(2)}) async-start(), calls=%async_computation.4 | async-start | bytes 7208960 | tf_op jit(solution)/shard_map/all_gather | solution.py:1004
  11.6 248.8 %all-gather.10.cloned.1.call-start = ((), (), s32[]{:S(2)}) async-start(), calls=%async_computation.10 | async-start | bytes 3604480 | tf_op jit(solution)/shard_map/all_gather | solution.py:1007
  15.8 34.1 %collective-permute-start.15 = (bf16[256,2048]{1,0:T(8,128)(2,1)}, bf16[256,2048]{1,0:T(8,128)(2,1)}, u32[]{:S(2)}, u32[]{:S(2)}) collective-permute-start(bf16[256,2048]{1,0:T(8,128)(2,1)} %norm_one.1.refs_0_), channel_id=1, source_target_pairs={{0,1},{1,0},{2,3},{3,2},{4,5},{5,4},{6,7},{7,6},{8,9},{9,8},{10,11... | collective-permute-start | bytes 3145736 | tf_op jit(solution)/shard_map/ppermute | solution.py:40
  16.3 26.6 %collective-permute-start.1 = (bf16[256,2048]{1,0:T(8,128)(2,1)}, bf16[256,2048]{1,0:T(8,128)(2,1)S(1)}, u32[]{:S(2)}, u32[]{:S(2)}) collective-permute-start(bf16[256,2048]{1,0:T(8,128)(2,1)} %norm_one.1.refs_0_), channel_id=1, source_target_pairs={{0,4},{4,0},{2,6},{6,2},{1,5},{5,1},{3,7},{7,3},{8,12},{12,8},{10,... | collective-permute-start | bytes 3145736 | tf_op jit(solution)/shard_map/ppermute | solution.py:28
  18.8 25.9 %collective-permute-start = (bf16[256,2048]{1,0:T(8,128)(2,1)}, bf16[256,2048]{1,0:T(8,128)(2,1)S(1)}, u32[]{:S(2)}, u32[]{:S(2)}) collective-permute-start(bf16[256,2048]{1,0:T(8,128)(2,1)} %norm_one.1.refs_0_), channel_id=1, source_target_pairs={{0,2},{2,0},{4,6},{6,4},{1,3},{3,1},{5,7},{7,5},{8,10},{10,8},{12,... | collective-permute-start | bytes 3145736 | tf_op jit(solution)/shard_map/ppermute | solution.py:24
  42.9 14.8 %collective-permute-start.13 = (bf16[128,2048]{1,0:T(8,128)(2,1)S(1)}, bf16[128,2048]{1,0:T(8,128)(2,1)S(1)}, u32[]{:S(2)}, u32[]{:S(2)}) collective-permute-start(bf16[128,2048]{1,0:T(8,128)(2,1)S(1)} %slice.297), channel_id=1, source_target_pairs={{0,2},{2,0},{4,6},{6,4},{1,3},{3,1},{5,7},{7,5},{8,10},{10,8},{12,... | collective-permute-start | bytes 1572872 | tf_op jit(solution)/shard_map/ppermute | solution.py:24
  45.6 36.4 %collective-permute-start.3 = (bf16[256,2048]{1,0:T(8,128)(2,1)S(1)}, bf16[256,2048]{1,0:T(8,128)(2,1)S(1)}, u32[]{:S(2)}, u32[]{:S(2)}) collective-permute-start(bf16[256,2048]{1,0:T(8,128)(2,1)S(1)} %bitcast.66), channel_id=1, source_target_pairs={{0,4},{4,0},{2,6},{6,2},{1,5},{5,1},{3,7},{7,3},{8,12},{12,8},{10,... | collective-permute-start | bytes 3145736 | tf_op jit(solution)/shard_map/ppermute | solution.py:28
  47.2 34.9 %collective-permute-start.2 = (bf16[256,2048]{1,0:T(8,128)(2,1)S(1)}, bf16[256,2048]{1,0:T(8,128)(2,1)S(1)}, u32[]{:S(2)}, u32[]{:S(2)}) collective-permute-start(bf16[256,2048]{1,0:T(8,128)(2,1)S(1)} %bitcast.67), channel_id=1, source_target_pairs={{0,2},{2,0},{4,6},{6,4},{1,3},{3,1},{5,7},{7,5},{8,10},{10,8},{12,... | collective-permute-start | bytes 3145736 | tf_op jit(solution)/shard_map/ppermute | solution.py:24
  48.8 32.7 %collective-permute-start.14 = (bf16[128,2048]{1,0:T(8,128)(2,1)S(1)}, bf16[128,2048]{1,0:T(8,128)(2,1)S(1)}, u32[]{:S(2)}, u32[]{:S(2)}) collective-permute-start(bf16[128,2048]{1,0:T(8,128)(2,1)S(1)} %slice.298), channel_id=1, source_target_pairs={{0,4},{4,0},{2,6},{6,2},{1,5},{5,1},{3,7},{7,3},{8,12},{12,8},{10,... | collective-permute-start | bytes 1572872 | tf_op jit(solution)/shard_map/ppermute | solution.py:28
  49.9 34.6 %collective-permute-start.17 = (bf16[256,2048]{1,0:T(8,128)(2,1)}, bf16[256,2048]{1,0:T(8,128)(2,1)}, u32[]{:S(2)}, u32[]{:S(2)}) collective-permute-start(bf16[256,2048]{1,0:T(8,128)(2,1)} %copy-done.7), channel_id=1, source_target_pairs={{0,1},{1,0},{2,3},{3,2},{4,5},{5,4},{6,7},{7,6},{8,9},{9,8},{10,11... | collective-permute-start | bytes 3145736 | tf_op jit(solution)/shard_map/ppermute | solution.py:40
  57.7 23.8 %collective-permute-start.18 = (bf16[128,2048]{1,0:T(8,128)(2,1)S(1)}, bf16[128,2048]{1,0:T(8,128)(2,1)S(1)}, u32[]{:S(2)}, u32[]{:S(2)}) collective-permute-start(bf16[128,2048]{1,0:T(8,128)(2,1)S(1)} %collective-permute-done.13.refs_3_), channel_id=1, source_target_pairs={{0,1},{1,0},{2,3},{3,2},{4,5},{5,4},{6,7},{7,6},{8,9},{9,8},{10,11... | collective-permute-start | bytes 1572872 | tf_op jit(solution)/shard_map/ppermute | solution.py:40
  81.5 19.0 %collective-permute-start.6 = (bf16[256,2048]{1,0:T(8,128)(2,1)S(1)}, bf16[256,2048]{1,0:T(8,128)(2,1)}, u32[]{:S(2)}, u32[]{:S(2)}) collective-permute-start(bf16[256,2048]{1,0:T(8,128)(2,1)S(1)} %bitcast.68), channel_id=1, source_target_pairs={{0,1},{1,0},{2,3},{3,2},{4,5},{5,4},{6,7},{7,6},{8,9},{9,8},{10,11... | collective-permute-start | bytes 3145736 | tf_op jit(solution)/shard_map/ppermute | solution.py:40
  82.0 23.1 %collective-permute-start.16 = (bf16[256,2048]{1,0:T(8,128)(2,1)}, bf16[256,2048]{1,0:T(8,128)(2,1)}, u32[]{:S(2)}, u32[]{:S(2)}) collective-permute-start(bf16[256,2048]{1,0:T(8,128)(2,1)} %copy-done.8), channel_id=1, source_target_pairs={{0,1},{1,0},{2,3},{3,2},{4,5},{5,4},{6,7},{7,6},{8,9},{9,8},{10,11... | collective-permute-start | bytes 3145736 | tf_op jit(solution)/shard_map/ppermute | solution.py:40
  82.4 22.7 %collective-permute-start.8 = (bf16[256,2048]{1,0:T(8,128)(2,1)S(1)}, bf16[256,2048]{1,0:T(8,128)(2,1)}, u32[]{:S(2)}, u32[]{:S(2)}) collective-permute-start(bf16[256,2048]{1,0:T(8,128)(2,1)S(1)} %collective-permute-done.3.refs_2_), channel_id=1, source_target_pairs={{0,1},{1,0},{2,3},{3,2},{4,5},{5,4},{6,7},{7,6},{8,9},{9,8},{10,11... | collective-permute-start | bytes 3145736 | tf_op jit(solution)/shard_map/ppermute | solution.py:40
  84.5 16.1 %collective-permute-start.4 = (bf16[128,2048]{1,0:T(8,128)(2,1)}, bf16[128,2048]{1,0:T(8,128)(2,1)}, u32[]{:S(2)}, u32[]{:S(2)}) collective-permute-start(bf16[128,2048]{1,0:T(8,128)(2,1)} %slice.293), channel_id=1, source_target_pairs={{0,2},{2,0},{4,6},{6,4},{1,3},{3,1},{5,7},{7,5},{8,10},{10,8},{12,... | collective-permute-start | bytes 1572872 | tf_op jit(solution)/shard_map/ppermute | solution.py:24
  86.8 15.3 %collective-permute-start.5 = (bf16[128,2048]{1,0:T(8,128)(2,1)}, bf16[128,2048]{1,0:T(8,128)(2,1)}, u32[]{:S(2)}, u32[]{:S(2)}) collective-permute-start(bf16[128,2048]{1,0:T(8,128)(2,1)} %slice.294), channel_id=1, source_target_pairs={{0,4},{4,0},{2,6},{6,2},{1,5},{5,1},{3,7},{7,3},{8,12},{12,8},{10,... | collective-permute-start | bytes 1572872 | tf_op jit(solution)/shard_map/ppermute | solution.py:28
  100.5 18.7 %collective-permute-start.7 = (bf16[256,2048]{1,0:T(8,128)(2,1)}, bf16[256,2048]{1,0:T(8,128)(2,1)}, u32[]{:S(2)}, u32[]{:S(2)}) collective-permute-start(bf16[256,2048]{1,0:T(8,128)(2,1)} %copy-done.4), channel_id=1, source_target_pairs={{0,1},{1,0},{2,3},{3,2},{4,5},{5,4},{6,7},{7,6},{8,9},{9,8},{10,11... | collective-permute-start | bytes 3145736 | tf_op jit(solution)/shard_map/ppermute | solution.py:40
  100.6 25.6 %collective-permute-start.12 = (bf16[256,2048]{1,0:T(8,128)(2,1)S(1)}, bf16[256,2048]{1,0:T(8,128)(2,1)S(1)}, u32[]{:S(2)}, u32[]{:S(2)}) collective-permute-start(bf16[256,2048]{1,0:T(8,128)(2,1)S(1)} %copy.50.refs_0_.refs_7_), channel_id=1, source_target_pairs={{0,4},{4,0},{2,6},{6,2},{1,5},{5,1},{3,7},{7,3},{8,12},{12,8},{10,... | collective-permute-start | bytes 3145736 | tf_op jit(solution)/shard_map/ppermute | solution.py:28
  102.2 25.3 %collective-permute-start.11 = (bf16[256,2048]{1,0:T(8,128)(2,1)S(1)}, bf16[256,2048]{1,0:T(8,128)(2,1)}, u32[]{:S(2)}, u32[]{:S(2)}) collective-permute-start(bf16[256,2048]{1,0:T(8,128)(2,1)S(1)} %copy.50.refs_0_.refs_7_), channel_id=1, source_target_pairs={{0,2},{2,0},{4,6},{6,4},{1,3},{3,1},{5,7},{7,5},{8,10},{10,8},{12,... | collective-permute-start | bytes 3145736 | tf_op jit(solution)/shard_map/ppermute | solution.py:24
  128.6 17.7 %collective-permute-start.20 = (bf16[128,2048]{1,0:T(8,128)(2,1)S(1)}, bf16[128,2048]{1,0:T(8,128)(2,1)S(1)}, u32[]{:S(2)}, u32[]{:S(2)}) collective-permute-start(bf16[128,2048]{1,0:T(8,128)(2,1)S(1)} %slice.296), channel_id=1, source_target_pairs={{0,2},{2,0},{4,6},{6,4},{1,3},{3,1},{5,7},{7,5},{8,10},{10,8},{12,... | collective-permute-start | bytes 1572872 | tf_op jit(solution)/shard_map/ppermute | solution.py:24
  130.2 16.2 %collective-permute-start.21 = (bf16[128,2048]{1,0:T(8,128)(2,1)S(1)}, bf16[128,2048]{1,0:T(8,128)(2,1)S(1)}, u32[]{:S(2)}, u32[]{:S(2)}) collective-permute-start(bf16[128,2048]{1,0:T(8,128)(2,1)S(1)} %slice.299), channel_id=1, source_target_pairs={{0,4},{4,0},{2,6},{6,2},{1,5},{5,1},{3,7},{7,3},{8,12},{12,8},{10,... | collective-permute-start | bytes 1572872 | tf_op jit(solution)/shard_map/ppermute | solution.py:28
  163.1 206.9 %reduce-scatter.5.cloned.1.call-start = ((), (), s32[]{:S(2)}) async-start(), calls=%async_computation.5 | async-start | bytes 3604480 | tf_op jit(solution)/shard_map/reduce_scatter | solution.py:1053
  178.5 25.5 %collective-permute-start.32 = (bf16[256,2048]{1,0:T(8,128)(2,1)}, bf16[256,2048]{1,0:T(8,128)(2,1)S(1)}, u32[]{:S(2)}, u32[]{:S(2)}) collective-permute-start(bf16[256,2048]{1,0:T(8,128)(2,1)} %get-tuple-element.109.refs_0_), channel_id=1, source_target_pairs={{0,4},{4,0},{2,6},{6,2},{1,5},{5,1},{3,7},{7,3},{8,12},{12,8},{10,... | collective-permute-start | bytes 3145736 | tf_op jit(solution)/shard_map/ppermute | solution.py:28
  179.5 25.9 %collective-permute-start.31 = (bf16[256,2048]{1,0:T(8,128)(2,1)}, bf16[256,2048]{1,0:T(8,128)(2,1)S(1)}, u32[]{:S(2)}, u32[]{:S(2)}) collective-permute-start(bf16[256,2048]{1,0:T(8,128)(2,1)} %get-tuple-element.109.refs_0_), channel_id=1, source_target_pairs={{0,2},{2,0},{4,6},{6,4},{1,3},{3,1},{5,7},{7,5},{8,10},{10,8},{12,... | collective-permute-start | bytes 3145736 | tf_op jit(solution)/shard_map/ppermute | solution.py:24
  180.9 39.1 %collective-permute-start.35 = (bf16[256,2048]{1,0:T(8,128)(2,1)}, bf16[256,2048]{1,0:T(8,128)(2,1)S(1)}, u32[]{:S(2)}, u32[]{:S(2)}) collective-permute-start(bf16[256,2048]{1,0:T(8,128)(2,1)} %get-tuple-element.109.refs_0_), channel_id=1, source_target_pairs={{0,1},{1,0},{2,3},{3,2},{4,5},{5,4},{6,7},{7,6},{8,9},{9,8},{10,11... | collective-permute-start | bytes 3145736 | tf_op jit(solution)/shard_map/ppermute | solution.py:40
  205.4 14.6 %collective-permute-start.37 = (bf16[256,2048]{1,0:T(8,128)(2,1)S(1)}, bf16[256,2048]{1,0:T(8,128)(2,1)}, u32[]{:S(2)}, u32[]{:S(2)}) collective-permute-start(bf16[256,2048]{1,0:T(8,128)(2,1)S(1)} %collective-permute-done.32.refs_2_), channel_id=1, source_target_pairs={{0,1},{1,0},{2,3},{3,2},{4,5},{5,4},{6,7},{7,6},{8,9},{9,8},{10,11... | collective-permute-start | bytes 3145736 | tf_op jit(solution)/shard_map/ppermute | solution.py:40
  205.5 14.5 %collective-permute-start.36 = (bf16[256,2048]{1,0:T(8,128)(2,1)S(1)}, bf16[256,2048]{1,0:T(8,128)(2,1)}, u32[]{:S(2)}, u32[]{:S(2)}) collective-permute-start(bf16[256,2048]{1,0:T(8,128)(2,1)S(1)} %collective-permute-done.31.refs_1_), channel_id=1, source_target_pairs={{0,1},{1,0},{2,3},{3,2},{4,5},{5,4},{6,7},{7,6},{8,9},{9,8},{10,11... | collective-permute-start | bytes 3145736 | tf_op jit(solution)/shard_map/ppermute | solution.py:40
  276.3 16.3 %collective-permute-start.40 = (bf16[1024,2048]{1,0:T(8,128)(2,1)}, bf16[1024,2048]{1,0:T(8,128)(2,1)}, u32[]{:S(2)}, u32[]{:S(2)}) collective-permute-start(bf16[1024,2048]{1,0:T(8,128)(2,1)} %get-tuple-element.116), channel_id=1, source_target_pairs={{0,1},{1,0},{2,3},{3,2},{4,5},{5,4},{6,7},{7,6},{8,9},{9,8},{10,11... | collective-permute-start | bytes 12582920 | tf_op jit(solution)/shard_map/ppermute | solution.py:40
  276.4 231.5 %reduce-scatter.7.cloned.1.call-start = ((), (), s32[]{:S(2)}) async-start(), calls=%async_computation.6 | async-start | bytes 7208960 | tf_op jit(solution)/shard_map/reduce_scatter | solution.py:1061
  296.8 25.8 %collective-permute-start.41 = (bf16[256,2048]{1,0:T(8,128)(2,1)}, bf16[256,2048]{1,0:T(8,128)(2,1)S(1)}, u32[]{:S(2)}, u32[]{:S(2)}) collective-permute-start(bf16[256,2048]{1,0:T(8,128)(2,1)} %get-tuple-element.121), channel_id=1, source_target_pairs={{0,2},{2,0},{4,6},{6,4},{1,3},{3,1},{5,7},{7,5},{8,10},{10,8},{12,... | collective-permute-start | bytes 3145736 | tf_op jit(solution)/shard_map/ppermute | solution.py:24
  298.2 25.3 %collective-permute-start.42 = (bf16[256,2048]{1,0:T(8,128)(2,1)S(1)}, bf16[256,2048]{1,0:T(8,128)(2,1)S(1)}, u32[]{:S(2)}, u32[]{:S(2)}) collective-permute-start(bf16[256,2048]{1,0:T(8,128)(2,1)S(1)} %get-tuple-element.122), channel_id=1, source_target_pairs={{0,4},{4,0},{2,6},{6,2},{1,5},{5,1},{3,7},{7,3},{8,12},{12,8},{10,... | collective-permute-start | bytes 3145736 | tf_op jit(solution)/shard_map/ppermute | solution.py:28
  326.0 216.5 %reduce-scatter.9.cloned.1.call-start = ((), (), s32[]{:S(2)}) async-start(), calls=%async_computation.7 | async-start | bytes 3932160 | tf_op jit(solution)/shard_map/reduce_scatter | solution.py:1098
  367.9 25.3 %collective-permute-start.50 = (bf16[256,2048]{1,0:T(8,128)(2,1)S(1)}, bf16[256,2048]{1,0:T(8,128)(2,1)S(1)}, u32[]{:S(2)}, u32[]{:S(2)}) collective-permute-start(bf16[256,2048]{1,0:T(8,128)(2,1)S(1)} %copy-done.23), channel_id=1, source_target_pairs={{0,4},{4,0},{2,6},{6,2},{1,5},{5,1},{3,7},{7,3},{8,12},{12,8},{10,... | collective-permute-start | bytes 3145736 | tf_op jit(solution)/shard_map/ppermute | solution.py:28
  369.4 25.4 %collective-permute-start.49 = (bf16[256,2048]{1,0:T(8,128)(2,1)S(1)}, bf16[256,2048]{1,0:T(8,128)(2,1)}, u32[]{:S(2)}, u32[]{:S(2)}) collective-permute-start(bf16[256,2048]{1,0:T(8,128)(2,1)S(1)} %copy-done.23), channel_id=1, source_target_pairs={{0,2},{2,0},{4,6},{6,4},{1,3},{3,1},{5,7},{7,5},{8,10},{10,8},{12,... | collective-permute-start | bytes 3145736 | tf_op jit(solution)/shard_map/ppermute | solution.py:24
  393.3 16.6 %collective-permute-start.51 = (bf16[128,2048]{1,0:T(8,128)(2,1)S(1)}, bf16[128,2048]{1,0:T(8,128)(2,1)}, u32[]{:S(2)}, u32[]{:S(2)}) collective-permute-start(bf16[128,2048]{1,0:T(8,128)(2,1)S(1)} %slice.314), channel_id=1, source_target_pairs={{0,2},{2,0},{4,6},{6,4},{1,3},{3,1},{5,7},{7,5},{8,10},{10,8},{12,... | collective-permute-start | bytes 1572872 | tf_op jit(solution)/shard_map/ppermute | solution.py:24
  418.2 35.1 %collective-permute-start.59 = (bf16[1024,2048]{1,0:T(8,128)(2,1)}, bf16[1024,2048]{1,0:T(8,128)(2,1)}, u32[]{:S(2)}, u32[]{:S(2)}) collective-permute-start(bf16[1024,2048]{1,0:T(8,128)(2,1)} %mlp_rows_sibling.1), channel_id=1, source_target_pairs={{0,1},{1,0},{2,3},{3,2},{4,5},{5,4},{6,7},{7,6},{8,9},{9,8},{10,11... | collective-permute-start | bytes 12582920 | tf_op jit(solution)/shard_map/ppermute | solution.py:40
  418.7 123.7 %reduce-scatter.11.cloned.1.call-start = ((), (), s32[]{:S(2)}) async-start(), calls=%async_computation.8 | async-start | bytes 1310720 | tf_op jit(solution)/shard_map/reduce_scatter | solution.py:1105
  419.1 16.2 %collective-permute-start.56 = (bf16[256,2048]{1,0:T(8,128)(2,1)S(1)}, bf16[256,2048]{1,0:T(8,128)(2,1)S(1)}, u32[]{:S(2)}, u32[]{:S(2)}) collective-permute-start(bf16[256,2048]{1,0:T(8,128)(2,1)S(1)} %collective-permute-done.50.refs_2_), channel_id=1, source_target_pairs={{0,1},{1,0},{2,3},{3,2},{4,5},{5,4},{6,7},{7,6},{8,9},{9,8},{10,11... | collective-permute-start | bytes 3145736 | tf_op jit(solution)/shard_map/ppermute | solution.py:40
  419.5 18.2 %collective-permute-start.55 = (bf16[256,2048]{1,0:T(8,128)(2,1)}, bf16[256,2048]{1,0:T(8,128)(2,1)}, u32[]{:S(2)}, u32[]{:S(2)}) collective-permute-start(bf16[256,2048]{1,0:T(8,128)(2,1)} %collective-permute-done.49.refs_1_), channel_id=1, source_target_pairs={{0,1},{1,0},{2,3},{3,2},{4,5},{5,4},{6,7},{7,6},{8,9},{9,8},{10,11... | collective-permute-start | bytes 3145736 | tf_op jit(solution)/shard_map/ppermute | solution.py:40
  433.9 25.4 %collective-permute-start.60 = (bf16[256,2048]{1,0:T(8,128)(2,1)}, bf16[256,2048]{1,0:T(8,128)(2,1)S(1)}, u32[]{:S(2)}, u32[]{:S(2)}) collective-permute-start(bf16[256,2048]{1,0:T(8,128)(2,1)} %pad_maximum_fusion.3), channel_id=1, source_target_pairs={{0,2},{2,0},{4,6},{6,4},{1,3},{3,1},{5,7},{7,5},{8,10},{10,8},{12,... | collective-permute-start | bytes 3145736 | tf_op jit(solution)/shard_map/ppermute | solution.py:24
  435.3 25.1 %collective-permute-start.61 = (bf16[256,2048]{1,0:T(8,128)(2,1)}, bf16[256,2048]{1,0:T(8,128)(2,1)S(1)}, u32[]{:S(2)}, u32[]{:S(2)}) collective-permute-start(bf16[256,2048]{1,0:T(8,128)(2,1)} %pad_maximum_fusion.4), channel_id=1, source_target_pairs={{0,4},{4,0},{2,6},{6,2},{1,5},{5,1},{3,7},{7,3},{8,12},{12,8},{10,... | collective-permute-start | bytes 3145736 | tf_op jit(solution)/shard_map/ppermute | solution.py:28
  463.9 24.2 %collective-permute-start.62 = (bf16[256,2048]{1,0:T(8,128)(2,1)S(1)}, bf16[256,2048]{1,0:T(8,128)(2,1)S(1)}, u32[]{:S(2)}, u32[]{:S(2)}) collective-permute-start(bf16[256,2048]{1,0:T(8,128)(2,1)S(1)} %pad_maximum_fusion.5), channel_id=1, source_target_pairs={{0,2},{2,0},{4,6},{6,4},{1,3},{3,1},{5,7},{7,5},{8,10},{10,8},{12,... | collective-permute-start | bytes 3145736 | tf_op jit(solution)/shard_map/ppermute | solution.py:24
  464.6 24.2 %collective-permute-start.63 = (bf16[256,2048]{1,0:T(8,128)(2,1)S(1)}, bf16[256,2048]{1,0:T(8,128)(2,1)S(1)}, u32[]{:S(2)}, u32[]{:S(2)}) collective-permute-start(bf16[256,2048]{1,0:T(8,128)(2,1)S(1)} %pad_maximum_fusion.6), channel_id=1, source_target_pairs={{0,4},{4,0},{2,6},{6,2},{1,5},{5,1},{3,7},{7,3},{8,12},{12,8},{10,... | collective-permute-start | bytes 3145736 | tf_op jit(solution)/shard_map/ppermute | solution.py:28
  491.7 15.0 %collective-permute-start.64 = (bf16[128,2048]{1,0:T(8,128)(2,1)S(1)}, bf16[128,2048]{1,0:T(8,128)(2,1)}, u32[]{:S(2)}, u32[]{:S(2)}) collective-permute-start(bf16[128,2048]{1,0:T(8,128)(2,1)S(1)} %get-tuple-element.165), channel_id=1, source_target_pairs={{0,4},{4,0},{2,6},{6,2},{1,5},{5,1},{3,7},{7,3},{8,12},{12,8},{10,... | collective-permute-start | bytes 1572872 | tf_op jit(solution)/shard_map/ppermute | solution.py:28
  493.0 19.6 %collective-permute-start.66 = (bf16[128,2048]{1,0:T(8,128)(2,1)}, bf16[128,2048]{1,0:T(8,128)(2,1)}, u32[]{:S(2)}, u32[]{:S(2)}) collective-permute-start(bf16[128,2048]{1,0:T(8,128)(2,1)} %get-tuple-element.167), channel_id=1, source_target_pairs={{0,2},{2,0},{4,6},{6,4},{1,3},{3,1},{5,7},{7,5},{8,10},{10,8},{12,... | collective-permute-start | bytes 1572872 | tf_op jit(solution)/shard_map/ppermute | solution.py:24
  494.1 21.1 %collective-permute-start.67 = (bf16[128,2048]{1,0:T(8,128)(2,1)}, bf16[128,2048]{1,0:T(8,128)(2,1)}, u32[]{:S(2)}, u32[]{:S(2)}) collective-permute-start(bf16[128,2048]{1,0:T(8,128)(2,1)} %get-tuple-element.168), channel_id=1, source_target_pairs={{0,4},{4,0},{2,6},{6,2},{1,5},{5,1},{3,7},{7,3},{8,12},{12,8},{10,... | collective-permute-start | bytes 1572872 | tf_op jit(solution)/shard_map/ppermute | solution.py:28
  495.0 31.3 %collective-permute-start.65 = (bf16[128,2048]{1,0:T(8,128)(2,1)}, bf16[128,2048]{1,0:T(8,128)(2,1)}, u32[]{:S(2)}, u32[]{:S(2)}) collective-permute-start(bf16[128,2048]{1,0:T(8,128)(2,1)} %get-tuple-element.166), channel_id=1, source_target_pairs={{0,2},{2,0},{4,6},{6,4},{1,3},{3,1},{5,7},{7,5},{8,10},{10,8},{12,... | collective-permute-start | bytes 1572872 | tf_op jit(solution)/shard_map/ppermute | solution.py:24
  (86 other events, 886.3 us)
Sparse Core Ops, SparseCore 0:
  10.9 83.4 all-gather.7
  96.0 105.2 all-gather.5
  202.9 57.4 all-gather.9
  276.5 54.9 reduce-scatter.4
  333.7 102.0 reduce-scatter.6
  438.0 60.8 reduce-scatter.8
  501.1 29.8 reduce-scatter.10
